TPU v7x, 128 devices: a whole 4x4x4 slice. The times are simulated.
128 devices in a mesh: blk: 32 (over y_lo, z, x), uly: 4 (over y_hi, core).
Axes of the slice: x: 4, y: 4 (y_hi: 2, y_lo: 2; y = y_hi * 2 + y_lo), z: 4, core: 2. Of those that a mesh axis runs over, the one named last changes fastest.
Arguments:
- tokens: bfloat16 [2, 8192, 1536], P(None, ('blk', 'uly')), may hold values from -6 to 6
- cotangent: bfloat16 [2, 8192, 1536], P(None, ('blk', 'uly')), may hold values from -6 to 6
- lengths: int32 [2], replicated, may hold values from 4097 to 8192, as said below
- set_index: int32 [2], replicated, may hold values from 0 to 7
- norm_in: float32 [1536], replicated, may hold values from 0.25 to 1.75
- norm_ff: float32 [1536], replicated, may hold values from 0.25 to 1.75
- qkv_bias: float32 [2048], replicated, may hold values from -3 to 3
- w_qkv: bfloat16 [1536, 2048], P(('blk', 'uly')), may hold values from -0.15625 to 0.15625
- w_out: bfloat16 [1536, 1536], P(('blk', 'uly')), may hold values from -2.5 to 2.5
- w_gate_up: bfloat16 [2, 1536, 8960], P(None, 'blk', 'uly'), may hold values from -0.15625 to 0.15625
- w_down: bfloat16 [8960, 1536], P('uly', 'blk'), may hold values from -0.0625 to 0.0625
- a_wide: bfloat16 [6, 8, 16, 1536], replicated, may hold values from -0.15625 to 0.15625
- a_down: bfloat16 [8, 16, 8960], replicated, may hold values from -0.0625 to 0.0625
- b_wide: bfloat16 [3, 8, 16, 1536], replicated, may hold values from -1.5 to 1.5
- b_kv: bfloat16 [2, 8, 16, 256], replicated, may hold values from -1.5 to 1.5
- b_ff: bfloat16 [2, 8, 16, 8960], replicated, may hold values from -1.5 to 1.5
Outputs:
- result_tokens: bfloat16 [2, 8192, 1536], P(None, ('blk', 'uly'))
- input_grad: float32 [2, 8192, 1536], P(None, ('blk', 'uly'))
- grad_a_wide: float32 [6, 8, 16, 1536], replicated
- grad_a_down: float32 [8, 16, 8960], replicated
- grad_b_wide: float32 [3, 8, 16, 1536], replicated
- grad_b_kv: float32 [2, 8, 16, 256], replicated
- grad_b_ff: float32 [2, 8, 16, 8960], replicated
Inputs may be any that keep to these rules, and one draw needn't show every extreme that they name: Each sequence's valid slots are its first lengths[s]; one sequence, drawn from the seed, fills all 8192 slots.
All inputs are finite; a program needn't handle non-finite values.
Results may differ from a plain program's by a relative error of at most 0.024.
Values may be sent and summed in bfloat16 or wider, within the bound.
A program may use at most 320 MiB of HBM per device.

v0:
```python
import functools

import jax
import jax.numpy as jnp
import numpy as np
from jax import lax
from jax.experimental import pallas as pl
from jax.experimental.pallas import tpu as pltpu
from jax.sharding import PartitionSpec as P

HEADS = 12
KV_HEADS = 2
HEAD = 128
GROUP = HEADS // KV_HEADS
FF = 8960
SETS = 8
D = 1536
CHUNK = 128
CHUNKS = 64
PADDED = 2304
EPS = 1e-06
THETA = 1000000.0
LOG2E = 1.4426950408889634
LN2 = 0.6931471805599453
MESH = pl.DeviceIdType.MESH
BF = jnp.bfloat16
F32 = jnp.float32
ANY = pl.BlockSpec(memory_space=pl.ANY)
IN_VMEM = pl.BlockSpec(memory_space=pltpu.VMEM)


def blk_of(y, z, x):
    return y * 16 + z * 4 + x


def place():
    blk = lax.axis_index("blk")
    return blk // 16, (blk // 4) % 4, blk % 4, blk, lax.axis_index("uly")


def ring_others():
    y, z, x, blk, uly = place()
    return [
        (blk_of(1 - y, z, x), uly),
        (blk_of(y, z, (x + 1) % 4), uly),
        (blk_of(y, z, (x + 3) % 4), uly),
        (blk_of(y, (z + 1) % 4, x), uly),
        (blk_of(y, (z + 3) % 4, x), uly),
    ]


def greet(others):
    barrier = pltpu.get_barrier_semaphore()
    for other in others:
        pl.semaphore_signal(barrier, inc=1, device_id=other, device_id_type=MESH)
    pl.semaphore_wait(barrier, len(others))


class Gather:
    sends = 31

    def __init__(self, src, dst, send_sem, recv_sem, local_sem):
        self.src, self.dst = src, dst
        self.send_sem, self.recv_sem, self.local_sem = send_sem, recv_sem, local_sem
        self.y, self.z, self.x, self.blk, self.uly = place()
        self.count = [0, 0]
        self.sent = []
        self.local = []

    def at(self, half, y, p, q):
        return blk_of(y, q, p) if half == 0 else blk_of(y, p, q)

    def pq(self, half):
        return (self.x, self.z) if half == 0 else (self.z, self.x)

    def send(self, half, item, target, src=None):
        copy = pltpu.make_async_remote_copy(
            src_ref=self.dst(half, item) if src is None else src,
            dst_ref=self.dst(half, item),
            send_sem=self.send_sem.at[half, self.count[half]],
            recv_sem=self.recv_sem.at[half, item],
            device_id=(target, self.uly),
            device_id_type=MESH,
        )
        self.count[half] += 1
        copy.start()
        self.sent.append(copy)

    def wait(self, half, item):
        ref = self.dst(half, item)
        pltpu.make_async_remote_copy(
            src_ref=ref,
            dst_ref=ref,
            send_sem=self.send_sem.at[half, 0],
            recv_sem=self.recv_sem.at[half, item],
            device_id=(self.blk, self.uly),
            device_id_type=MESH,
        ).wait_recv()

    def start(self):
        for half in (0, 1):
            p, q = self.pq(half)
            self.send(half, self.blk, self.at(half, 1 - self.y, p, q), self.src(half))
        for half in (0, 1):
            p, q = self.pq(half)
            for d in (1, 3):
                self.send(half, self.blk, self.at(half, self.y, (p + d) % 4, q), self.src(half))
            copy = pltpu.make_async_copy(
                self.src(half), self.dst(half, self.blk), self.local_sem.at[half]
            )
            copy.start()
            self.local.append(copy)

    def second(self):
        for half in (0, 1):
            p, q = self.pq(half)
            item = self.at(half, 1 - self.y, p, q)
            self.wait(half, item)
            for d in (1, 3):
                self.send(half, item, self.at(half, self.y, (p + d) % 4, q))
            for d in (1, 3):
                onward = self.at(half, self.y, p, (q + d) % 4)
                self.send(half, self.blk, onward, self.src(half))
                self.send(half, item, onward)

    def spread(self, half, item):
        p, q = self.pq(half)
        for d in (1, 3):
            self.send(half, item, self.at(half, self.y, p, (q + d) % 4))

    def third(self):
        for k, y in enumerate((self.y, 1 - self.y)):
            for half in (0, 1):
                p, q = self.pq(half)
                for d in (3, 1):
                    item = self.at(half, y, (p + d) % 4, q)
                    self.wait(half, item)
                    if (d == 3) == (k == 0):
                        self.send(half, item, self.at(half, self.y, (p + 4 - d) % 4, q))
                    self.spread(half, item)
        for y in (self.y, 1 - self.y):
            for half in (0, 1):
                p, q = self.pq(half)
                item = self.at(half, y, (p + 2) % 4, q)
                self.wait(half, item)
                self.spread(half, item)

    def fourth(self):
        for e in (0, 1, 3, 2):
            for k, y in enumerate((self.y, 1 - self.y)):
                for half in (0, 1):
                    p, q = self.pq(half)
                    for d in (3, 1):
                        item = self.at(half, y, (p + e) % 4, (q + d) % 4)
                        self.wait(half, item)
                        if (d == 3) == (k == 0):
                            self.send(half, item, self.at(half, self.y, p, (q + 4 - d) % 4))

    def last(self):
        for e in (0, 1, 3, 2):
            for y in (self.y, 1 - self.y):
                for half in (0, 1):
                    p, q = self.pq(half)
                    self.wait(half, self.at(half, y, (p + e) % 4, (q + 2) % 4))
        for copy in self.local:
            copy.wait()
        for copy in self.sent:
            copy.wait_send()

    def all(self):
        self.start()
        self.second()
        self.third()
        self.fourth()
        self.last()


GATHER_SEMS = lambda *lead: [
    pltpu.SemaphoreType.DMA(lead + (2, Gather.sends)),
    pltpu.SemaphoreType.DMA(lead + (2, 32)),
    pltpu.SemaphoreType.DMA(lead + (2,)),
]


def proj_kernel(qkv_ref, out_ref, qkv_all, out_all, *sems):
    y, z, x, blk, uly = place()
    core = uly % 2
    sibling = (blk, uly + 1 - 2 * core)
    greet(ring_others() + [sibling])
    (send_a, recv_a, local_a, send_b, recv_b, local_b, pair_send, pair_recv) = sems

    def columns(item, half):
        start = ((item % 2) * 2 + core) * 384
        return pl.ds(pl.multiple_of(start + 128 * half, 128), 128 + 128 * half)

    a = Gather(
        lambda half: qkv_ref.at[:, pl.ds(256 * half, 256)],
        lambda half, item: qkv_all.at[
            core, pl.ds(pl.multiple_of(item * 48, 16), 48), pl.ds(256 * half, 256)
        ],
        send_a, recv_a, local_a,
    )
    b = Gather(
        lambda half: out_ref.at[:, pl.ds(128 * half, 128 + 128 * half)],
        lambda half, item: out_all.at[
            pl.ds(pl.multiple_of((item // 2) * 48, 16), 48), columns(item, half)
        ],
        send_b, recv_b, local_b,
    )
    a.start()
    b.start()
    a.second()
    b.second()
    a.third()
    b.third()
    a.fourth()
    b.fourth()
    a.last()
    b.last()
    parts = [lambda c: qkv_all.at[c]] + [
        lambda c, n=n: out_all.at[:, pl.ds(pl.multiple_of((2 * n + c) * 384, 128), 384)]
        for n in (0, 1)
    ]
    copies = []
    for n, part in enumerate(parts):
        copy = pltpu.make_async_remote_copy(
            src_ref=part(core), dst_ref=part(core),
            send_sem=pair_send.at[n], recv_sem=pair_recv.at[n],
            device_id=sibling, device_id_type=MESH,
        )
        copy.start()
        copies.append(copy)
    for n, part in enumerate(parts):
        copies[n].wait_send()
        pltpu.make_async_remote_copy(
            src_ref=part(1 - core), dst_ref=part(1 - core),
            send_sem=pair_send.at[n], recv_sem=pair_recv.at[n],
            device_id=sibling, device_id_type=MESH,
        ).wait_recv()


def gather_proj(qkv_part, out_part):
    return pl.pallas_call(
        proj_kernel,
        out_shape=(
            jax.ShapeDtypeStruct((2, D, 512), BF),
            jax.ShapeDtypeStruct((D // 2, D), BF),
        ),
        in_specs=[ANY, ANY],
        out_specs=(ANY, ANY),
        scratch_shapes=GATHER_SEMS() + GATHER_SEMS() + [pltpu.SemaphoreType.DMA((3,))] * 2,
        compiler_params=pltpu.CompilerParams(collective_id=0, has_side_effects=True),
        name="gather_proj",
    )(qkv_part, out_part)


KEYS = 512
STEP = KEYS // CHUNK
ROWS = GROUP * CHUNK


def head_columns(ref, slot):
    return jnp.concatenate(
        [
            ref[slot * CHUNK : (slot + 1) * CHUNK, n * HEAD : (n + 1) * HEAD].T
            for n in range(GROUP)
        ],
        axis=1,
    )


def head_rows(ref, slot):
    return jnp.concatenate(
        [
            ref[slot * CHUNK : (slot + 1) * CHUNK, n * HEAD : (n + 1) * HEAD]
            for n in range(GROUP)
        ],
        axis=0,
    )


def key_block(kv_ref, step):
    rows = kv_ref[pl.ds(step * STEP, STEP)].reshape(KEYS, 2 * HEAD)
    return rows[:, :HEAD], rows[:, HEAD:]


def dot(a, b):
    return jnp.dot(a, b, preferred_element_type=F32)


def key_places(step):
    return lax.broadcasted_iota(jnp.int32, (KEYS, ROWS), 0) + step * KEYS


def attend_slot(slot, chunk, q_ref, kv_ref, limit_ref, mixed_ref, lse_ref, acc_ref):
    turned = head_columns(q_ref, slot)
    limit = limit_ref[slot, 0:1, :]
    acc_ref[...] = jnp.zeros_like(acc_ref)

    def step(n, carry):
        top, total = carry
        keys, values = key_block(kv_ref, n)
        scores = jnp.where(key_places(n) <= limit, dot(keys, turned), -1e30)
        new_top = jnp.maximum(top, jnp.max(scores, axis=0, keepdims=True))
        fade = jnp.exp2(top - new_top)
        probs = jnp.exp2(scores - new_top)
        total = total * fade + jnp.sum(probs, axis=0, keepdims=True)
        acc_ref[...] = acc_ref[...] * fade + dot(values.T, probs.astype(BF))
        return new_top, total

    top, total = lax.fori_loop(
        0,
        chunk // STEP + 1,
        step,
        (jnp.full((1, ROWS), -1e30, F32), jnp.zeros((1, ROWS), F32)),
    )
    out = acc_ref[...] / total
    for n in range(GROUP):
        mixed_ref[slot * CHUNK : (slot + 1) * CHUNK, n * HEAD : (n + 1) * HEAD] = out[
            :, n * CHUNK : (n + 1) * CHUNK
        ].T.astype(BF)
    lse_ref[slot] = jnp.broadcast_to(top + jnp.log2(total), (8, ROWS))


def forward_kernel(
    q_ref, kv_ref, limit_ref, ff_ref, mixed_ref, lse_ref, kv_out, gate_all, up_all, down_all,
    kv_all, acc_ref, *sems,
):
    y, z, x, blk, uly = place()
    greet(ring_others())
    kv_send, kv_recv, kv_local, ff_send, ff_recv, ff_local, out_sem = sems
    kv = Gather(
        lambda half: kv_ref.at[half],
        lambda half, item: kv_all.at[item if half == 0 else 63 - item],
        kv_send, kv_recv, kv_local,
    )
    wide = PADDED // 2
    weights = [
        Gather(
            lambda half, n=n: ff_ref.at[n, :, pl.ds(wide * half, wide)],
            lambda half, item, ref=ref: ref.at[item, :, pl.ds(wide * half, wide)],
            ff_send.at[n], ff_recv.at[n], ff_local.at[n],
        )
        for n, ref in enumerate((gate_all, up_all, down_all))
    ]
    kv.start()
    for w in weights:
        w.start()
    kv.second()
    kv.third()
    kv.fourth()
    for w in weights:
        w.second()
    kv.last()
    out_copy = pltpu.make_async_copy(kv_all, kv_out, out_sem)
    out_copy.start()
    attend_slot(0, blk, q_ref, kv_all, limit_ref, mixed_ref, lse_ref, acc_ref)
    for w in weights:
        w.third()
    attend_slot(1, 63 - blk, q_ref, kv_all, limit_ref, mixed_ref, lse_ref, acc_ref)
    for w in weights:
        w.fourth()
    for w in weights:
        w.last()
    out_copy.wait()


def attend_forward(q, kv, limit, ff):
    weight = jax.ShapeDtypeStruct((32, 48, PADDED), BF)
    return pl.pallas_call(
        forward_kernel,
        out_shape=(
            jax.ShapeDtypeStruct((2 * CHUNK, GROUP * HEAD), BF),
            jax.ShapeDtypeStruct((2, 8, ROWS), F32),
            jax.ShapeDtypeStruct((CHUNKS, CHUNK, 2 * HEAD), BF),
            weight, weight, weight,
        ),
        in_specs=[IN_VMEM, ANY, IN_VMEM, ANY],
        out_specs=(IN_VMEM, IN_VMEM, ANY, ANY, ANY, ANY),
        scratch_shapes=[
            pltpu.VMEM((CHUNKS, CHUNK, 2 * HEAD), BF),
            pltpu.VMEM((HEAD, ROWS), F32),
        ]
        + GATHER_SEMS()
        + GATHER_SEMS(3)
        + [pltpu.SemaphoreType.DMA],
        compiler_params=pltpu.CompilerParams(
            collective_id=1, has_side_effects=True, vmem_limit_bytes=40 * 2**20
        ),
        name="attend_forward",
    )(q, kv, limit, ff)


def backward_slot(slot, chunk, q_ref, kv_ref, limit_ref, mixed_ref, grad_ref, lse_ref, dq_ref, dkv_ref, acc_ref):
    turned = head_columns(q_ref, slot)
    rows = head_rows(q_ref, slot)
    grad_turned = head_columns(grad_ref, slot)
    grad_rows = head_rows(grad_ref, slot)
    mixed_turned = head_columns(mixed_ref, slot)
    row_dot = jnp.sum(
        grad_turned.astype(F32) * mixed_turned.astype(F32), axis=0, keepdims=True
    )
    limit = limit_ref[slot, 0:1, :]
    lse = lse_ref[slot, 0:1, :]
    acc_ref[...] = jnp.zeros_like(acc_ref)

    def step(n, carry):
        keys, values = key_block(kv_ref, n)
        scores = jnp.where(key_places(n) <= limit, dot(keys, turned), -1e30)
        probs = jnp.exp2(scores - lse)
        grad_probs = dot(values, grad_turned)
        grad_scores = (probs * (grad_probs - row_dot)).astype(BF)
        acc_ref[...] += dot(keys.T, grad_scores)
        at = pl.ds(pl.multiple_of(n * KEYS, KEYS), KEYS)
        dkv_ref[at, :HEAD] += dot(grad_scores, rows)
        dkv_ref[at, HEAD:] += dot(probs.astype(BF), grad_rows)
        return carry

    lax.fori_loop(0, chunk // STEP + 1, step, 0)
    for n in range(GROUP):
        dq_ref[slot * CHUNK : (slot + 1) * CHUNK, n * HEAD : (n + 1) * HEAD] = (
            acc_ref[:, n * CHUNK : (n + 1) * CHUNK].T * HEAD ** (-0.5)
        )


def reduce_dkv(part, own_ref, bufs, sums, sems):
    y, z, x, blk, uly = place()
    buf_q, buf_p, buf_y = bufs
    sum_p, sum_y = sums
    send_sem, recv_sem = sems

    def index(half, y, p, q):
        item = blk_of(y, q, p) if half == 0 else blk_of(y, p, q)
        return item if half == 0 else 63 - item

    def pq(half):
        return (x, z) if half == 0 else (z, x)

    def device(half, y, p, q):
        return (blk_of(y, q, p) if half == 0 else blk_of(y, p, q), uly)

    def remote(src, dst, half, n, target):
        return pltpu.make_async_remote_copy(
            src_ref=src, dst_ref=dst, send_sem=send_sem.at[half, n], recv_sem=recv_sem.at[half, n],
            device_id=target, device_id_type=MESH,
        )

    done = []
    for d in (2, 1, 3):
        for half in (0, 1):
            p, q = pq(half)
            for yy in (0, 1):
                for pp in range(4):
                    copy = remote(
                        part.at[index(half, yy, pp, (q + d) % 4)],
                        buf_q.at[half, d - 1, yy, pp],
                        half, (d - 1) * 8 + yy * 4 + pp,
                        device(half, y, p, (q + d) % 4),
                    )
                    copy.start()
                    done.append(copy)
    for copy in done:
        copy.wait()
    done = []
    for d in (2, 1, 3, 0):
        for half in (0, 1):
            p, q = pq(half)
            to = (p + d) % 4
            for yy in (0, 1):
                total = part[index(half, yy, to, q)].astype(F32)
                for n in range(3):
                    total += buf_q[half, n, yy, to].astype(F32)
                sum_p[half, d, yy] = total.astype(BF)
            if d > 0:
                copy = remote(
                    sum_p.at[half, d], buf_p.at[half, d - 1], half, 24 + d - 1,
                    device(half, y, to, q),
                )
                copy.start()
                done.append(copy)
    for copy in done:
        copy.wait()
    done = []
    for k in (1, 0):
        for half in (0, 1):
            p, q = pq(half)
            yy = y if k == 0 else 1 - y
            total = sum_p[half, 0, yy].astype(F32)
            for n in range(3):
                total += buf_p[half, n, yy].astype(F32)
            sum_y[half, k] = total.astype(BF)
            if k == 1:
                copy = remote(
                    sum_y.at[half, 1], buf_y.at[half], half, 27, device(half, 1 - y, p, q)
                )
                copy.start()
                done.append(copy)
    for copy in done:
        copy.wait()
    for half in (0, 1):
        own_ref[half] = sum_y[half, 0].astype(F32) + buf_y[half].astype(F32)


def reduce_others():
    y, z, x, blk, uly = place()
    return (
        [(blk_of(1 - y, z, x), uly)]
        + [(blk_of(y, z, (x + d) % 4), uly) for d in (1, 2, 3)]
        + [(blk_of(y, (z + d) % 4, x), uly) for d in (1, 2, 3)]
    )


def backward_kernel(
    q_ref, kv_ref, limit_ref, mixed_ref, grad_ref, lse_ref, dq_ref, own_ref,
    dkv_ref, acc_ref, part, buf_q, buf_p, buf_y, sum_p, sum_y, send_sem, recv_sem,
):
    y, z, x, blk, uly = place()
    greet(reduce_others())
    dkv_ref[...] = jnp.zeros_like(dkv_ref)
    args = (q_ref, kv_ref, limit_ref, mixed_ref, grad_ref, lse_ref, dq_ref, dkv_ref, acc_ref)
    backward_slot(0, blk, *args)
    backward_slot(1, 63 - blk, *args)

    def pack(n, carry):
        rows = dkv_ref[pl.ds(pl.multiple_of(n * CHUNK, CHUNK), CHUNK), :]
        part[n] = jnp.concatenate([rows[:, :HEAD] * LN2, rows[:, HEAD:]], axis=1).astype(BF)
        return carry

    lax.fori_loop(0, CHUNKS, pack, 0)
    reduce_dkv(part, own_ref, (buf_q, buf_p, buf_y), (sum_p, sum_y), (send_sem, recv_sem))


def attend_backward(q, kv, limit, mixed, grad, lse):
    return pl.pallas_call(
        backward_kernel,
        out_shape=(
            jax.ShapeDtypeStruct((2 * CHUNK, GROUP * HEAD), F32),
            jax.ShapeDtypeStruct((2, CHUNK, 2 * HEAD), F32),
        ),
        in_specs=[IN_VMEM] * 6,
        out_specs=(IN_VMEM, IN_VMEM),
        scratch_shapes=[
            pltpu.VMEM((CHUNKS * CHUNK, 2 * HEAD), F32),
            pltpu.VMEM((HEAD, ROWS), F32),
            pltpu.VMEM((CHUNKS, CHUNK, 2 * HEAD), BF),
            pltpu.VMEM((2, 3, 2, 4, CHUNK, 2 * HEAD), BF),
            pltpu.VMEM((2, 3, 2, CHUNK, 2 * HEAD), BF),
            pltpu.VMEM((2, CHUNK, 2 * HEAD), BF),
            pltpu.VMEM((2, 4, 2, CHUNK, 2 * HEAD), BF),
            pltpu.VMEM((2, 2, CHUNK, 2 * HEAD), BF),
            pltpu.SemaphoreType.DMA((2, 28)),
            pltpu.SemaphoreType.DMA((2, 28)),
        ],
        compiler_params=pltpu.CompilerParams(
            collective_id=2, has_side_effects=True, vmem_limit_bytes=56 * 2**20
        ),
        name="attend_backward",
    )(q, kv, limit, mixed, grad, lse)


def device_at(blk, h, core):
    return blk * 4 + h * 2 + core


def moves():
    def home(blk, h):
        chunk = 2 * blk + h
        return (chunk, 0) if chunk < 32 else (63 - chunk, 1)

    fetch = {}
    for j in (0, 1):
        for k in (0, 1):
            fetch[k, j] = [
                (device_at(b, h, c), device_at(home(b, h)[0], h ^ k, c ^ j))
                for b in range(32) for h in (0, 1) for c in (0, 1)
            ]
    own = [
        [
            (device_at(b, h, c), device_at(home(b, h)[0], home(b, h)[1], c ^ j))
            for b in range(32) for h in (0, 1) for c in (0, 1)
        ]
        for j in (0, 1)
    ]
    back = [[(t, s) for s, t in pairs] for pairs in own]
    out_rows = [
        [
            (device_at(b, u // 2, u % 2), device_at(2 * (b % 16) + q // 2, b // 16, q % 2))
            for b in range(32) for u in range(4) for q in ((u + t) % 4,)
        ]
        for t in range(4)
    ]
    return fetch, own, back, out_rows


ALL = ("blk", "uly")
OVER_H = [(0, 2), (2, 0), (1, 3), (3, 1)]
OVER_CORE = [(0, 1), (1, 0), (2, 3), (3, 2)]
OVER_BOTH = [(0, 3), (3, 0), (1, 2), (2, 1)]


def flip(parts, first, second):
    return jnp.where(parts, second, first), jnp.where(parts, first, second)


def rope_tables(positions):
    halves = jnp.arange(0, HEAD, 2, dtype=jnp.int32).astype(F32)
    freq_table = THETA ** (-halves / HEAD)
    angles = positions.astype(F32)[:, None] * freq_table[None, :]
    angles = jnp.concatenate([angles, angles], axis=-1)
    return jnp.cos(angles), jnp.sin(angles)


def rope_turn(values, cos_table, sine_table):
    middle = HEAD // 2
    turned = jnp.concatenate([-values[..., middle:], values[..., :middle]], axis=-1)
    return values * cos_table + turned * sine_table


def rope_back(values, cos_table, sine_table):
    middle = HEAD // 2
    turned = jnp.concatenate([values[..., middle:], -values[..., :middle]], axis=-1)
    return values * cos_table + turned * sine_table


def norm_scale(hidden):
    return lax.rsqrt(jnp.mean(hidden * hidden, axis=-1, keepdims=True) + EPS)


def norm_back(hidden, scaled, gain_vec, upstream):
    normed = hidden * scaled
    weighted = upstream * gain_vec
    return scaled * (weighted - normed * jnp.mean(weighted * normed, axis=-1, keepdims=True))


def mm(spec, a, b):
    return jnp.einsum(spec, a.astype(BF), b.astype(BF), preferred_element_type=F32)


def body(
    tokens, cotangent, lengths, set_index, norm_in, norm_ff, qkv_bias, w_qkv, w_out, w_gate_up, w_down,
    a_wide, a_down, b_wide, b_kv, b_ff,
):
    blk = lax.axis_index("blk")
    uly = lax.axis_index("uly")
    h = uly // 2
    core = uly % 2
    fetch, own_moves, back_moves, out_moves = moves()
    local_ff = w_down.shape[0]
    group_cols = GROUP * HEAD

    by_head = jnp.concatenate(
        [
            w_qkv[:, : HEADS * HEAD].reshape(12, 2, group_cols),
            w_qkv[:, HEADS * HEAD : HEADS * HEAD + 256].reshape(12, 2, HEAD),
            w_qkv[:, HEADS * HEAD + 256 :].reshape(12, 2, HEAD),
        ],
        axis=2,
    )
    quarters = jnp.moveaxis(by_head.reshape(12, 4, 512), 1, 0)
    qkv_part = lax.all_to_all(quarters, "uly", split_axis=0, concat_axis=0, tiled=True).reshape(48, 512)
    out_quarters = jnp.moveaxis(w_out.reshape(12, 4, 384), 1, 0)
    got = [
        lax.ppermute(
            lax.dynamic_index_in_dim(out_quarters, (uly + t) % 4, 0, keepdims=False), ALL, out_moves[t]
        )
        for t in range(4)
    ]
    quarter = (blk % 2) * 2 + core
    got = jnp.stack(got)
    out_part = jnp.take(got, (quarter - jnp.arange(4)) % 4, axis=0).reshape(48, 384)
    qkv_w, out_w = gather_proj(qkv_part, out_part)

    pieces = [
        [
            lax.ppermute(lax.dynamic_index_in_dim(tokens, core ^ j, 0, keepdims=False), ALL, fetch[k, j])
            for j in (0, 1)
        ]
        for k in (0, 1)
    ]
    first, second = flip((blk % 2) != h, jnp.stack(pieces[0]), jnp.stack(pieces[1]))
    rows = jnp.stack([first, second])
    rows = jnp.stack(flip(core == 1, rows[:, 0], rows[:, 1]), axis=1)
    rows = rows.reshape(2, CHUNK, D).astype(F32)
    cot_pieces = [
        lax.ppermute(lax.dynamic_index_in_dim(cotangent, core ^ j, 0, keepdims=False), ALL, own_moves[j])
        for j in (0, 1)
    ]
    cot_rows = jnp.concatenate(flip(core == 1, cot_pieces[0], cot_pieces[1]), axis=0)
    chunks = jnp.stack([blk, 63 - blk])
    positions = (chunks[:, None] * CHUNK + jnp.arange(CHUNK, dtype=jnp.int32)[None, :]).reshape(-1)
    length = lengths[core]
    own_positions = jnp.where(h == 0, blk, 63 - blk) * CHUNK + jnp.arange(CHUNK, dtype=jnp.int32)
    grad_out = jnp.where((own_positions < length)[:, None], cot_rows, 0).astype(BF)

    own_set = set_index[core]
    sets = jnp.stack([set_index[core], set_index[1 - core]])
    a_own = jnp.take(a_wide, own_set, axis=1)
    bq = lax.dynamic_slice_in_dim(jnp.take(b_wide[0], own_set, axis=0), h * group_cols, group_cols, 1)
    bo = jnp.take(b_wide[1], own_set, axis=0)
    bk, bv = (
        lax.dynamic_slice_in_dim(jnp.take(b_kv[n], own_set, axis=0), h * HEAD, HEAD, 1) for n in (0, 1)
    )
    ao = lax.dynamic_slice_in_dim(a_own[3], h * group_cols, group_cols, 1)
    bias = jnp.concatenate(
        [
            lax.dynamic_slice_in_dim(qkv_bias, h * group_cols, group_cols, 0),
            lax.dynamic_slice_in_dim(qkv_bias, HEADS * HEAD + h * HEAD, HEAD, 0),
            lax.dynamic_slice_in_dim(qkv_bias, HEADS * HEAD + 256 + h * HEAD, HEAD, 0),
        ]
    )
    zero = jnp.zeros
    a_qkv = a_own[:3].reshape(48, D)
    b_qkv = jnp.concatenate(
        [
            jnp.concatenate([bq, zero((16, 256), BF)], axis=1),
            jnp.concatenate([zero((16, group_cols), BF), bk, zero((16, HEAD), BF)], axis=1),
            jnp.concatenate([zero((16, group_cols + HEAD), BF), bv], axis=1),
        ],
        axis=0,
    )
    a_ff = jnp.take(a_wide[4:6], sets, axis=1).transpose(1, 0, 2, 3).reshape(2, 32, D)
    b_cols = lax.dynamic_slice_in_dim(jnp.take(b_ff, sets, axis=1), uly * local_ff, local_ff, 3)
    b_cols = jnp.pad(b_cols, ((0, 0), (0, 0), (0, 0), (0, PADDED - local_ff)))
    a_cols = lax.dynamic_slice_in_dim(jnp.take(a_down, sets, axis=0), uly * local_ff, local_ff, 2)
    a_cols = jnp.pad(a_cols, ((0, 0), (0, 0), (0, PADDED - local_ff)))
    b_out = jnp.take(b_wide[2], sets, axis=0)

    scale_in = norm_scale(rows)
    normed = (rows * scale_in * norm_in).astype(BF).reshape(2 * CHUNK, D)
    latent_qkv = mm("td,rd->tr", normed, a_qkv)
    projected = jnp.concatenate([dot(normed, qkv_w[0]), dot(normed, qkv_w[1])], axis=1)
    projected = projected + bias + mm("tr,ro->to", latent_qkv, b_qkv)
    cos_table, sine_table = rope_tables(positions)
    cos_heads, sine_heads = cos_table[:, None, :], sine_table[:, None, :]
    queries = projected[:, :group_cols].reshape(2 * CHUNK, GROUP, HEAD)
    q = rope_turn(queries, cos_heads, sine_heads) * (HEAD ** (-0.5) * LOG2E)
    q = q.astype(BF).reshape(2 * CHUNK, group_cols)
    k = rope_turn(projected[:, group_cols : group_cols + HEAD], cos_table, sine_table)
    kv = jnp.concatenate([k, projected[:, group_cols + HEAD :]], axis=1).astype(BF)
    kv = kv.reshape(2, CHUNK, 2 * HEAD)
    limit = jnp.minimum(positions, length - 1).reshape(2, 1, 1, CHUNK)
    limit = jnp.broadcast_to(limit, (2, 8, GROUP, CHUNK)).reshape(2, 8, ROWS)
    ff_part = jnp.pad(
        jnp.concatenate([w_gate_up, w_down.T[None]], axis=0), ((0, 0), (0, 0), (0, PADDED - local_ff))
    )
    mixed, lse, kv_all, gate_w, up_w, down_w = attend_forward(q, kv, limit, ff_part)
    gate_w, up_w, down_w = (w.reshape(D, PADDED) for w in (gate_w, up_w, down_w))

    def swap_h(v):
        return lax.ppermute(v, "uly", OVER_H)

    def own_slot(v):
        return flip(h == 1, v[0], v[1])

    latent_o = mm("tc,rc->tr", mixed, ao)
    part = (dot(mixed, out_w) + mm("tr,ro->to", latent_o, bo)).reshape(2, CHUNK, D)
    mine, theirs = own_slot(part)
    attn_out = mine + swap_h(theirs.astype(BF)).astype(F32)
    own_rows = jnp.where(h == 0, rows[0], rows[1])
    residual = own_rows + attn_out
    scale_ff = norm_scale(residual)
    normed_ff = (residual * scale_ff * norm_ff).astype(BF)

    def spread(v):
        across, beside, both = (lax.ppermute(v, "uly", over) for over in (OVER_H, OVER_CORE, OVER_BOTH))
        return jnp.stack([jnp.concatenate([v, across]), jnp.concatenate([beside, both])])

    def collect(v):
        low = v.astype(BF)
        total = v[0, :CHUNK]
        for over, part in ((OVER_H, low[0, CHUNK:]), (OVER_CORE, low[1, :CHUNK]), (OVER_BOTH, low[1, CHUNK:])):
            total = total + lax.ppermute(part, "uly", over).astype(F32)
        return total

    gathered = spread(normed_ff)
    grad_gathered = spread(grad_out)
    latent_ff = mm("std,srd->str", gathered, a_ff)
    gate = mm("std,df->stf", gathered, gate_w) + mm("str,srf->stf", latent_ff[..., :16], b_cols[0])
    up = mm("std,df->stf", gathered, up_w) + mm("str,srf->stf", latent_ff[..., 16:], b_cols[1])
    sigmoid = jax.nn.sigmoid(gate)
    silu = gate * sigmoid
    hidden = (silu * up).astype(BF)
    latent_down = mm("stf,srf->str", hidden, a_cols)
    down = mm("stf,df->std", hidden, down_w) + mm("str,srd->std", latent_down, b_out)
    ff_out = collect(down)
    result = (residual + ff_out).astype(BF)

    latent_back = mm("std,srd->str", grad_gathered, b_out)
    grad_hidden = mm("std,df->stf", grad_gathered, down_w) + mm("str,srf->stf", latent_back, a_cols)
    grad_a_cols = mm("str,stf->srf", latent_back, hidden)
    grad_b_out = mm("str,std->srd", latent_down, grad_gathered)
    grad_up = (grad_hidden * silu).astype(BF)
    grad_gate = (grad_hidden * up * (sigmoid * (1.0 + gate * (1.0 - sigmoid)))).astype(BF)
    back_gate = mm("stf,srf->str", grad_gate, b_cols[0])
    back_up = mm("stf,srf->str", grad_up, b_cols[1])
    back_ff = jnp.concatenate([back_gate, back_up], axis=-1)
    grad_a_ff = mm("str,std->srd", back_ff, gathered)
    grad_b_gate = mm("str,stf->srf", latent_ff[..., :16], grad_gate)
    grad_b_up = mm("str,stf->srf", latent_ff[..., 16:], grad_up)
    grad_ff_in = (
        mm("stf,df->std", grad_gate, gate_w)
        + mm("stf,df->std", grad_up, up_w)
        + mm("str,srd->std", back_ff, a_ff)
    )
    grad_normed_ff = collect(grad_ff_in)
    grad_resid = grad_out.astype(F32) + norm_back(residual, scale_ff, norm_ff, grad_normed_ff)
    grad_attn = grad_resid.astype(BF)
    grad_attn = jnp.concatenate(flip(h == 1, grad_attn, swap_h(grad_attn)), axis=0)

    back_o = mm("td,rd->tr", grad_attn, bo)
    grad_a_o = mm("tr,tc->rc", back_o, mixed)
    grad_b_o = mm("tr,td->rd", latent_o, grad_attn)
    grad_mixed = (mm("td,cd->tc", grad_attn, out_w) + mm("tr,rc->tc", back_o, ao)).astype(BF)
    dq, dkv = attend_backward(q, kv_all, limit, mixed, grad_mixed, lse)
    dkv = dkv.reshape(2 * CHUNK, 2 * HEAD)
    grad_q = rope_back(dq.reshape(2 * CHUNK, GROUP, HEAD), cos_heads, sine_heads)
    grad_k = rope_back(dkv[:, :HEAD], cos_table, sine_table)
    grad_qkv = jnp.concatenate(
        [grad_q.reshape(2 * CHUNK, group_cols), grad_k, dkv[:, HEAD:]], axis=1
    ).astype(BF)
    back_qkv = mm("to,ro->tr", grad_qkv, b_qkv)
    grad_a_qkv = mm("tr,td->rd", back_qkv, normed)
    grad_b_qkv = mm("tr,to->ro", latent_qkv, grad_qkv)
    grad_normed = (
        mm("to,do->td", grad_qkv[:, :512], qkv_w[0])
        + mm("to,do->td", grad_qkv[:, 512:], qkv_w[1])
        + mm("tr,rd->td", back_qkv, a_qkv)
    ).reshape(2, CHUNK, D)
    mine, theirs = own_slot(grad_normed)
    grad_normed = mine + swap_h(theirs.astype(BF)).astype(F32)
    own_scale = jnp.where(h == 0, scale_in[0], scale_in[1])
    input_grad = grad_resid + norm_back(own_rows, own_scale, norm_in, grad_normed)

    def home(v):
        halves = v.astype(BF).reshape(2, CHUNK // 2, D)
        got = [
            lax.ppermute(lax.dynamic_index_in_dim(halves, core ^ j, 0, keepdims=False), ALL, back_moves[j])
            for j in (0, 1)
        ]
        return jnp.stack(flip(core == 1, got[0], got[1]))

    result_tokens = home(result)
    input_grad = home(input_grad).astype(F32)

    def ordered(v):
        return jnp.stack(flip(core == 1, v[0], v[1]))

    def by_sequence(v):
        return jnp.where((core == jnp.arange(2)).reshape((2,) + (1,) * v.ndim), v[None], 0.0)

    def widen(v, total, start):
        full = zero(v.shape[:-1] + (total,), F32)
        return lax.dynamic_update_slice_in_dim(full, v, start, v.ndim - 1)

    col_parts = ordered(jnp.stack([grad_a_cols, grad_b_gate, grad_b_up], axis=1)[..., :local_ff])
    ff_parts = ordered(
        jnp.concatenate([grad_a_ff.reshape(2, 2, 16, D), grad_b_out[:, None]], axis=1)
    )
    o_parts = by_sequence(jnp.stack([widen(grad_a_o, D, h * group_cols), grad_b_o]))
    qkv_parts = by_sequence(
        jnp.concatenate(
            [grad_a_qkv.reshape(3, 16, D), widen(grad_b_qkv[:16, :group_cols], D, h * group_cols)[None]]
        )
    )
    kv_parts = by_sequence(
        jnp.stack(
            [
                widen(grad_b_qkv[16:32, group_cols : group_cols + HEAD], 2 * HEAD, h * HEAD),
                widen(grad_b_qkv[32:, group_cols + HEAD :], 2 * HEAD, h * HEAD),
            ]
        )
    )
    cols = lax.psum(col_parts, "blk")
    cols = lax.all_gather(cols, "uly", axis=3, tiled=True)
    ff_parts, o_parts = lax.psum((ff_parts, o_parts), ALL)
    qkv_parts, kv_parts = lax.psum((qkv_parts, kv_parts), ALL)
    chosen = (jnp.arange(SETS, dtype=jnp.int32)[:, None] == set_index[None, :]).astype(F32)

    def fold(v):
        v = jnp.moveaxis(v, 0, 1)
        pick = chosen[None, :, :, None, None]
        return pick[:, :, 0] * v[:, 0][:, None] + pick[:, :, 1] * v[:, 1][:, None]

    wide_a = jnp.concatenate([qkv_parts[:, :3], o_parts[:, :1], ff_parts[:, :2]], axis=1)
    wide_b = jnp.concatenate([qkv_parts[:, 3:], o_parts[:, 1:], ff_parts[:, 2:]], axis=1)
    return (
        result_tokens,
        input_grad,
        fold(wide_a),
        fold(cols[:, :1])[0],
        fold(wide_b),
        fold(kv_parts),
        fold(cols[:, 1:]),
    )


def solution(mesh):
    spread = P(None, ("blk", "uly"), None)
    in_specs = (
        spread, spread, P(), P(), P(), P(), P(),
        P(("blk", "uly"), None), P(("blk", "uly"), None), P(None, "blk", "uly"), P("uly", "blk"),
        P(), P(), P(), P(), P(),
    )
    out_specs = (spread, spread, P(), P(), P(), P(), P())
    return jax.shard_map(body, mesh=mesh, in_specs=in_specs, out_specs=out_specs, check_vma=False)
```

profile of v0, /device:TPU:1, one launch (start us, length us, event | category | flops | bytes accessed | tf_op | source)
XLA Modules:
  0.0 1141.6 jit_solution(5546512290221942925)
XLA Ops:
  12.9 5.8 all-to-all-start
  67.9 9.8 collective-permute-start
  81.3 45.7 %gather_proj.1 = (bf16[2,1536,512]{2,1,0:T(8,128)(2,1)}, bf16[768,1536]{1,0:T(8,128)(2,1)}) custom-call(bf16[48,512]{1,0:T(8,128)(2,1)} %reshape.805.qkv_ref, bf16[48,384]{1,0:T(8,128)(2,1)} %broadcast_select_fusion.16.out_ref), custom_call_target="tpu_custom_call" | custom-call | tf_op jit(solution)/shard_map/gather_proj/pallas_call | solution.py:243
  138.5 6.5 collective-permute-start.21
  159.1 144.9 %attend_forward.1 = (bf16[256,768]{1,0:T(8,128)(2,1)S(1)}, f32[2,8,768]{2,1,0:T(8,128)S(1)}, bf16[64,128,256]{2,1,0:T(8,128)(2,1)S(1)}, bf16[32,48,2304]{2,1,0:T...) custom-call(bf16[256,768]{1,0:T(8,128)(2,1)S(1)} %multiply_convert_fusion.5.q_ref, ...), custom_call_target="tpu_custom_call" | custom-call | tf_op jit(solution)/shard_map/attend_forward/pallas_call | solution.py:370
  312.8 5.9 collective-permute-done.8
  320.6 6.4 collective-permute-start.11
  332.5 8.8 fusion.26
  366.4 6.1 fusion.118
  376.0 5.8 convolution_add_fusion.5
  407.8 8.5 collective-permute-done.14
  416.3 6.9 collective-permute-done.12
  435.7 18.9 %collective-permute-done.25 = bf16[128,1536]{1,0:T(8,128)(2,1)S(1)} collective-permute-done((bf16[128,1536]{1,0:T(8,128)(2,1)S(1)}, bf16[128,1536]{1,0:T(8,128)(2,1)S(1)}, u32[]{:S(2)}, u32[]{:S(2)}) %collective-permute-start.25) | collective-permute-done | bytes 393248 | tf_op jit(solution)/shard_map/ppermute | solution.py:750
  457.7 68.2 %attend_backward.1 = (f32[256,768]{1,0:T(8,128)}, f32[2,128,256]{2,1,0:T(8,128)}) custom-call(bf16[256,768]{1,0:T(8,128)(2,1)} %copy-done.5, bf16[64,128,256]{2,1,0:T(8,128)(2,1)} %copy-done.4, s32[2,8,768]{2,1,0:T(8,128)} %copy-done.6, bf16[256,768]{1,0:T(8,128)(2,1)} %copy-done.2, bf16[256,768]{1,0:T(8,128)(2,1)} %fusion.14.grad_ref, f32[2,8,768]{2,1,0:T(8,128)} %copy-done.7), custom_call_target="tpu_custom_call" | custom-call | tf_op jit(solution)/shard_map/attend_backward/pallas_call | solution.py:534
  545.9 146.8 %all-reduce.9.cloned.1.call-done = f32[2,3,16,2240]{3,2,0,1:T(8,128)} async-done(((f32[2,3,16,2240]{3,2,0,1:T(8,128)}), f32[2,3,16,2240]{3,2,0,1:T(8,128)}) %all-reduce.9.cloned.1.call-update) | async-done | bytes 860176 | tf_op jit(solution)/shard_map/psum | solution.py:873
  692.7 9.0 copy.57
  703.3 19.9 %collective-permute-start.27 = (bf16[64,1536]{1,0:T(8,128)(2,1)S(1)}, bf16[64,1536]{1,0:T(8,128)(2,1)S(1)}, u32[]{:S(2)}, u32[]{:S(2)}) collective-permute-start(bf16[64,1536]{1,0:T(8,128)(2,1)S(1)} %get-tuple-element.111), channel_id=1, source_target_pairs={{1,0},{0,1},{5,2},{4,3},{9,4},{8,5},{13,6},{12,7},{17,8},{16,9},{2... | collective-permute-start | bytes 589832 | tf_op jit(solution)/shard_map/ppermute | solution.py:837
  725.6 154.4 %all-reduce.11.cloned.1.call-done = (f32[2,3,16,1536]{3,2,1,0:T(8,128)}, f32[2,2,16,1536]{3,2,1,0:T(8,128)}, f32[2,4,16,1536]{3,2,1,0:T(8,128)}, f32[2,2,16,256]{3,2,0,1:T(8,128)}) async-done(((f32[2,3,16,1536]{3,2,1,0:T(8,128)}, f32[2,2,16,1536]{3,2,1,0:T(8,128)}, f32[2,4,16,1536]{3,2,1,0:T(8,128)}, f32[2,2,16,256]{3,2,0,1:T(8,128)}), (f32[2,3,16,1536]{3,2,1,0:T(8,128)}, f32[2,2,16,1536]{3,2,1,0:T(8,128)}, ...) | async-done | bytes 1835024 | tf_op jit(solution)/shard_map/psum | solution.py:875
  890.0 163.3 %all-gather.2.cloned.1.call-done = f32[2,3,16,8960]{2,0,1,3:T(2,128)} async-done(((f32[2,3,16,2240]{2,0,1,3:T(2,128)}), f32[2,3,16,8960]{2,0,1,3:T(2,128)}) %all-gather.2.cloned.1.call-update) | async-done | bytes 3440656 | tf_op jit(solution)/shard_map/all_gather | solution.py:874
  1058.1 8.3 fusion.108
  1072.3 13.0 %slice_bitcast_fusion = f32[2,2,16,8960]{2,1,0,3:T(2,128)} fusion(f32[2,3,16,8960]{2,0,1,3:T(2,128)} %all-gather.2.cloned.1.call-done), kind=kLoop, calls=%fused_computation.5 | loop fusion | bytes 4587520 | tf_op jit(solution)/shard_map/transpose | solution.py:880
  1085.3 21.3 %fusion.107 = (f32[2,1,16,8960]{2,1,0,3:T(1,128)}, f32[2,1,16,8960]{2,1,0,3:T(1,128)}) fusion(f32[2,2,16,8960]{2,1,0,3:T(2,128)} %slice_bitcast_fusion), kind=kLoop, calls=%fused_computation.313 | loop fusion | bytes 4587520 | tf_op jit(solution)/shard_map/slice | solution.py:882
  1106.6 9.5 copy.61
  1116.2 10.8 copy.60
  (400 shorter events, 218.9 us)
Async XLA Ops:
  9.2 117.9 %collective-permute-start.3 = (bf16[64,1536]{1,0:T(8,128)(2,1)}, bf16[64,1536]{1,0:T(8,128)(2,1)}, u32[]{:S(2)}, u32[]{:S(2)}) collective-permute-start(bf16[64,1536]{1,0:T(8,128)(2,1)} %get-tuple-element.122), channel_id=1, source_target_pairs={{0,1},{1,0},{2,7},{3,6},{4,9},{5,8},{6,15},{7,14},{8,17},{9,16},{1... | collective-permute-start | bytes 589832 | tf_op jit(solution)/shard_map/ppermute | solution.py:675
  12.9 67.0 %all-to-all-start = ((bf16[4,12,512]{2,1,0:T(8,128)(2,1)}), bf16[4,12,512]{2,1,0:T(8,128)(2,1)}, u32[]{:S(2)}, u32[]{:S(2)}) async-start(bf16[4,12,512]{2,1,0:T(8,128)(2,1)} %copy.46), calls=%async_computation | async-start | bytes 131072 | tf_op jit(solution)/shard_map/all_to_all | solution.py:660
  18.7 674.0 %all-reduce.9.cloned.1.call-start = ((), (), s32[]{:S(2)}) async-start(), calls=%async_computation.1 | async-start | bytes 1769472 | tf_op jit(solution)/shard_map/psum | solution.py:873
  20.2 44.1 %collective-permute-start.7 = (bf16[12,384]{1,0:T(8,128)(2,1)}, bf16[12,384]{1,0:T(8,128)(2,1)}, u32[]{:S(2)}, u32[]{:S(2)}) collective-permute-start(bf16[12,384]{1,0:T(8,128)(2,1)} %bitcast.289), channel_id=1, source_target_pairs={{0,5},{1,0},{2,1},{3,4},{4,13},{5,8},{6,9},{7,12},{8,21},{9,16},{1... | collective-permute-start | bytes 27656 | tf_op jit(solution)/shard_map/ppermute | solution.py:663
  20.8 46.4 %collective-permute-start.6 = (bf16[12,384]{1,0:T(8,128)(2,1)}, bf16[12,384]{1,0:T(8,128)(2,1)}, u32[]{:S(2)}, u32[]{:S(2)}) collective-permute-start(bf16[12,384]{1,0:T(8,128)(2,1)} %bitcast.290), channel_id=1, source_target_pairs={{0,4},{1,5},{2,0},{3,1},{4,12},{5,13},{6,8},{7,9},{8,20},{9,21},{1... | collective-permute-start | bytes 27656 | tf_op jit(solution)/shard_map/ppermute | solution.py:663
  24.1 43.8 %collective-permute-start.5 = (bf16[12,384]{1,0:T(8,128)(2,1)}, bf16[12,384]{1,0:T(8,128)(2,1)}, u32[]{:S(2)}, u32[]{:S(2)}) collective-permute-start(bf16[12,384]{1,0:T(8,128)(2,1)} %bitcast.291), channel_id=1, source_target_pairs={{0,1},{1,4},{2,5},{3,0},{4,9},{5,12},{6,13},{7,8},{8,17},{9,20},{1... | collective-permute-start | bytes 27656 | tf_op jit(solution)/shard_map/ppermute | solution.py:663
  28.7 48.9 %collective-permute-start.4 = (bf16[12,384]{1,0:T(8,128)(2,1)}, bf16[12,384]{1,0:T(8,128)(2,1)}, u32[]{:S(2)}, u32[]{:S(2)}) collective-permute-start(bf16[12,384]{1,0:T(8,128)(2,1)} %bitcast.292), channel_id=1, source_target_pairs={{0,0},{1,1},{2,4},{3,5},{4,8},{5,9},{6,12},{7,13},{8,16},{9,17},{1... | collective-permute-start | bytes 27656 | tf_op jit(solution)/shard_map/ppermute | solution.py:663
  64.2 64.4 %collective-permute-start.1 = (bf16[64,1536]{1,0:T(8,128)(2,1)}, bf16[64,1536]{1,0:T(8,128)(2,1)S(1)}, u32[]{:S(2)}, u32[]{:S(2)}) collective-permute-start(bf16[64,1536]{1,0:T(8,128)(2,1)} %get-tuple-element.122), channel_id=1, source_target_pairs={{0,3},{1,2},{2,5},{3,4},{4,11},{5,10},{6,13},{7,12},{8,19},{9,18},... | collective-permute-start | bytes 589832 | tf_op jit(solution)/shard_map/ppermute | solution.py:675
  67.2 61.5 %collective-permute-start.2 = (bf16[64,1536]{1,0:T(8,128)(2,1)S(1)}, bf16[64,1536]{1,0:T(8,128)(2,1)S(1)}, u32[]{:S(2)}, u32[]{:S(2)}) collective-permute-start(bf16[64,1536]{1,0:T(8,128)(2,1)S(1)} %copy-done.35), channel_id=1, source_target_pairs={{0,0},{1,1},{2,6},{3,7},{4,8},{5,9},{6,14},{7,15},{8,16},{9,17},{1... | collective-permute-start | bytes 589832 | tf_op jit(solution)/shard_map/ppermute | solution.py:675
  67.9 60.8 %collective-permute-start = (bf16[64,1536]{1,0:T(8,128)(2,1)S(1)}, bf16[64,1536]{1,0:T(8,128)(2,1)S(1)}, u32[]{:S(2)}, u32[]{:S(2)}) collective-permute-start(bf16[64,1536]{1,0:T(8,128)(2,1)S(1)} %copy-done.35), channel_id=1, source_target_pairs={{0,2},{1,3},{2,4},{3,5},{4,10},{5,11},{6,12},{7,13},{8,18},{9,19},... | collective-permute-start | bytes 589832 | tf_op jit(solution)/shard_map/ppermute | solution.py:675
  77.7 58.9 %collective-permute-start.17 = (bf16[64,1536]{1,0:T(8,128)(2,1)}, bf16[64,1536]{1,0:T(8,128)(2,1)}, u32[]{:S(2)}, u32[]{:S(2)}) collective-permute-start(bf16[64,1536]{1,0:T(8,128)(2,1)} %get-tuple-element.115), channel_id=1, source_target_pairs={{0,1},{1,0},{2,5},{3,4},{4,9},{5,8},{6,13},{7,12},{8,17},{9,16},{1... | collective-permute-start | bytes 589832 | tf_op jit(solution)/shard_map/ppermute | solution.py:685
  138.5 192.6 %collective-permute-start.21 = (bf16[128,1536]{1,0:T(8,128)(2,1)}, bf16[128,1536]{1,0:T(8,128)(2,1)}, u32[]{:S(2)}, u32[]{:S(2)}) collective-permute-start(bf16[128,1536]{1,0:T(8,128)(2,1)} %maximum_select_fusion), channel_id=1, source_target_pairs={{0,3},{3,0},{1,2},{2,1},{4,7},{7,4},{5,6},{6,5},{8,11},{11,8},{9,1... | collective-permute-start | bytes 1179656 | tf_op jit(solution)/shard_map/ppermute | solution.py:765
  144.9 186.1 %collective-permute-start.20 = (bf16[128,1536]{1,0:T(8,128)(2,1)}, bf16[128,1536]{1,0:T(8,128)(2,1)}, u32[]{:S(2)}, u32[]{:S(2)}) collective-permute-start(bf16[128,1536]{1,0:T(8,128)(2,1)} %maximum_select_fusion), channel_id=1, source_target_pairs={{0,1},{1,0},{2,3},{3,2},{4,5},{5,4},{6,7},{7,6},{8,9},{9,8},{10,11... | collective-permute-start | bytes 1179656 | tf_op jit(solution)/shard_map/ppermute | solution.py:765
  144.9 182.1 %collective-permute-start.19 = (bf16[128,1536]{1,0:T(8,128)(2,1)}, bf16[128,1536]{1,0:T(8,128)(2,1)}, u32[]{:S(2)}, u32[]{:S(2)}) collective-permute-start(bf16[128,1536]{1,0:T(8,128)(2,1)} %maximum_select_fusion), channel_id=1, source_target_pairs={{0,2},{2,0},{1,3},{3,1},{4,6},{6,4},{5,7},{7,5},{8,10},{10,8},{9,1... | collective-permute-start | bytes 1179656 | tf_op jit(solution)/shard_map/ppermute | solution.py:765
  320.6 24.6 %collective-permute-start.11 = (bf16[128,1536]{1,0:T(8,128)(2,1)S(1)}, bf16[128,1536]{1,0:T(8,128)(2,1)S(1)}, u32[]{:S(2)}, u32[]{:S(2)}) collective-permute-start(bf16[128,1536]{1,0:T(8,128)(2,1)S(1)} %multiply_convert_fusion.4), channel_id=1, source_target_pairs={{0,3},{3,0},{1,2},{2,1},{4,7},{7,4},{5,6},{6,5},{8,11},{11,8},{9,1... | collective-permute-start | bytes 1179656 | tf_op jit(solution)/shard_map/ppermute | solution.py:765
  392.9 23.4 %collective-permute-start.14 = (bf16[128,1536]{1,0:T(8,128)(2,1)}, bf16[128,1536]{1,0:T(8,128)(2,1)}, u32[]{:S(2)}, u32[]{:S(2)}) collective-permute-start(bf16[128,1536]{1,0:T(8,128)(2,1)} %get-tuple-element.81), channel_id=1, source_target_pairs={{0,3},{3,0},{1,2},{2,1},{4,7},{7,4},{5,6},{6,5},{8,11},{11,8},{9,1... | collective-permute-start | bytes 1179656 | tf_op jit(solution)/shard_map/ppermute | solution.py:772
  397.1 482.9 %all-reduce.11.cloned.1.call-start = ((), (), s32[]{:S(2)}) async-start(), calls=%async_computation.3 | async-start | bytes 3670016 | tf_op jit(solution)/shard_map/psum | solution.py:875
  400.3 22.8 %collective-permute-start.12 = (bf16[128,1536]{1,0:T(8,128)(2,1)}, bf16[128,1536]{1,0:T(8,128)(2,1)S(1)}, u32[]{:S(2)}, u32[]{:S(2)}) collective-permute-start(bf16[128,1536]{1,0:T(8,128)(2,1)} %get-tuple-element.80), channel_id=1, source_target_pairs={{0,2},{2,0},{1,3},{3,1},{4,6},{6,4},{5,7},{7,5},{8,10},{10,8},{9,1... | collective-permute-start | bytes 1179656 | tf_op jit(solution)/shard_map/ppermute | solution.py:772
  426.4 28.2 %collective-permute-start.25 = (bf16[128,1536]{1,0:T(8,128)(2,1)S(1)}, bf16[128,1536]{1,0:T(8,128)(2,1)S(1)}, u32[]{:S(2)}, u32[]{:S(2)}) collective-permute-start(bf16[128,1536]{1,0:T(8,128)(2,1)S(1)} %get-tuple-element.66), channel_id=1, source_target_pairs={{0,2},{2,0},{1,3},{3,1},{4,6},{6,4},{5,7},{7,5},{8,10},{10,8},{9,1... | collective-permute-start | bytes 1179656 | tf_op jit(solution)/shard_map/ppermute | solution.py:750
  431.7 112.5 %collective-permute-start.15 = (bf16[64,1536]{1,0:T(8,128)(2,1)}, bf16[64,1536]{1,0:T(8,128)(2,1)}, u32[]{:S(2)}, u32[]{:S(2)}) collective-permute-start(bf16[64,1536]{1,0:T(8,128)(2,1)} %get-tuple-element.119), channel_id=1, source_target_pairs={{1,0},{0,1},{5,2},{4,3},{9,4},{8,5},{13,6},{12,7},{17,8},{16,9},{2... | collective-permute-start | bytes 589832 | tf_op jit(solution)/shard_map/ppermute | solution.py:837
  432.7 111.5 %collective-permute-start.16 = (bf16[64,1536]{1,0:T(8,128)(2,1)}, bf16[64,1536]{1,0:T(8,128)(2,1)}, u32[]{:S(2)}, u32[]{:S(2)}) collective-permute-start(bf16[64,1536]{1,0:T(8,128)(2,1)} %get-tuple-element.120), channel_id=1, source_target_pairs={{0,0},{1,1},{4,2},{5,3},{8,4},{9,5},{12,6},{13,7},{16,8},{17,9},{2... | collective-permute-start | bytes 589832 | tf_op jit(solution)/shard_map/ppermute | solution.py:837
  542.8 510.5 %all-gather.2.cloned.1.call-start = ((), (), s32[]{:S(2)}) async-start(), calls=%async_computation.2 | async-start | bytes 34406400 | tf_op jit(solution)/shard_map/all_gather | solution.py:874
  542.9 158.9 %collective-permute-start.26 = (bf16[128,1536]{1,0:T(8,128)(2,1)S(1)}, bf16[128,1536]{1,0:T(8,128)(2,1)S(1)}, u32[]{:S(2)}, u32[]{:S(2)}) collective-permute-start(bf16[128,1536]{1,0:T(8,128)(2,1)S(1)} %select_convert_fusion), channel_id=1, source_target_pairs={{0,2},{2,0},{1,3},{3,1},{4,6},{6,4},{5,7},{7,5},{8,10},{10,8},{9,1... | collective-permute-start | bytes 1179656 | tf_op jit(solution)/shard_map/ppermute | solution.py:750
  703.3 21.4 %collective-permute-start.27 = (bf16[64,1536]{1,0:T(8,128)(2,1)S(1)}, bf16[64,1536]{1,0:T(8,128)(2,1)S(1)}, u32[]{:S(2)}, u32[]{:S(2)}) collective-permute-start(bf16[64,1536]{1,0:T(8,128)(2,1)S(1)} %get-tuple-element.111), channel_id=1, source_target_pairs={{1,0},{0,1},{5,2},{4,3},{9,4},{8,5},{13,6},{12,7},{17,8},{16,9},{2... | collective-permute-start | bytes 589832 | tf_op jit(solution)/shard_map/ppermute | solution.py:837
  (82 other events, 1726.6 us)
Sparse Core Ops, SparseCore 0:
  397.2 295.4 all-reduce.8
  699.6 180.3 all-reduce.10
  882.3 170.9 all-gather.1
where the time goes:
time: 1150 us; the launch traced here: 1140 us
  waiting for transfers between devices  512 us (45%)
  Pallas kernels  259 us (23%)
  local copies, waits for them, and re-layouts  139 us (12%)
  starting transfers between devices  84.6 us (7%)
  other arithmetic  65.4 us (6%)
  matrix products  63.1 us (5%)
  between operations  18.3 us (2%)
    all_gather x1, waiting for transfers between devices, body(): cols = lax.all_gather(cols, 'uly', axis=3, tiled=True)  163 us
    psum x1, waiting for transfers between devices, body(): ff_parts, o_parts = lax.psum((ff_parts, o_parts), ALL)  154 us
    psum x1, waiting for transfers between devices, body(): cols = lax.psum(col_parts, 'blk')  147 us
    pallas_call x1, Pallas kernels, attend_forward(): pl.pallas_call(forward_kernel, out_shape=(jax.ShapeDtypeStruct((2 * CHUNK...  145 us
    pallas_call x1, Pallas kernels, attend_backward(): pl.pallas_call(backward_kernel, out_shape=(jax.ShapeDtypeStruct((2 * CHUN...  68.2 us
    dot_general x36, matrix products, mm(): jnp.einsum(spec, a.astype(BF), b.astype(BF), preferred_element_type=F32)  61.2 us
    pallas_call x1, Pallas kernels, gather_proj(): pl.pallas_call(proj_kernel, out_shape=(jax.ShapeDtypeStruct((2, D, 512),...  45.7 us
    slice x2, local copies, waits for them, and re-layouts, fold(): return pick[:, :, 0] * v[:, 0][:, None] + pick[:, :, 1] * v[:, 1][:, None]  29.6 us
  transfers between devices with their start and end apart: 33, of which 9 were waited for; matrix products, arithmetic and copies ran while one was open for 12% of the time, Pallas kernels for 23%

commit v1 on v0

v1 whole, which is shorter than its diff:
```python
import functools

import jax
import jax.numpy as jnp
import numpy as np
from jax import lax
from jax.experimental import pallas as pl
from jax.experimental.pallas import tpu as pltpu
from jax.sharding import PartitionSpec as P

HEADS = 12
KV_HEADS = 2
HEAD = 128
GROUP = HEADS // KV_HEADS
FF = 8960
SETS = 8
D = 1536
CHUNK = 128
CHUNKS = 64
PADDED = 2304
EPS = 1e-06
THETA = 1000000.0
LOG2E = 1.4426950408889634
LN2 = 0.6931471805599453
MESH = pl.DeviceIdType.MESH
BF = jnp.bfloat16
F32 = jnp.float32
ANY = pl.BlockSpec(memory_space=pl.ANY)
IN_VMEM = pl.BlockSpec(memory_space=pltpu.VMEM)


def blk_of(y, z, x):
    return y * 16 + z * 4 + x


def place():
    blk = lax.axis_index("blk")
    return blk // 16, (blk // 4) % 4, blk % 4, blk, lax.axis_index("uly")


def ring_others():
    y, z, x, blk, uly = place()
    return [
        (blk_of(1 - y, z, x), uly),
        (blk_of(y, z, (x + 1) % 4), uly),
        (blk_of(y, z, (x + 3) % 4), uly),
        (blk_of(y, (z + 1) % 4, x), uly),
        (blk_of(y, (z + 3) % 4, x), uly),
    ]


def greet(others):
    barrier = pltpu.get_barrier_semaphore()
    for other in others:
        pl.semaphore_signal(barrier, inc=1, device_id=other, device_id_type=MESH)
    pl.semaphore_wait(barrier, len(others))


class Gather:
    sends = 31

    def __init__(self, src, dst, send_sem, recv_sem, local_sem, orders=(0, 1)):
        self.src, self.dst, self.orders = src, dst, orders
        self.streams = range(len(orders))
        self.send_sem, self.recv_sem, self.local_sem = send_sem, recv_sem, local_sem
        self.y, self.z, self.x, self.blk, self.uly = place()
        self.count = [0] * len(orders)
        self.sent = []
        self.local = []

    def at(self, stream, y, p, q):
        order = self.orders[stream]
        return blk_of(y, order * p + (1 - order) * q, order * q + (1 - order) * p)

    def pq(self, stream):
        order = self.orders[stream]
        return (
            order * self.z + (1 - order) * self.x,
            order * self.x + (1 - order) * self.z,
        )

    def send(self, stream, item, target, src=None):
        copy = pltpu.make_async_remote_copy(
            src_ref=self.dst(stream, item) if src is None else src,
            dst_ref=self.dst(stream, item),
            send_sem=self.send_sem.at[stream, self.count[stream]],
            recv_sem=self.recv_sem.at[stream, item],
            device_id=(target, self.uly),
            device_id_type=MESH,
        )
        self.count[stream] += 1
        copy.start()
        self.sent.append(copy)

    def wait(self, stream, item):
        ref = self.dst(stream, item)
        pltpu.make_async_remote_copy(
            src_ref=ref,
            dst_ref=ref,
            send_sem=self.send_sem.at[stream, 0],
            recv_sem=self.recv_sem.at[stream, item],
            device_id=(self.blk, self.uly),
            device_id_type=MESH,
        ).wait_recv()

    def start(self):
        for s in self.streams:
            p, q = self.pq(s)
            self.send(s, self.blk, self.at(s, 1 - self.y, p, q), self.src(s))
        for s in self.streams:
            p, q = self.pq(s)
            for d in (1, 3):
                self.send(s, self.blk, self.at(s, self.y, (p + d) % 4, q), self.src(s))
            copy = pltpu.make_async_copy(self.src(s), self.dst(s, self.blk), self.local_sem.at[s])
            copy.start()
            self.local.append(copy)

    def second(self):
        for s in self.streams:
            p, q = self.pq(s)
            item = self.at(s, 1 - self.y, p, q)
            self.wait(s, item)
            for d in (1, 3):
                self.send(s, item, self.at(s, self.y, (p + d) % 4, q))
            for d in (1, 3):
                onward = self.at(s, self.y, p, (q + d) % 4)
                self.send(s, self.blk, onward, self.src(s))
                self.send(s, item, onward)

    def spread(self, s, item):
        p, q = self.pq(s)
        for d in (1, 3):
            self.send(s, item, self.at(s, self.y, p, (q + d) % 4))

    def third(self):
        for k, y in enumerate((self.y, 1 - self.y)):
            for s in self.streams:
                p, q = self.pq(s)
                for d in (3, 1):
                    item = self.at(s, y, (p + d) % 4, q)
                    self.wait(s, item)
                    if (d == 3) == (k == 0):
                        self.send(s, item, self.at(s, self.y, (p + 4 - d) % 4, q))
                    self.spread(s, item)
        for y in (self.y, 1 - self.y):
            for s in self.streams:
                p, q = self.pq(s)
                item = self.at(s, y, (p + 2) % 4, q)
                self.wait(s, item)
                self.spread(s, item)

    def fourth(self):
        for e in (0, 1, 3, 2):
            for k, y in enumerate((self.y, 1 - self.y)):
                for s in self.streams:
                    p, q = self.pq(s)
                    for d in (3, 1):
                        item = self.at(s, y, (p + e) % 4, (q + d) % 4)
                        self.wait(s, item)
                        if (d == 3) == (k == 0):
                            self.send(s, item, self.at(s, self.y, p, (q + 4 - d) % 4))

    def last(self):
        for e in (0, 1, 3, 2):
            for y in (self.y, 1 - self.y):
                for s in self.streams:
                    p, q = self.pq(s)
                    self.wait(s, self.at(s, y, (p + e) % 4, (q + 2) % 4))
        for copy in self.local:
            copy.wait()
        for copy in self.sent:
            copy.wait_send()


GATHER_SEMS = lambda *lead: [
    pltpu.SemaphoreType.DMA(lead + (2, Gather.sends)),
    pltpu.SemaphoreType.DMA(lead + (2, 32)),
    pltpu.SemaphoreType.DMA(lead + (2,)),
]


KEYS = 512
STEP = KEYS // CHUNK
ROWS = GROUP * CHUNK


def head_columns(ref, slot):
    return jnp.concatenate(
        [
            ref[slot * CHUNK : (slot + 1) * CHUNK, n * HEAD : (n + 1) * HEAD].T
            for n in range(GROUP)
        ],
        axis=1,
    )


def head_rows(ref, slot):
    return jnp.concatenate(
        [
            ref[slot * CHUNK : (slot + 1) * CHUNK, n * HEAD : (n + 1) * HEAD]
            for n in range(GROUP)
        ],
        axis=0,
    )


def key_block(kv_ref, step):
    rows = kv_ref[pl.ds(step * STEP, STEP)].reshape(KEYS, 2 * HEAD)
    return rows[:, :HEAD], rows[:, HEAD:]


def dot(a, b):
    return jnp.dot(a, b, preferred_element_type=F32)


def key_places(step):
    return lax.broadcasted_iota(jnp.int32, (KEYS, ROWS), 0) + step * KEYS


def dot_nt(a, b):
    return lax.dot_general(a, b, (((1,), (1,)), ((), ())), preferred_element_type=F32)


def forward_slot(slot, chunk, part, q_ref, kv_ref, limit_ref, mixed_ref, lse_ref, acc_ref, stat_ref):
    turned = head_columns(q_ref, slot)
    limit = limit_ref[slot, 0:1, :]
    if part == 0:
        acc_ref[...] = jnp.zeros_like(acc_ref)
        stat_ref[0] = jnp.full(stat_ref.shape[1:], -1e30, F32)
        stat_ref[1] = jnp.zeros(stat_ref.shape[1:], F32)

    def step(n, carry):
        top, total = carry
        keys, values = key_block(kv_ref, n)
        scores = jnp.where(key_places(n) <= limit, dot(keys, turned), -1e30)
        new_top = jnp.maximum(top, jnp.max(scores, axis=0, keepdims=True))
        fade = jnp.exp2(top - new_top)
        probs = jnp.exp2(scores - new_top)
        total = total * fade + jnp.sum(probs, axis=0, keepdims=True)
        acc_ref[...] = acc_ref[...] * fade + dot(values.T, probs.astype(BF))
        return new_top, total

    blocks = chunk // STEP + 1
    top, total = lax.fori_loop(
        blocks * part // 4, blocks * (part + 1) // 4, step, (stat_ref[0, 0:1, :], stat_ref[1, 0:1, :])
    )
    if part < 3:
        stat_ref[0, 0:1, :] = top
        stat_ref[1, 0:1, :] = total
        return
    out = acc_ref[...] / total
    for n in range(GROUP):
        mixed_ref[slot * CHUNK : (slot + 1) * CHUNK, n * HEAD : (n + 1) * HEAD] = out[
            :, n * CHUNK : (n + 1) * CHUNK
        ].T.astype(BF)
    lse_ref[slot] = jnp.broadcast_to(top + jnp.log2(total), (8, ROWS))


def uly_others():
    y, z, x, blk, uly = place()
    return [(blk, (uly + 2) % 4), (blk, uly + 1 - 2 * (uly % 2)), (blk, 3 - uly)]


def ring_place(w):
    y, z, x, blk, uly = place()
    return (blk_of(w % 2, z, x), (w // 2) * 2 + uly % 2)


def ring_at():
    y, z, x, blk, uly = place()
    return (uly // 2) * 2 + y


def wait_arrival(ref, sem):
    pltpu.make_async_copy(ref, ref, sem).wait()


def remote(src, dst, send, recv, device):
    return pltpu.make_async_remote_copy(
        src_ref=src, dst_ref=dst, send_sem=send, recv_sem=recv, device_id=device, device_id_type=MESH
    )


class Deliver:
    def __init__(self):
        self.sent = []

    def send(self, src, dst, send, recv, device):
        y, z, x, blk, uly = place()
        here = jnp.logical_and(device[0] == blk, device[1] == uly)

        @pl.when(here)
        def _():
            pltpu.make_async_copy(src, dst, recv).start()

        @pl.when(jnp.logical_not(here))
        def _():
            remote(src, dst, send, recv, device).start()

        self.sent.append((here, src, dst, send, recv, device))

    def end(self):
        for here, *copy in self.sent:

            @pl.when(jnp.logical_not(here))
            def _():
                remote(*copy).wait_send()


class Ring:
    sends = 15

    def __init__(self, src, dst, y, order, way, send_sem, recv_sem):
        self.src, self.dst, self.y, self.order, self.way = src, dst, y, order, way
        self.send_sem, self.recv_sem = send_sem, recv_sem
        self.own_y, self.z, self.x, self.blk, self.uly = place()
        self.p = order * self.z + (1 - order) * self.x
        self.q = order * self.x + (1 - order) * self.z
        self.sent = []

    def at(self, y, p, q):
        order = self.order
        return blk_of(y, order * p + (1 - order) * q, order * q + (1 - order) * p)

    def index(self, p, q):
        return self.at(0, p, q)

    def send(self, p, q, dp, dq, src=None):
        ref = self.dst(self.at(self.y, p, q))
        target = self.at(self.own_y, (self.p + dp) % 4, (self.q + dq) % 4)
        copy = remote(
            ref if src is None else src, ref, self.send_sem.at[len(self.sent)],
            self.recv_sem.at[self.index(p, q)], (target, self.uly),
        )
        copy.start()
        self.sent.append(copy)

    def wait(self, p, q):
        wait_arrival(self.dst(self.at(self.y, p, q)), self.recv_sem.at[self.index(p, q)])

    def start(self):
        for d in (1, 3):
            self.send(self.p, self.q, d, 0, self.src)
        for d in (1, 3):
            self.send(self.p, self.q, 0, d, self.src)

    def third(self):
        for d in (4 - self.way, self.way):
            p = (self.p + d) % 4
            self.wait(p, self.q)
            if d == 4 - self.way:
                self.send(p, self.q, self.way, 0)
            for e in (1, 3):
                self.send(p, self.q, 0, e)

    def third_late(self):
        p = (self.p + 2) % 4
        self.wait(p, self.q)
        for e in (1, 3):
            self.send(p, self.q, 0, e)

    def fourth(self, e):
        p = (self.p + e) % 4
        for d in (4 - self.way, self.way):
            q = (self.q + d) % 4
            self.wait(p, q)
            if d == 4 - self.way:
                self.send(p, q, 0, self.way)

    def last(self):
        for e in (0, 1, 3, 2):
            self.wait((self.p + e) % 4, (self.q + 2) % 4)
        for copy in self.sent:
            copy.wait_send()


class Spread:
    def __init__(self, own, all_ref, send_sem, recv_sem, local_sem):
        self.own, self.all_ref = own, all_ref
        self.send_sem, self.recv_sem, self.local_sem = send_sem, recv_sem, local_sem
        self.w = ring_at()
        self.core = lax.axis_index("uly") % 2
        self.sibling = uly_others()[1]
        self.sent = []

    def piece(self, d, rows=slice(None), core=None):
        core = self.core if core is None else core
        ref = self.all_ref.at[core, (self.w + d) % 4]
        return ref if rows == slice(None) else ref.at[pl.ds(rows.start, rows.stop - rows.start)]

    def send(self, src, dst, recv, device):
        copy = remote(src, dst, self.send_sem.at[len(self.sent)], self.recv_sem.at[recv], device)
        copy.start()
        self.sent.append(copy)

    def pair(self, d, src=None):
        self.send(self.piece(d) if src is None else src, self.piece(d), 4 + d, self.sibling)

    def start(self):
        self.local = pltpu.make_async_copy(self.own, self.piece(0), self.local_sem)
        self.local.start()
        self.send(self.own, self.piece(0), 0, ring_place((self.w + 1) % 4))
        self.send(self.own, self.piece(0), 1, ring_place((self.w + 3) % 4))
        self.pair(0, self.own)

    def second(self):
        half = CHUNK // 2
        wait_arrival(self.piece(3), self.recv_sem.at[0])
        low = self.piece(3, slice(0, half))
        self.send(low, low, 2, ring_place((self.w + 1) % 4))
        self.pair(3)
        wait_arrival(self.piece(1), self.recv_sem.at[1])
        high = self.piece(1, slice(half, CHUNK))
        self.send(high, high, 3, ring_place((self.w + 3) % 4))
        self.pair(1)

    def third(self):
        half = CHUNK // 2
        wait_arrival(self.piece(2, slice(0, half)), self.recv_sem.at[2])
        wait_arrival(self.piece(2, slice(half, CHUNK)), self.recv_sem.at[3])
        self.pair(2)

    def last(self):
        for d in range(4):
            wait_arrival(self.piece(d, core=1 - self.core), self.recv_sem.at[4 + d])
        for copy in self.sent:
            copy.wait_send()
        self.local.wait()


SPREAD_SEMS = [pltpu.SemaphoreType.DMA((8,)), pltpu.SemaphoreType.DMA((8,)), pltpu.SemaphoreType.DMA]
FF_COLS = PADDED // 2


def forward_kernel(
    qkv_ref, out_ref, tokens_ref, cot_ref, ff_ref, limit_ref, length_ref, norm_in_ref, norm_ff_ref, bias_ref, cos_ref, sin_ref,
    a_qkv_ref, b_qkv_ref, ao_ref, bo_ref,
    q_ref, mixed_ref, lse_ref, kv_out, wq_out, wo_out, gate_all, up_all, down_all, rows_out, normed_ref,
    latent_ref, resid_ref, cot_own, nf_all, cot_all,
    kv_all, wq_all, wo_all, rows, cot_in, kv_part, acc_ref, stat_ref, qkv_in, out_in, qkv_part, out_part,
    nf_own, cross_out, cross_in,
    *sems,
):
    y, z, x, blk, uly = place()
    core, h = uly % 2, uly // 2
    sems = list(sems)

    def take(count):
        got = sems[:count]
        del sems[:count]
        return got

    chunk = 2 * blk + h
    upper = chunk // 32
    home = (1 - upper) * chunk + upper * (63 - chunk)
    row_to = [[(home, hh * 2 + s) for hh in (0, 1)] for s in (0, 1)]
    row_from = [(c // 2, (c % 2) * 2 + half) for c in (blk, 63 - blk) for half in (0, 1)]
    out_to = [(2 * (blk % 16) + q // 2, (blk // 16) * 2 + q % 2) for q in range(4)]
    out_from = [(16 * h + blk // 2, u) for u in range(4)]
    sibling = uly_others()[1]
    greet(
        ring_others() + uly_others() + [(blk_of(1 - y, z, x), (uly + 2) % 4)]
        + row_to[0] + row_to[1] + row_from + out_to + out_from
    )

    deliver = Deliver()
    piece_send, piece_recv, row_send, row_recv = take(4)
    for q in range(4):
        deliver.send(qkv_ref.at[q], qkv_in.at[uly], piece_send.at[q], piece_recv.at[uly], (blk, q))
    for q in range(4):
        deliver.send(out_ref.at[q], out_in.at[uly], piece_send.at[4 + q], piece_recv.at[4 + uly], out_to[q])
    for s in (0, 1):
        for hh in (0, 1):
            deliver.send(
                tokens_ref.at[s], rows.at[upper, core], row_send.at[s * 2 + hh],
                row_recv.at[upper * 2 + core], row_to[s][hh],
            )

    wide = PADDED // 2
    gathered = (gate_all, up_all, down_all)
    ff_send, ff_recv, y_send, y_recv, y_local = take(5)
    other_blk = blk_of(1 - y, z, x)

    def ff_part(n, half):
        return ff_ref.at[n, :, pl.ds(pl.multiple_of(half * wide, 128), wide)]

    picked = lax.broadcasted_iota(jnp.int32, (48, 64), 1)
    picked = jnp.where(picked % 16 < 12, picked // 16 * 12 + picked % 16, -1)
    picked = jnp.where(picked == lax.broadcasted_iota(jnp.int32, (48, 64), 0), 1.0, 0.0).astype(BF)
    for u in range(4):
        wait_arrival(qkv_in.at[u], piece_recv.at[u])
    qkv_part[...] = dot(picked, qkv_in[...].reshape(64, 512)).astype(BF)
    wq = Gather(
        lambda s: qkv_part.at[:, pl.ds(256 * s, 256)],
        lambda s, item: wq_all.at[
            core, pl.ds(pl.multiple_of(item * 48, 16), 48), pl.ds(256 * s, 256)
        ],
        *take(3),
    )
    wq.start()
    for u in range(4):
        wait_arrival(out_in.at[u], piece_recv.at[4 + u])
    out_part[...] = dot(picked, out_in[...].reshape(64, 384)).astype(BF)
    y_copies = []
    for n, ref in enumerate(gathered):
        copy = remote(ff_part(n, 1 - y), ref.at[blk], y_send.at[n], y_recv.at[n], (other_blk, uly))
        copy.start()
        y_copies.append(copy)
        copy = pltpu.make_async_copy(ff_part(n, y), ref.at[blk], y_local.at[n])
        copy.start()
        y_copies.append(copy)
    for s in (0, 1):
        deliver.send(
            cot_ref.at[s], cot_in.at[core], row_send.at[4 + s], row_recv.at[4 + core], (home, upper * 2 + s)
        )

    def out_columns(item, s):
        start = ((item % 2) * 2 + core) * 384
        return pl.ds(pl.multiple_of(start + 128 * s, 128), 128 + 128 * s)

    wo = Gather(
        lambda s: out_part.at[:, pl.ds(128 * s, 128 + 128 * s)],
        lambda s, item: wo_all.at[pl.ds(pl.multiple_of((item // 2) * 48, 16), 48), out_columns(item, s)],
        *take(3),
    )
    own_ff, other_ff = (
        [
            Ring(
                ff_part(n, y) if k == 0 else ref.at[other_blk],
                lambda item, ref=ref: ref.at[item],
                y if k == 0 else 1 - y,
                y if k == 0 else 1 - y,
                (1, 3, 1 + 2 * k)[n],
                ff_send.at[k, n], ff_recv.at[k, n],
            )
            for n, ref in enumerate(gathered)
        ]
        for k in (0, 1)
    )
    wq.second()
    for ring in own_ff:
        ring.start()

    for n in range(4):
        wait_arrival(rows.at[n // 2, n % 2], row_recv.at[n])
        value = rows[n // 2, n % 2].astype(F32)
        at = slice(n * 64, (n + 1) * 64)
        rows_out[at, :] = rows[n // 2, n % 2]
        normed_ref[at, :] = (value * norm_scale(value) * norm_in_ref[...]).astype(BF)
    latent = dot_nt(normed_ref[...], a_qkv_ref[...])
    latent_ref[...] = latent
    wq.third()
    wo.start()
    wq.fourth()
    wo.second()
    for n in range(3):
        y_copies[2 * n].wait_recv()
    for ring in other_ff:
        ring.start()
    wq.last()
    pair_send, pair_recv = take(2)

    def pair_copy(ref, n):
        return remote(ref, ref, pair_send.at[n], pair_recv.at[n], sibling)

    pair_copy(wq_all.at[core], 0).start()
    wo.third()
    pair_copy(wq_all.at[core], 0).wait_send()
    pair_copy(wq_all.at[1 - core], 0).wait_recv()

    adapted = dot(latent.astype(BF), b_qkv_ref[...]) + bias_ref[...]
    cos_table, sine_table = cos_ref[...], sin_ref[...]
    for c in (0, 1):
        columns = dot(normed_ref[...], wq_all[c]) + adapted[:, c * 512 : (c + 1) * 512]
        for n in range(4):
            head = columns[:, n * HEAD : (n + 1) * HEAD]
            if c * 4 + n < GROUP + 1:
                head = head * cos_table + pltpu.roll(head, HEAD // 2, 1) * sine_table
            if c * 4 + n < GROUP:
                at = (c * 4 + n) * HEAD
                q_ref[:, at : at + HEAD] = (head * (HEAD ** (-0.5) * LOG2E)).astype(BF)
            else:
                at = (n - 2) * HEAD
                kv_part[0, :, at : at + HEAD] = head[:CHUNK].astype(BF)
                kv_part[1, :, at : at + HEAD] = head[CHUNK:].astype(BF)
    kv = Gather(
        lambda s: kv_part.at[s],
        lambda s, item: kv_all.at[item if s == 0 else 63 - item],
        *take(3),
    )
    kv.start()
    for ring in own_ff:
        ring.third()
    kv.second()
    for ring in own_ff:
        ring.third_late()
    for ring in other_ff:
        ring.third()
    kv.third()
    wo.fourth()
    for ring in other_ff:
        ring.third_late()
    kv.fourth()

    for half in (0, 1):
        wait_arrival(cot_in.at[half], row_recv.at[4 + half])
        start = ((1 - h) * blk + h * (63 - blk)) * CHUNK + half * 64
        at = lax.broadcasted_iota(jnp.int32, (64, D), 0) + start
        cot_own[half * 64 : (half + 1) * 64, :] = jnp.where(
            at < length_ref[...], cot_in[half].astype(F32), 0.0
        ).astype(BF)
    cot_spread = Spread(cot_own, cot_all, *take(3))
    cot_spread.start()
    kv.last()
    (out_sem,) = take(1)
    copies = [
        pltpu.make_async_copy(src, dst, out_sem.at[n])
        for n, (src, dst) in enumerate(((kv_all, kv_out), (wq_all, wq_out), (wo_all, wo_out)))
    ]
    copies[0].start()
    copies[1].start()
    wo.last()

    def wo_columns(c, n):
        return wo_all.at[:, pl.ds(pl.multiple_of((2 * n + c) * 384, 128), 384)]

    for n in (0, 1):
        pair_copy(wo_columns(core, n), 1 + n).start()
    args = (q_ref, kv_all, limit_ref, mixed_ref, lse_ref, acc_ref, stat_ref)
    beside = [
        lambda: [ring.fourth(0) for ring in own_ff],
        lambda: [ring.fourth(0) for ring in other_ff] + [cot_spread.second()],
        lambda: [ring.fourth(1) for ring in own_ff],
        lambda: [ring.fourth(1) for ring in other_ff] + [cot_spread.third()],
        lambda: [ring.fourth(3) for ring in own_ff],
        lambda: [ring.fourth(3) for ring in other_ff],
        lambda: [ring.fourth(2) for ring in own_ff],
        lambda: [ring.fourth(2) for ring in other_ff],
    ]
    for slot, at in ((0, blk), (1, 63 - blk)):
        for part in range(4):
            forward_slot(slot, at, part, *args)
            beside.pop(0)()
    for n in (0, 1):
        pair_copy(wo_columns(core, n), 1 + n).wait_send()
        pair_copy(wo_columns(1 - core, n), 1 + n).wait_recv()
    copies[2].start()

    def project(slot):
        mixed = mixed_ref[pl.ds(pl.multiple_of(slot * CHUNK, CHUNK), CHUNK), :]
        lifted = dot(dot_nt(mixed, ao_ref[...]).astype(BF), bo_ref[...])
        return dot(mixed, wo_all[...]) + lifted

    (cross_sem,) = take(1)
    cross_out[...] = project(1 - h).astype(BF)
    cross = remote(cross_out, cross_in, cross_sem.at[0], cross_sem.at[1], uly_others()[0])
    cross.start()
    mine = project(h) + rows_out[pl.ds(pl.multiple_of(h * CHUNK, CHUNK), CHUNK), :].astype(F32)
    cross.wait()
    residual = mine + cross_in[...].astype(F32)
    resid_ref[...] = residual
    nf_own[...] = (residual * norm_scale(residual) * norm_ff_ref[...]).astype(BF)
    nf_spread = Spread(nf_own, nf_all, *take(3))
    nf_spread.start()
    nf_spread.second()
    nf_spread.third()
    nf_spread.last()
    cot_spread.last()
    for ring in own_ff + other_ff:
        ring.last()
    for n in range(3):
        y_copies[2 * n].wait_send()
        y_copies[2 * n + 1].wait()
    deliver.end()
    for copy in copies:
        copy.wait()


def forward(*args):
    weight = jax.ShapeDtypeStruct((32, 48, FF_COLS), BF)
    group = GROUP * HEAD
    dma = pltpu.SemaphoreType.DMA
    spread = jax.ShapeDtypeStruct((2, 4, CHUNK, D), BF)
    return pl.pallas_call(
        forward_kernel,
        out_shape=(
            jax.ShapeDtypeStruct((2 * CHUNK, group), BF),
            jax.ShapeDtypeStruct((2 * CHUNK, group), BF),
            jax.ShapeDtypeStruct((2, 8, ROWS), F32),
            jax.ShapeDtypeStruct((CHUNKS, CHUNK, 2 * HEAD), BF),
            jax.ShapeDtypeStruct((2, D, 512), BF),
            jax.ShapeDtypeStruct((D // 2, D), BF),
            weight, weight, weight,
            jax.ShapeDtypeStruct((2 * CHUNK, D), BF),
            jax.ShapeDtypeStruct((2 * CHUNK, D), BF),
            jax.ShapeDtypeStruct((2 * CHUNK, 48), F32),
            jax.ShapeDtypeStruct((CHUNK, D), F32),
            jax.ShapeDtypeStruct((CHUNK, D), BF),
            spread, spread,
        ),
        in_specs=[ANY] * 5 + [IN_VMEM] * 11,
        out_specs=(IN_VMEM,) * 3 + (ANY,) * 6 + (IN_VMEM,) * 5 + (ANY,) * 2,
        scratch_shapes=[
            pltpu.VMEM((CHUNKS, CHUNK, 2 * HEAD), BF),
            pltpu.VMEM((2, D, 512), BF),
            pltpu.VMEM((D // 2, D), BF),
            pltpu.VMEM((2, 2, 64, D), BF),
            pltpu.VMEM((2, 64, D), BF),
            pltpu.VMEM((2, CHUNK, 2 * HEAD), BF),
            pltpu.VMEM((HEAD, ROWS), F32),
            pltpu.VMEM((2, 8, ROWS), F32),
            pltpu.VMEM((4, 16, 512), BF),
            pltpu.VMEM((4, 16, 384), BF),
            pltpu.VMEM((48, 512), BF),
            pltpu.VMEM((48, 384), BF),
            pltpu.VMEM((CHUNK, D), BF),
            pltpu.VMEM((CHUNK, D), BF),
            pltpu.VMEM((CHUNK, D), BF),
            dma((8,)), dma((8,)), dma((6,)), dma((6,)),
            dma((2, 3, Ring.sends)), dma((2, 3, 16)), dma((3,)), dma((3,)), dma((3,)),
        ]
        + GATHER_SEMS()
        + GATHER_SEMS()
        + [dma((3,)), dma((3,))]
        + GATHER_SEMS()
        + SPREAD_SEMS
        + [dma((3,)), dma((2,))]
        + SPREAD_SEMS,
        compiler_params=pltpu.CompilerParams(
            collective_id=1, has_side_effects=True, vmem_limit_bytes=48 * 2**20
        ),
        name="forward",
    )(*args)


class Collect:
    @staticmethod
    def scratch():
        piece, half = (CHUNK, D), (CHUNK // 2, D)
        return [
            pltpu.VMEM((4,) + piece, BF),
            pltpu.VMEM((4,) + piece, BF),
            pltpu.VMEM((2,) + half, BF),
            pltpu.VMEM((2,) + piece, BF),
            pltpu.VMEM(piece, BF),
            pltpu.VMEM((2,) + piece, BF),
            pltpu.SemaphoreType.DMA((8,)),
            pltpu.SemaphoreType.DMA((8,)),
            pltpu.SemaphoreType.DMA,
        ]

    scratches = 9

    def __init__(self, src, scratch):
        self.src = src
        (
            self.mine, self.pair, self.halves, self.last_in, self.far, self.near,
            self.send_sem, self.recv_sem, self.local_sem,
        ) = scratch
        self.w = ring_at()
        self.core = lax.axis_index("uly") % 2
        self.sent = []

    def send(self, src, dst, recv, device):
        copy = remote(src, dst, self.send_sem.at[recv], self.recv_sem.at[recv], device)
        copy.start()
        self.sent.append(copy)

    def start(self):
        self.local = pltpu.make_async_copy(self.src.at[self.core], self.mine, self.local_sem)
        self.local.start()
        for d in (2, 1, 3, 0):
            at = (self.w + d) % 4
            self.send(self.src.at[1 - self.core, at], self.pair.at[at], d, uly_others()[1])

    def both(self, d):
        at = (self.w + d) % 4
        wait_arrival(self.pair.at[at], self.recv_sem.at[d])
        return self.mine[at].astype(F32) + self.pair[at].astype(F32)

    def second(self):
        half = CHUNK // 2
        self.local.wait()
        self.far[...] = self.both(2).astype(BF)
        self.send(self.far.at[pl.ds(0, half)], self.halves.at[0], 4, ring_place((self.w + 1) % 4))
        self.send(self.far.at[pl.ds(half, half)], self.halves.at[1], 5, ring_place((self.w + 3) % 4))

    def third(self):
        half = CHUNK // 2
        for k, d in ((0, 1), (1, 3)):
            total = self.both(d)
            wait_arrival(self.halves.at[k], self.recv_sem.at[4 + k])
            rows = slice(k * half, (k + 1) * half)
            other = slice((1 - k) * half, (2 - k) * half)
            self.near[k, rows] = (total[rows] + self.halves[k].astype(F32)).astype(BF)
            self.near[k, other] = total[other].astype(BF)
            self.send(self.near.at[k], self.last_in.at[k], 6 + k, ring_place((self.w + d) % 4))

    def fourth(self):
        total = self.both(0)
        for k in (0, 1):
            wait_arrival(self.last_in.at[k], self.recv_sem.at[6 + k])
            total += self.last_in[k].astype(F32)
        for copy in self.sent:
            copy.wait_send()
        return total


def collect_kernel(a_ref, b_ref, a_out, b_out, *scratch):
    y, z, x, blk, uly = place()
    greet([uly_others()[1], (blk_of(1 - y, z, x), uly), (blk_of(1 - y, z, x), (uly + 2) % 4)])
    a = Collect(a_ref, scratch[: Collect.scratches])
    b = Collect(b_ref, scratch[Collect.scratches :])
    a.start()
    a.second()
    a.third()
    b.start()
    a_out[...] = a.fourth()
    b.second()
    b.third()
    b_out[...] = b.fourth()


def collect(a, b):
    out = jax.ShapeDtypeStruct((CHUNK, D), F32)
    return pl.pallas_call(
        collect_kernel,
        out_shape=(out, out),
        in_specs=[ANY, ANY],
        out_specs=(IN_VMEM, IN_VMEM),
        scratch_shapes=Collect.scratch() * 2,
        compiler_params=pltpu.CompilerParams(
            collective_id=4, has_side_effects=True, vmem_limit_bytes=24 * 2**20
        ),
        name="collect",
    )(a, b)


def backward_slot(
    slot, chunk, part, q_ref, kv_ref, limit_ref, mixed_ref, grad_ref, lse_ref, dq_ref, dkv_ref, acc_ref
):
    turned = head_columns(q_ref, slot)
    rows = head_rows(q_ref, slot)
    grad_turned = head_columns(grad_ref, slot)
    grad_rows = head_rows(grad_ref, slot)
    mixed_turned = head_columns(mixed_ref, slot)
    row_dot = jnp.sum(
        grad_turned.astype(F32) * mixed_turned.astype(F32), axis=0, keepdims=True
    )
    limit = limit_ref[slot, 0:1, :]
    lse = lse_ref[slot, 0:1, :]
    if part == 0:
        acc_ref[...] = jnp.zeros_like(acc_ref)

    def step(n, carry):
        keys, values = key_block(kv_ref, n)
        scores = jnp.where(key_places(n) <= limit, dot(keys, turned), -1e30)
        probs = jnp.exp2(scores - lse)
        grad_probs = dot(values, grad_turned)
        grad_scores = (probs * (grad_probs - row_dot)).astype(BF)
        acc_ref[...] += dot(keys.T, grad_scores)
        at = pl.ds(pl.multiple_of(n * KEYS, KEYS), KEYS)
        dkv_ref[at, :HEAD] += dot(grad_scores, rows)
        dkv_ref[at, HEAD:] += dot(probs.astype(BF), grad_rows)
        return carry

    blocks = chunk // STEP + 1
    lax.fori_loop(blocks * part // 4, blocks * (part + 1) // 4, step, 0)
    if part == 3:
        for n in range(GROUP):
            dq_ref[slot * CHUNK : (slot + 1) * CHUNK, n * HEAD : (n + 1) * HEAD] = (
                acc_ref[:, n * CHUNK : (n + 1) * CHUNK].T * HEAD ** (-0.5)
            )


class Reduce:
    sends = 28

    @staticmethod
    def scratch(shape):
        return [
            pltpu.VMEM((2, 3, 2, 4) + shape, BF),
            pltpu.VMEM((2, 3, 2) + shape, BF),
            pltpu.VMEM((2,) + shape, BF),
            pltpu.VMEM((2, 4, 2) + shape, BF),
            pltpu.VMEM((2, 2) + shape, BF),
            pltpu.SemaphoreType.DMA((2, Reduce.sends)),
            pltpu.SemaphoreType.DMA((2, Reduce.sends)),
        ]

    def __init__(self, part, index, scratch):
        self.part, self.index = part, index
        self.buf_q, self.buf_p, self.buf_y, self.sum_p, self.sum_y, self.send_sem, self.recv_sem = scratch
        self.y, self.z, self.x, self.blk, self.uly = place()
        self.pq = ((self.x, self.z), (self.z, self.x))
        self.flying = []

    def at(self, half, y, p, q):
        return blk_of(y, q, p) if half == 0 else blk_of(y, p, q)

    def send(self, src, dst, half, n, y, p, q):
        copy = pltpu.make_async_remote_copy(
            src_ref=src, dst_ref=dst,
            send_sem=self.send_sem.at[half, n], recv_sem=self.recv_sem.at[half, n],
            device_id=(self.at(half, y, p, q), self.uly), device_id_type=MESH,
        )
        copy.start()
        self.flying.append(copy)

    def land(self):
        for copy in self.flying:
            copy.wait()
        self.flying = []

    def first(self):
        for d in (2, 1, 3):
            for half in (0, 1):
                p, q = self.pq[half]
                to = (q + d) % 4
                for y in (0, 1):
                    for pp in range(4):
                        self.send(
                            self.part.at[self.index(half, self.at(half, y, pp, to))],
                            self.buf_q.at[half, d - 1, y, pp],
                            half, (d - 1) * 8 + y * 4 + pp, self.y, p, to,
                        )

    def second(self):
        self.land()
        for d in (2, 1, 3, 0):
            for half in (0, 1):
                p, q = self.pq[half]
                to = (p + d) % 4
                for y in (0, 1):
                    total = self.part[self.index(half, self.at(half, y, to, q))].astype(F32)
                    for n in range(3):
                        total += self.buf_q[half, n, y, to].astype(F32)
                    self.sum_p[half, d, y] = total.astype(BF)
                if d > 0:
                    self.send(
                        self.sum_p.at[half, d], self.buf_p.at[half, d - 1], half, 23 + d, self.y, to, q
                    )

    def third(self):
        self.land()
        for k in (1, 0):
            for half in (0, 1):
                p, q = self.pq[half]
                y = self.y if k == 0 else 1 - self.y
                total = self.sum_p[half, 0, y].astype(F32)
                for n in range(3):
                    total += self.buf_p[half, n, y].astype(F32)
                self.sum_y[half, k] = total.astype(BF)
                if k == 1:
                    self.send(self.sum_y.at[half, 1], self.buf_y.at[half], half, 27, 1 - self.y, p, q)

    def fourth(self):
        self.land()
        return [self.sum_y[half, 0].astype(F32) + self.buf_y[half].astype(F32) for half in (0, 1)]


def reduce_others():
    y, z, x, blk, uly = place()
    return (
        [(blk_of(1 - y, z, x), uly)]
        + [(blk_of(y, z, (x + d) % 4), uly) for d in (1, 2, 3)]
        + [(blk_of(y, (z + d) % 4, x), uly) for d in (1, 2, 3)]
    )


UNIT = (16, 128)


class Total:
    @staticmethod
    def scratch(kept, summed):
        shape = (kept + summed,) + UNIT
        return (
            [pltpu.VMEM((64,) + shape, BF)]
            + Reduce.scratch(shape)
            + [
                pltpu.VMEM((2,) + shape, BF),
                pltpu.VMEM((3, 2) + shape, BF),
                pltpu.VMEM((2, 4 * kept + summed) + UNIT, BF),
                pltpu.SemaphoreType.DMA((3,)),
                pltpu.SemaphoreType.DMA((3,)),
                pltpu.SemaphoreType.DMA((1, Gather.sends)),
                pltpu.SemaphoreType.DMA((1, 32)),
                pltpu.SemaphoreType.DMA((1,)),
                pltpu.SemaphoreType.DMA,
                pltpu.SemaphoreType.DMA,
            ]
        )

    scratches = 18

    @staticmethod
    def shape(kept, summed):
        return jax.ShapeDtypeStruct((2, 32, 4 * kept + summed) + UNIT, BF)

    def __init__(self, kept, summed, all_ref, scratch):
        self.kept, self.summed, self.all_ref = kept, summed, all_ref
        self.part = scratch[0]
        self.reduce = Reduce(self.part, lambda half, item: half * 32 + item, scratch[1:8])
        self.own, self.buf, self.full, self.send_sem, self.recv_sem = scratch[8:13]
        self.pair_send, self.pair_recv = scratch[16:18]
        self.y, self.z, self.x, self.blk, self.uly = place()
        self.core = self.uly % 2
        self.gather = Gather(
            lambda s: self.full.at[self.core],
            lambda s, item: self.all_ref.at[self.core, item],
            *scratch[13:16],
            orders=(self.core,),
        )

    def pack(self, kept, summed):
        for n in range(64 * self.kept):
            self.part[n // self.kept, n % self.kept] = (
                kept[n].astype(BF) if n < len(kept) else jnp.zeros(UNIT, BF)
            )
        for n in range(64 * self.summed):
            self.part[n // self.summed, self.kept + n % self.summed] = (
                summed[n].astype(BF) if n < len(summed) else jnp.zeros(UNIT, BF)
            )

    def across(self):
        for half, total in enumerate(self.reduce.fourth()):
            self.own[half] = total.astype(BF)
        self.copies = []
        for n, other in enumerate(uly_others()):
            copy = pltpu.make_async_remote_copy(
                src_ref=self.own, dst_ref=self.buf.at[n],
                send_sem=self.send_sem.at[n], recv_sem=self.recv_sem.at[n],
                device_id=other, device_id_type=MESH,
            )
            copy.start()
            self.copies.append(copy)

    def join(self):
        for copy in self.copies:
            copy.wait()
        kept = self.kept
        terms = [self.own] + [self.buf.at[n] for n in range(3)]
        who = [self.uly] + [other[1] for other in uly_others()]
        for half in (0, 1):
            for term, uly in zip(terms, who):
                self.full[half, pl.ds(uly * kept, kept)] = term[half, :kept]
            if self.summed:
                self.full[half, 4 * kept :] = sum(
                    term[half, kept:].astype(F32) for term in terms
                ).astype(BF)
        self.gather.start()

    def hand(self):
        self.gather.last()
        self.pair(self.core).start()

    def pair(self, core):
        return pltpu.make_async_remote_copy(
            src_ref=self.all_ref.at[core], dst_ref=self.all_ref.at[core],
            send_sem=self.pair_send, recv_sem=self.pair_recv,
            device_id=uly_others()[1], device_id_type=MESH,
        )

    def end(self):
        self.pair(self.core).wait_send()
        self.pair(1 - self.core).wait_recv()

    def steps(self):
        return [
            self.reduce.first, self.reduce.second, self.reduce.third, self.across, self.join,
            self.gather.second, self.gather.third, self.gather.fourth, self.hand, self.end,
        ]


def units(ref, tiles):
    return [
        ref[n, :, t * 128 : (t + 1) * 128] for n in range(ref.shape[0]) for t in range(tiles)
    ]


FF_KEPT, FF_SUMMED = 2, 2
COL_TILES = PADDED // 128
D_TILES = D // 128


def backward_kernel(
    q_ref, kv_ref, limit_ref, mixed_ref, grad_ref, lse_ref, cols_ref, oa_ref, ob_ref, ff_ref,
    dq_ref, own_ref, all_ref, dkv_ref, acc_ref, part, *scratch,
):
    y, z, x, blk, uly = place()
    greet(reduce_others() + uly_others())
    reduce = Reduce(
        part, lambda half, item: item if half == 0 else 63 - item, scratch[:7]
    )
    total = Total(FF_KEPT, FF_SUMMED, all_ref, scratch[7:])
    total.pack(
        units(cols_ref, COL_TILES) + units(oa_ref, D_TILES // 2) + units(ob_ref, D_TILES),
        units(ff_ref, D_TILES),
    )
    steps = total.steps()
    steps.pop(0)()
    dkv_ref[...] = jnp.zeros_like(dkv_ref)
    args = (q_ref, kv_ref, limit_ref, mixed_ref, grad_ref, lse_ref, dq_ref, dkv_ref, acc_ref)
    for slot, chunk in ((0, blk), (1, 63 - blk)):
        for part_of in range(4):
            backward_slot(slot, chunk, part_of, *args)
            if steps:
                steps.pop(0)()

    def pack(n, carry):
        rows = dkv_ref[pl.ds(pl.multiple_of(n * CHUNK, CHUNK), CHUNK), :]
        part[n] = jnp.concatenate([rows[:, :HEAD] * LN2, rows[:, HEAD:]], axis=1).astype(BF)
        return carry

    lax.fori_loop(0, CHUNKS, pack, 0)
    reduce.first()
    while steps:
        steps.pop(0)()
    reduce.second()
    reduce.third()
    for half, value in enumerate(reduce.fourth()):
        own_ref[half] = value


def attend_backward(q, kv, limit, mixed, grad, lse, cols, oa, ob, ff):
    return pl.pallas_call(
        backward_kernel,
        out_shape=(
            jax.ShapeDtypeStruct((2 * CHUNK, GROUP * HEAD), F32),
            jax.ShapeDtypeStruct((2, CHUNK, 2 * HEAD), F32),
            Total.shape(FF_KEPT, FF_SUMMED),
        ),
        in_specs=[IN_VMEM] * 10,
        out_specs=(IN_VMEM, IN_VMEM, ANY),
        scratch_shapes=[
            pltpu.VMEM((CHUNKS * CHUNK, 2 * HEAD), F32),
            pltpu.VMEM((HEAD, ROWS), F32),
            pltpu.VMEM((CHUNKS, CHUNK, 2 * HEAD), BF),
        ]
        + Reduce.scratch((CHUNK, 2 * HEAD))
        + Total.scratch(FF_KEPT, FF_SUMMED),
        compiler_params=pltpu.CompilerParams(
            collective_id=2, has_side_effects=True, vmem_limit_bytes=56 * 2**20
        ),
        name="attend_backward",
    )(q, kv, limit, mixed, grad, lse, cols, oa, ob, ff)


QKV_KEPT = 1


def qkv_total_kernel(a_ref, bq_ref, bkv_ref, all_ref, *scratch):
    greet(reduce_others() + uly_others())
    total = Total(QKV_KEPT, 0, all_ref, scratch)
    total.pack(units(a_ref, D_TILES) + units(bq_ref, D_TILES // 2) + units(bkv_ref, 1), [])
    for step in total.steps():
        step()


def qkv_total(a, bq, bkv):
    return pl.pallas_call(
        qkv_total_kernel,
        out_shape=Total.shape(QKV_KEPT, 0),
        in_specs=[IN_VMEM] * 3,
        out_specs=ANY,
        scratch_shapes=Total.scratch(QKV_KEPT, 0),
        compiler_params=pltpu.CompilerParams(
            collective_id=3, has_side_effects=True, vmem_limit_bytes=24 * 2**20
        ),
        name="qkv_total",
    )(a, bq, bkv)


def fold_kernel(pick_ref, ff_ref, qkv_ref, a_wide, a_down, b_wide, b_kv, b_ff):
    c = pl.program_id(0)

    def kept(ref, per, n, u):
        return ref[n // per // 32, n // per % 32, u * per + n % per].astype(F32)

    def ff_kept(n, u):
        return kept(ff_ref, FF_KEPT, n, u)

    def qkv_kept(n, u):
        return kept(qkv_ref, QKV_KEPT, n, u)

    def summed(n):
        item = n // FF_SUMMED
        return ff_ref[item // 32, item % 32, 4 * FF_KEPT + n % FF_SUMMED].astype(F32)

    def put(ref, at, tile, value):
        ref[at + (slice(None), slice(tile * 128, (tile + 1) * 128))] = (
            pick_ref[c, 0] * value(0) + pick_ref[c, 1] * value(1)
        )

    for n in range(3):
        for t in range(D_TILES):
            put(a_wide, (n, 0), t, lambda s: qkv_kept(n * D_TILES + t, s) + qkv_kept(n * D_TILES + t, 2 + s))
    at_o = 6 * COL_TILES
    half = D_TILES // 2
    for t in range(D_TILES):
        h, part = t // half, t % half
        put(a_wide, (3, 0), t, lambda s: ff_kept(at_o + part, 2 * h + s))
        put(b_wide, (0, 0), t, lambda s: qkv_kept(3 * D_TILES + part, 2 * h + s))
        put(
            b_wide, (1, 0), t,
            lambda s: ff_kept(at_o + half + t, s) + ff_kept(at_o + half + t, 2 + s),
        )
        for n, (ref, at) in enumerate(((a_wide, (4, 0)), (a_wide, (5, 0)), (b_wide, (2, 0)))):
            put(ref, at, t, lambda s: summed((2 * n + s) * D_TILES + t))
    for n in (0, 1):
        for h in (0, 1):
            put(b_kv, (n, 0), h, lambda s: qkv_kept(3 * D_TILES + half + n, 2 * h + s))
    for n, (ref, at) in enumerate(((a_down, (0,)), (b_ff, (0, 0)), (b_ff, (1, 0)))):
        for t in range(FF // 128):
            where = [
                (u, t - start) for u, start in enumerate((0, 17, 35, 52)) if 0 <= t - start < COL_TILES
            ]
            put(
                ref, at, t,
                lambda s: sum(ff_kept((2 * n + s) * COL_TILES + tile, u) for u, tile in where),
            )


def fold(pick, ff_all, qkv_all):
    def whole(v):
        return pl.BlockSpec(v.shape, lambda c: (0,) * v.ndim)

    def by_set(lead, columns):
        shape = lead + (1, 16, columns)
        return pl.BlockSpec(shape, lambda c: (0,) * len(lead) + (c, 0, 0))

    def out(lead, columns):
        return jax.ShapeDtypeStruct(lead + (SETS, 16, columns), F32)

    outs = (((6,), D), ((), FF), ((3,), D), ((2,), 2 * HEAD), ((2,), FF))
    return pl.pallas_call(
        fold_kernel,
        grid=(SETS,),
        out_shape=tuple(out(*o) for o in outs),
        in_specs=[pl.BlockSpec(memory_space=pltpu.SMEM), whole(ff_all), whole(qkv_all)],
        out_specs=tuple(by_set(*o) for o in outs),
        compiler_params=pltpu.CompilerParams(vmem_limit_bytes=40 * 2**20),
        name="fold",
    )(pick, ff_all, qkv_all)


def device_at(blk, h, core):
    return blk * 4 + h * 2 + core


def moves():
    def home(blk, h):
        chunk = 2 * blk + h
        return (chunk, 0) if chunk < 32 else (63 - chunk, 1)

    return [
        [
            (device_at(home(b, h)[0], home(b, h)[1], c ^ j), device_at(b, h, c))
            for b in range(32) for h in (0, 1) for c in (0, 1)
        ]
        for j in (0, 1)
    ]


ALL = ("blk", "uly")
OVER_H = [(0, 2), (2, 0), (1, 3), (3, 1)]
OVER_CORE = [(0, 1), (1, 0), (2, 3), (3, 2)]
OVER_BOTH = [(0, 3), (3, 0), (1, 2), (2, 1)]


def flip(parts, first, second):
    return jnp.where(parts, second, first), jnp.where(parts, first, second)


def rope_tables(positions):
    halves = jnp.arange(0, HEAD, 2, dtype=jnp.int32).astype(F32)
    freq_table = THETA ** (-halves / HEAD)
    angles = positions.astype(F32)[:, None] * freq_table[None, :]
    angles = jnp.concatenate([angles, angles], axis=-1)
    return jnp.cos(angles), jnp.sin(angles)


def rope_turn(values, cos_table, sine_table):
    middle = HEAD // 2
    turned = jnp.concatenate([-values[..., middle:], values[..., :middle]], axis=-1)
    return values * cos_table + turned * sine_table


def rope_back(values, cos_table, sine_table):
    middle = HEAD // 2
    turned = jnp.concatenate([values[..., middle:], -values[..., :middle]], axis=-1)
    return values * cos_table + turned * sine_table


def norm_scale(hidden):
    return lax.rsqrt(jnp.mean(hidden * hidden, axis=-1, keepdims=True) + EPS)


def norm_back(hidden, scaled, gain_vec, upstream):
    normed = hidden * scaled
    weighted = upstream * gain_vec
    return scaled * (weighted - normed * jnp.mean(weighted * normed, axis=-1, keepdims=True))


def mm(spec, a, b):
    return jnp.einsum(spec, a.astype(BF), b.astype(BF), preferred_element_type=F32)


def body(
    tokens, cotangent, lengths, set_index, norm_in, norm_ff, qkv_bias, w_qkv, w_out, w_gate_up, w_down,
    a_wide, a_down, b_wide, b_kv, b_ff,
):
    blk = lax.axis_index("blk")
    uly = lax.axis_index("uly")
    h = uly // 2
    core = uly % 2
    y_lo = blk // 16
    back_moves = moves()
    local_ff = w_down.shape[0]
    group_cols = GROUP * HEAD
    zero = jnp.zeros

    def pick_set(table, axis, at):
        return lax.dynamic_index_in_dim(table, at, axis, keepdims=False)

    def halve(v, size, axis):
        return lax.dynamic_slice_in_dim(v, h * size, size, axis)

    def widen(v):
        left, right = (
            jnp.pad(v, ((0, 0),) * (v.ndim - 1) + (side,))
            for side in ((0, PADDED - local_ff), (PADDED - local_ff, 0))
        )
        return jnp.where(core == 1, right, left)

    quarters = jnp.concatenate(
        [
            w_qkv[:, : HEADS * HEAD].reshape(12, 2, group_cols),
            w_qkv[:, HEADS * HEAD : HEADS * HEAD + 256].reshape(12, 2, HEAD),
            w_qkv[:, HEADS * HEAD + 256 :].reshape(12, 2, HEAD),
        ],
        axis=2,
    )
    quarters = jnp.moveaxis(quarters.reshape(12, 4, 512), 1, 0)
    quarters = jnp.pad(quarters, ((0, 0), (0, 4), (0, 0)))
    out_quarters = jnp.pad(jnp.moveaxis(w_out.reshape(12, 4, 384), 1, 0), ((0, 0), (0, 4), (0, 0)))
    ff_part = widen(jnp.concatenate([w_gate_up, w_down.T[None]], axis=0))

    chunks = jnp.stack([blk, 63 - blk])
    positions = (chunks[:, None] * CHUNK + jnp.arange(CHUNK, dtype=jnp.int32)[None, :]).reshape(-1)
    length = lengths[core]
    limit = jnp.minimum(positions, length - 1).reshape(2, 1, 1, CHUNK)
    limit = jnp.broadcast_to(limit, (2, 8, GROUP, CHUNK)).reshape(2, 8, ROWS)
    cos_table, sine_table = rope_tables(positions)
    cos_heads, sine_heads = cos_table[:, None, :], sine_table[:, None, :]
    signed = jnp.where(jnp.arange(HEAD) < HEAD // 2, -sine_table, sine_table)

    own_set = set_index[core]
    a_own = pick_set(a_wide, 1, own_set)
    bq = halve(pick_set(b_wide[0], 0, own_set), group_cols, 1)
    bo = pick_set(b_wide[1], 0, own_set)
    bk, bv = (halve(pick_set(b_kv[n], 0, own_set), HEAD, 1) for n in (0, 1))
    ao = halve(a_own[3], group_cols, 1)
    bias = jnp.concatenate(
        [
            halve(qkv_bias[: HEADS * HEAD], group_cols, 0),
            halve(qkv_bias[HEADS * HEAD : HEADS * HEAD + 256], HEAD, 0),
            halve(qkv_bias[HEADS * HEAD + 256 :], HEAD, 0),
        ]
    )
    a_qkv = a_own[:3].reshape(48, D)
    b_qkv = jnp.concatenate(
        [
            jnp.concatenate([bq, zero((16, 256), BF)], axis=1),
            jnp.concatenate([zero((16, group_cols), BF), bk, zero((16, HEAD), BF)], axis=1),
            jnp.concatenate([zero((16, group_cols + HEAD), BF), bv], axis=1),
        ],
        axis=0,
    )
    (
        q, mixed, lse, kv_all, qkv_w, out_w, gate_w, up_w, down_w, rows, normed, latent_qkv, residual,
        grad_out, gathered, grad_gathered,
    ) = forward(
        quarters, out_quarters, tokens, cotangent, ff_part, limit,
        jnp.broadcast_to(length, (1, D)), norm_in[None], norm_ff[None], bias[None], cos_table, signed,
        a_qkv, b_qkv, ao, bo,
    )
    gate_w, up_w, down_w = (w.reshape(D, FF_COLS) for w in (gate_w, up_w, down_w))
    gathered, grad_gathered = (v.reshape(2, 4 * CHUNK, D) for v in (gathered, grad_gathered))
    rows = rows.reshape(2, CHUNK, D).astype(F32)
    scale_in = norm_scale(rows)
    own_rows = jnp.where(h == 0, rows[0], rows[1])
    scale_ff = norm_scale(residual)
    latent_o = mm("tc,rc->tr", mixed, ao)

    def swap_h(v):
        return lax.ppermute(v, "uly", OVER_H)

    def own_slot(v):
        return flip(h == 1, v[0], v[1])

    def by_sequence(table, axis):
        return jnp.stack([pick_set(table, axis, set_index[s]) for s in (0, 1)])

    def own_cols(v):
        v = lax.dynamic_slice_in_dim(v, uly * local_ff, local_ff, v.ndim - 1)
        return lax.dynamic_slice_in_dim(widen(v), y_lo * FF_COLS, FF_COLS, v.ndim - 1)

    a_ff = by_sequence(a_wide[4:6], 1).reshape(2, 32, D)
    b_cols = own_cols(by_sequence(b_ff, 1))
    a_cols = own_cols(by_sequence(a_down, 0))
    b_out = by_sequence(b_wide[2], 0)
    latent_ff = mm("std,srd->str", gathered, a_ff)
    gate = mm("std,df->stf", gathered, gate_w) + mm("str,srf->stf", latent_ff[..., :16], b_cols[:, 0])
    up = mm("std,df->stf", gathered, up_w) + mm("str,srf->stf", latent_ff[..., 16:], b_cols[:, 1])
    sigmoid = jax.nn.sigmoid(gate)
    silu = gate * sigmoid
    hidden = (silu * up).astype(BF)
    latent_down = mm("stf,srf->str", hidden, a_cols)
    down = mm("stf,df->std", hidden, down_w) + mm("str,srd->std", latent_down, b_out)
    latent_back = mm("std,srd->str", grad_gathered, b_out)
    grad_hidden = mm("std,df->stf", grad_gathered, down_w) + mm("str,srf->stf", latent_back, a_cols)
    grad_a_cols = mm("str,stf->srf", latent_back, hidden)
    grad_b_out = mm("str,std->srd", latent_down, grad_gathered)
    grad_up = (grad_hidden * silu).astype(BF)
    grad_gate = (grad_hidden * up * (sigmoid * (1.0 + gate * (1.0 - sigmoid)))).astype(BF)
    back_gate = mm("stf,srf->str", grad_gate, b_cols[:, 0])
    back_up = mm("stf,srf->str", grad_up, b_cols[:, 1])
    back_ff = jnp.concatenate([back_gate, back_up], axis=-1)
    grad_a_ff = mm("str,std->srd", back_ff, gathered)
    grad_b_gate = mm("str,stf->srf", latent_ff[..., :16], grad_gate)
    grad_b_up = mm("str,stf->srf", latent_ff[..., 16:], grad_up)
    grad_ff_in = (
        mm("stf,df->std", grad_gate, gate_w)
        + mm("stf,df->std", grad_up, up_w)
        + mm("str,srd->std", back_ff, a_ff)
    )
    grad_normed_ff, ff_out = collect(
        grad_ff_in.astype(BF).reshape(2, 4, CHUNK, D), down.astype(BF).reshape(2, 4, CHUNK, D)
    )
    result = (residual + ff_out).astype(BF)
    grad_resid = grad_out.astype(F32) + norm_back(residual, scale_ff, norm_ff, grad_normed_ff)
    grad_attn = grad_resid.astype(BF)
    grad_attn = jnp.concatenate(flip(h == 1, grad_attn, swap_h(grad_attn)), axis=0)

    back_o = mm("td,rd->tr", grad_attn, bo)
    grad_a_o = mm("tr,tc->rc", back_o, mixed)
    grad_b_o = mm("tr,td->rd", latent_o, grad_attn)
    grad_mixed = (mm("td,cd->tc", grad_attn, out_w) + mm("tr,rc->tc", back_o, ao)).astype(BF)

    cols = jnp.stack([grad_a_cols, grad_b_gate, grad_b_up]).reshape(6, 16, FF_COLS).astype(BF)
    none = jnp.zeros_like(cols)
    cols = jnp.concatenate(flip(y_lo == 1, cols, none), axis=2)
    ff_wide = jnp.concatenate([grad_a_ff.reshape(2, 2, 16, D), grad_b_out[:, None]], axis=1)
    ff_wide = jnp.moveaxis(ff_wide, 0, 1).reshape(6, 16, D).astype(BF)
    dq, dkv, ff_all = attend_backward(
        q, kv_all, limit, mixed, grad_mixed, lse, cols, grad_a_o.astype(BF)[None],
        grad_b_o.astype(BF)[None], ff_wide,
    )
    dkv = dkv.reshape(2 * CHUNK, 2 * HEAD)
    grad_q = rope_back(dq.reshape(2 * CHUNK, GROUP, HEAD), cos_heads, sine_heads)
    grad_k = rope_back(dkv[:, :HEAD], cos_table, sine_table)
    grad_qkv = jnp.concatenate(
        [grad_q.reshape(2 * CHUNK, group_cols), grad_k, dkv[:, HEAD:]], axis=1
    ).astype(BF)
    back_qkv = mm("to,ro->tr", grad_qkv, b_qkv)
    grad_a_qkv = mm("tr,td->rd", back_qkv, normed)
    grad_b_qkv = mm("tr,to->ro", latent_qkv, grad_qkv)
    grad_normed = (
        mm("to,do->td", grad_qkv[:, :512], qkv_w[0])
        + mm("to,do->td", grad_qkv[:, 512:], qkv_w[1])
        + mm("tr,rd->td", back_qkv, a_qkv)
    ).reshape(2, CHUNK, D)
    mine, theirs = own_slot(grad_normed)
    grad_normed = mine + swap_h(theirs.astype(BF)).astype(F32)
    own_scale = jnp.where(h == 0, scale_in[0], scale_in[1])
    input_grad = grad_resid + norm_back(own_rows, own_scale, norm_in, grad_normed)

    def home(v):
        halves = v.astype(BF).reshape(2, CHUNK // 2, D)
        got = [
            lax.ppermute(lax.dynamic_index_in_dim(halves, core ^ j, 0, keepdims=False), ALL, back_moves[j])
            for j in (0, 1)
        ]
        return jnp.stack(flip(core == 1, got[0], got[1]))

    result_tokens = home(result)
    input_grad = home(input_grad).astype(F32)

    qkv_all = qkv_total(
        grad_a_qkv.reshape(3, 16, D).astype(BF),
        grad_b_qkv[:16, :group_cols].astype(BF)[None],
        jnp.stack(
            [
                grad_b_qkv[16:32, group_cols : group_cols + HEAD],
                grad_b_qkv[32:, group_cols + HEAD :],
            ]
        ).astype(BF),
    )
    pick = (jnp.arange(SETS, dtype=jnp.int32)[:, None] == set_index[None, :]).astype(F32)
    return (result_tokens, input_grad) + tuple(fold(pick, ff_all, qkv_all))


def solution(mesh):
    spread = P(None, ("blk", "uly"), None)
    in_specs = (
        spread, spread, P(), P(), P(), P(), P(),
        P(("blk", "uly"), None), P(("blk", "uly"), None), P(None, "blk", "uly"), P("uly", "blk"),
        P(), P(), P(), P(), P(),
    )
    out_specs = (spread, spread, P(), P(), P(), P(), P())
    return jax.shard_map(body, mesh=mesh, in_specs=in_specs, out_specs=out_specs, check_vma=False)
```

time: 1150 us -> 554 us (0.48)
  the two profiles are of different devices: /device:TPU:1 before, /device:TPU:8 now
where the time goes in v1:
time: 554 us; the launch traced here: 545 us
  Pallas kernels  359 us (65%)
  matrix products  64.1 us (12%)
  waiting for transfers between devices  46 us (8%)
  local copies, waits for them, and re-layouts  32.6 us (6%)
  other arithmetic  23.2 us (4%)
  starting transfers between devices  11.5 us (2%)
  between operations  8.34 us (2%)
    pallas_call x1, Pallas kernels, forward(): pl.pallas_call(forward_kernel, out_shape=(jax.ShapeDtypeStruct((2 * CHUNK...  185 us
    pallas_call x1, Pallas kernels, attend_backward(): pl.pallas_call(backward_kernel, out_shape=(jax.ShapeDtypeStruct((2 * CHUN...  92 us
    dot_general x32, matrix products, mm(): jnp.einsum(spec, a.astype(BF), b.astype(BF), preferred_element_type=F32)  64.1 us
    ppermute x4, waiting for transfers between devices, home(): lax.ppermute(lax.dynamic_index_in_dim(halves, core ^ j, 0, keepdims=False...  46 us
    pallas_call x1, Pallas kernels, collect(): pl.pallas_call(collect_kernel, out_shape=(out, out), in_specs=[ANY, ANY],...  37.4 us
    pallas_call x1, Pallas kernels, qkv_total(): pl.pallas_call(qkv_total_kernel, out_shape=Total.shape(QKV_KEPT, 0), in_s...  34.7 us
  transfers between devices with their start and end apart: 6, of which 4 were waited for; matrix products, arithmetic and copies ran while one was open for 3% of the time, Pallas kernels for 8%

profile of v1, /device:TPU:8, one launch (start us, length us, event | category | flops | bytes accessed | tf_op | source)
XLA Modules:
  0.0 545.0 jit_solution(1252538974212983243)
XLA Ops:
  30.2 185.5 %forward.1 = (bf16[256,768]{1,0:T(8,128)(2,1)S(1)}, bf16[256,768]{1,0:T(8,128)(2,1)S(1)}, f32[2,8,768]{2,1,0:T(8,128)S(1)}, bf16[64,128,256]{2,1,0:T(8,128)(2,1)...) custom-call(bf16[4,16,512]{2,1,0:T(8,128)(2,1)S(1)} %pad.34.qkv_ref,, ...), custom_call_target="tpu_custom_call" | custom-call | tf_op jit(solution)/shard_map/forward/pallas_call | solution.py:684
  215.7 10.0 %fusion.64 = f32[2,512,1152]{2,1,0:T(8,128)} fusion(bf16[2,512,1536]{2,1,0:T(8,128)(2,1)} %bitcast.168, bf16[1536,1152,1]{1,0,2:T(8,128)(2,1)} %bitcast.197), kind=kOutput, calls=%fused_computation.181 | convolution fusion | flops 3623878656 | bytes 11403264 | tf_op jit(solution)/shard_map/std,df->stf/dot_general | solution.py:1307
  225.8 5.8 %fusion.65 = f32[2,512,1152]{2,1,0:T(8,128)} fusion(bf16[2,512,1536]{2,1,0:T(8,128)(2,1)S(1)} %bitcast.170, bf16[1536,1152,1]{1,0,2:T(8,128)(2,1)S(1)} %bitcast.195), kind=kOutput, calls=%fused_computation.182 | convolution fusion | flops 3623878656 | bytes 11403264 | tf_op jit(solution)/shard_map/std,df->stf/dot_general | solution.py:1307
  234.4 5.9 %fusion.63 = f32[2,512,1152]{2,1,0:T(8,128)} fusion(bf16[2,512,1536]{2,1,0:T(8,128)(2,1)S(1)} %bitcast.165, bf16[1536,1152,1]{1,0,2:T(8,128)(2,1)S(1)} %bitcast.199), kind=kOutput, calls=%fused_computation.180 | convolution fusion | flops 3623878656 | bytes 11403264 | tf_op jit(solution)/shard_map/std,df->stf/dot_general | solution.py:1307
  241.8 3.0 convolution_convert_fusion.9
  250.2 5.0 multiply_convert_fusion
  256.0 4.3 fusion.68
  261.0 4.3 fusion.67
  265.9 4.3 fusion.66
  272.5 37.4 %collect.1 = (f32[128,1536]{1,0:T(8,128)S(1)}, f32[128,1536]{1,0:T(8,128)S(1)}) custom-call(bf16[2,4,128,1536]{3,2,1,0:T(8,128)(2,1)S(1)} %bitcast.160, bf16[2,4,128,1536]{3,2,1,0:T(8,128)(2,1)S(1)} %bitcast.159), custom_call_target="tpu_custom_call" | custom-call | tf_op jit(solution)/shard_map/collect/pallas_call | solution.py:826
  311.2 2.2 collective-permute-start.2
  332.7 3.2 fusion.11.grad_ref
  335.9 92.0 %attend_backward.1 = (f32[256,768]{1,0:T(8,128)}, f32[2,128,256]{2,1,0:T(8,128)}, bf16[2,32,10,16,128]{4,3,2,1,0:T(8,128)(2,1)}) custom-call(bf16[256,768]{1,0:T(8,128)(2,1)} %copy-done.9, bf16[64,128,256]{2,1,0:T(8,128)(2,1)} %get-tuple-element.44.kv_ref, s32[2,8,768]{2,1,0:T(8,128)} %copy-done.6, bf16[256,768]{1,0:T(8,128)(2,1)} %copy-done.1, ...), custom_call_target="tpu_custom_call" | custom-call | tf_op jit(solution)/shard_map/attend_backward/pallas_call | solution.py:1127
  429.9 2.1 fusion.26
  434.6 2.3 copy.31
  442.5 34.7 %qkv_total.1.qkv_ref = bf16[2,32,4,16,128]{4,3,2,1,0:T(8,128)(2,1)S(1)} custom-call(bf16[3,16,1536]{2,1,0:T(8,128)(2,1)S(1)} %bitcast.163, bf16[1,16,768]{2,1,0:T(8,128)(2,1)S(1)} %slice_bitcast_fusion.6.bq_ref, bf16[2,16,128]{2,1,0:T(8,128)(2,1)S(1)} %pad_maximum_fusion.23.bkv_ref), custom_call_target="tpu_custom_call" | custom-call | tf_op jit(solution)/shard_map/qkv_total/pallas_call | solution.py:1162
  477.3 9.7 %fold.1 = (f32[6,8,16,1536]{3,2,1,0:T(8,128)}, f32[8,16,8960]{2,1,0:T(8,128)}, f32[3,8,16,1536]{3,2,1,0:T(8,128)}, f32[2,8,16,256]{3,2,1,0:T(8,128)}, f32[2,8,16,8960]{3,2,1,0:T(8,128)}) custom-call(f32[8,2]{1,0:T(8,128)S(1)} %fusion.39.pick_ref, bf16[2,32,10,16,128]{4,3,2,1,0:T(8,128)(2,1)S(1)} %copy-done, bf16[2,32,4,16,128]{4,3,2,1,0:T(8,128)(2,1)S(1)} %qkv_total.1.qkv_ref), custom_call_target="tpu_custom_call" | custom-call | tf_op jit(solution)/shard_map/fold/pallas_call | solution.py:1237
  489.5 2.5 collective-permute-start.5
  492.1 2.4 collective-permute-start
  494.5 2.4 collective-permute-start.1
  497.0 21.9 %collective-permute-done.4 = bf16[64,1536]{1,0:T(8,128)(2,1)S(1)} collective-permute-done((bf16[64,1536]{1,0:T(8,128)(2,1)S(1)}, bf16[64,1536]{1,0:T(8,128)(2,1)S(1)}, u32[]{:S(2)}, u32[]{:S(2)}) %collective-permute-start.4) | collective-permute-done | bytes 196640 | tf_op jit(solution)/shard_map/ppermute | solution.py:1483
  518.8 8.7 %collective-permute-done.5 = bf16[64,1536]{1,0:T(8,128)(2,1)S(1)} collective-permute-done((bf16[64,1536]{1,0:T(8,128)(2,1)S(1)}, bf16[64,1536]{1,0:T(8,128)(2,1)S(1)}, u32[]{:S(2)}, u32[]{:S(2)}) %collective-permute-start.5) | collective-permute-done | bytes 196640 | tf_op jit(solution)/shard_map/ppermute | solution.py:1483
  528.5 7.4 %collective-permute-done = bf16[64,1536]{1,0:T(8,128)(2,1)S(1)} collective-permute-done((bf16[64,1536]{1,0:T(8,128)(2,1)S(1)}, bf16[64,1536]{1,0:T(8,128)(2,1)S(1)}, u32[]{:S(2)}, u32[]{:S(2)}) %collective-permute-start) | collective-permute-done | bytes 196640 | tf_op jit(solution)/shard_map/ppermute | solution.py:1483
  535.9 8.1 %collective-permute-done.1 = bf16[64,1536]{1,0:T(8,128)(2,1)S(1)} collective-permute-done((bf16[64,1536]{1,0:T(8,128)(2,1)S(1)}, bf16[64,1536]{1,0:T(8,128)(2,1)S(1)}, u32[]{:S(2)}, u32[]{:S(2)}) %collective-permute-start.1) | collective-permute-done | bytes 196640 | tf_op jit(solution)/shard_map/ppermute | solution.py:1483
  (226 shorter events, 71.5 us)
Async XLA Ops:
  0.6 17.0 %slice-start.3 = ((bf16[12,2048]{1,0:T(8,128)(2,1)}), bf16[12,1536]{1,0:T(8,128)(2,1)S(1)}, s32[]{:S(2)}) async-start(bf16[12,2048]{1,0:T(8,128)(2,1)} %param.23), calls=%async_computation.3 | async-start | bytes 98304 | tf_op jit(solution)/shard_map/slice | solution.py:1339
  0.6 13.8 %copy-start.26 = (bf16[6,8,16,1536]{3,2,1,0:T(8,128)(2,1)S(1)}, bf16[6,8,16,1536]{3,2,1,0:T(8,128)(2,1)}, u32[]{:S(2)}) copy-start(bf16[6,8,16,1536]{3,2,1,0:T(8,128)(2,1)} %param.27) | copy-start | bytes 7077892
  0.7 10.6 %copy-start.37 = (bf16[2,8,16,256]{3,2,1,0:T(8,128)(2,1)S(1)}, bf16[2,8,16,256]{3,2,1,0:T(8,128)(2,1)}, u32[]{:S(2)}) copy-start(bf16[2,8,16,256]{3,2,1,0:T(8,128)(2,1)} %param.30) | copy-start | bytes 393220
  0.7 18.6 %copy-start.42 = (f32[1536]{0:T(1024)S(1)}, f32[1536]{0:T(1024)}, u32[]{:S(2)}) copy-start(f32[1536]{0:T(1024)} %param.20) | copy-start | bytes 18436
  0.7 18.6 %copy-start.38 = (f32[1536]{0:T(1024)S(1)}, f32[1536]{0:T(1024)}, u32[]{:S(2)}) copy-start(f32[1536]{0:T(1024)} %param.21) | copy-start | bytes 18436
  12.5 11.3 %copy-start.34 = (bf16[2,48,2240]{2,1,0:T(8,128)(2,1)S(1)}, bf16[2,48,2240]{2,1,0:T(8,128)(2,1)}, u32[]{:S(2)}) copy-start(bf16[2,48,2240]{2,1,0:T(8,128)(2,1)} %param.25) | copy-start | bytes 1290244
  26.9 198.8 %copy-start.6 = (s32[2,8,768]{2,1,0:T(8,128)}, s32[2,8,768]{2,1,0:T(8,128)S(1)}, u32[]{:S(2)}) copy-start(s32[2,8,768]{2,1,0:T(8,128)S(1)} %broadcast_in_dim.69.limit_ref) | copy-start | bytes 147460
  215.7 10.1 %copy-start.2 = (bf16[256,1536]{1,0:T(8,128)(2,1)}, bf16[256,1536]{1,0:T(8,128)(2,1)S(1)}, u32[]{:S(2)}) copy-start(bf16[256,1536]{1,0:T(8,128)(2,1)S(1)} %get-tuple-element.52) | copy-start | bytes 2359300
  215.7 10.0 %copy-start.9 = (bf16[256,768]{1,0:T(8,128)(2,1)}, bf16[256,768]{1,0:T(8,128)(2,1)S(1)}, u32[]{:S(2)}) copy-start(bf16[256,768]{1,0:T(8,128)(2,1)S(1)} %get-tuple-element.43.q_ref) | copy-start | bytes 1179652
  215.7 10.0 %copy-start.15 = (f32[2,8,768]{2,1,0:T(8,128)}, f32[2,8,768]{2,1,0:T(8,128)S(1)}, u32[]{:S(2)}) copy-start(f32[2,8,768]{2,1,0:T(8,128)S(1)} %get-tuple-element.47.lse_ref) | copy-start | bytes 147460
  215.7 10.0 %copy-start.16 = (f32[256,48]{1,0:T(8,128)}, f32[256,48]{1,0:T(8,128)S(1)}, u32[]{:S(2)}) copy-start(f32[256,48]{1,0:T(8,128)S(1)} %get-tuple-element.53) | copy-start | bytes 147460
  215.7 115.9 %copy-start.1 = (bf16[256,768]{1,0:T(8,128)(2,1)}, bf16[256,768]{1,0:T(8,128)(2,1)S(1)}, u32[]{:S(2)}) copy-start(bf16[256,768]{1,0:T(8,128)(2,1)S(1)} %get-tuple-element.45.mixed_ref) | copy-start | bytes 1179652
  215.7 10.0 %copy-start.21 = (bf16[2,4,128,1536]{3,2,1,0:T(8,128)(2,1)S(1)}, bf16[2,4,128,1536]{3,2,1,0:T(8,128)(2,1)}, u32[]{:S(2)}) copy-start(bf16[2,4,128,1536]{3,2,1,0:T(8,128)(2,1)} %get-tuple-element.36) | copy-start | bytes 9437188
  215.7 10.0 %copy-start.47 = (bf16[32,48,1152]{2,1,0:T(8,128)(2,1)S(1)}, bf16[32,48,1152]{2,1,0:T(8,128)(2,1)}, u32[]{:S(2)}) copy-start(bf16[32,48,1152]{2,1,0:T(8,128)(2,1)} %get-tuple-element.38) | copy-start | bytes 10616836
  270.4 39.8 %copy-start.43 = (f32[128]{0:T(128)}, f32[128]{0:T(128)S(1)}, u32[]{:S(2)}) copy-start(f32[128]{0:T(128)S(1)} %add_rsqrt_fusion.1) | copy-start | bytes 1540
  311.2 17.6 %collective-permute-start.2 = (bf16[128,1536]{1,0:T(8,128)(2,1)}, bf16[128,1536]{1,0:T(8,128)(2,1)}, u32[]{:S(2)}, u32[]{:S(2)}) collective-permute-start(bf16[128,1536]{1,0:T(8,128)(2,1)} %fusion.55), channel_id=1, source_target_pairs={{0,2},{2,0},{1,3},{3,1},{4,6},{6,4},{5,7},{7,5},{8,10},{10,8},{9,1... | collective-permute-start | bytes 1179656 | tf_op jit(solution)/shard_map/ppermute | solution.py:1398
  335.9 94.0 %copy-start.28 = (f32[256,64]{1,0:T(8,128)S(1)}, f32[256,64]{1,0:T(8,128)}, u32[]{:S(2)}) copy-start(f32[256,64]{1,0:T(8,128)} %copy-done.27) | copy-start | bytes 196612
  441.2 36.1 %copy-start = (bf16[2,32,10,16,128]{4,3,2,1,0:T(8,128)(2,1)S(1)}, bf16[2,32,10,16,128]{4,3,2,1,0:T(8,128)(2,1)}, u32[]{:S(2)}) copy-start(bf16[2,32,10,16,128]{4,3,2,1,0:T(8,128)(2,1)} %get-tuple-element.51.ff_ref) | copy-start | bytes 7864324
  441.7 45.3 %copy-start.18 = (f32[256,1536]{1,0:T(8,128)S(1)}, f32[256,1536]{1,0:T(8,128)}, u32[]{:S(2)}) copy-start(f32[256,1536]{1,0:T(8,128)} %convert_element_type.141) | copy-start | bytes 4718596
  441.7 45.3 %collective-permute-start.3 = (bf16[128,1536]{1,0:T(8,128)(2,1)S(1)}, bf16[128,1536]{1,0:T(8,128)(2,1)S(1)}, u32[]{:S(2)}, u32[]{:S(2)}) collective-permute-start(bf16[128,1536]{1,0:T(8,128)(2,1)S(1)} %select_convert_fusion), channel_id=1, source_target_pairs={{0,2},{2,0},{1,3},{3,1},{4,6},{6,4},{5,7},{7,5},{8,10},{10,8},{9,1... | collective-permute-start | bytes 1179656 | tf_op jit(solution)/shard_map/ppermute | solution.py:1398
  488.0 30.8 %collective-permute-start.4 = (bf16[64,1536]{1,0:T(8,128)(2,1)S(1)}, bf16[64,1536]{1,0:T(8,128)(2,1)S(1)}, u32[]{:S(2)}, u32[]{:S(2)}) collective-permute-start(bf16[64,1536]{1,0:T(8,128)(2,1)S(1)} %get-tuple-element.79), channel_id=1, source_target_pairs={{1,0},{0,1},{5,2},{4,3},{9,4},{8,5},{13,6},{12,7},{17,8},{16,9},{2... | collective-permute-start | bytes 589832 | tf_op jit(solution)/shard_map/ppermute | solution.py:1483
  489.5 38.1 %collective-permute-start.5 = (bf16[64,1536]{1,0:T(8,128)(2,1)S(1)}, bf16[64,1536]{1,0:T(8,128)(2,1)S(1)}, u32[]{:S(2)}, u32[]{:S(2)}) collective-permute-start(bf16[64,1536]{1,0:T(8,128)(2,1)S(1)} %get-tuple-element.80), channel_id=1, source_target_pairs={{0,0},{1,1},{4,2},{5,3},{8,4},{9,5},{12,6},{13,7},{16,8},{17,9},{2... | collective-permute-start | bytes 589832 | tf_op jit(solution)/shard_map/ppermute | solution.py:1483
  492.1 43.8 %collective-permute-start = (bf16[64,1536]{1,0:T(8,128)(2,1)S(1)}, bf16[64,1536]{1,0:T(8,128)(2,1)S(1)}, u32[]{:S(2)}, u32[]{:S(2)}) collective-permute-start(bf16[64,1536]{1,0:T(8,128)(2,1)S(1)} %get-tuple-element.83), channel_id=1, source_target_pairs={{1,0},{0,1},{5,2},{4,3},{9,4},{8,5},{13,6},{12,7},{17,8},{16,9},{2... | collective-permute-start | bytes 589832 | tf_op jit(solution)/shard_map/ppermute | solution.py:1483
  494.5 49.5 %collective-permute-start.1 = (bf16[64,1536]{1,0:T(8,128)(2,1)S(1)}, bf16[64,1536]{1,0:T(8,128)(2,1)S(1)}, u32[]{:S(2)}, u32[]{:S(2)}) collective-permute-start(bf16[64,1536]{1,0:T(8,128)(2,1)S(1)} %get-tuple-element.84), channel_id=1, source_target_pairs={{0,0},{1,1},{4,2},{5,3},{8,4},{9,5},{12,6},{13,7},{16,8},{17,9},{2... | collective-permute-start | bytes 589832 | tf_op jit(solution)/shard_map/ppermute | solution.py:1483
  (38 other events, 173.1 us)

commit v2 on v1

--- a/solution.py
+++ b/solution.py
@@ -49,10 +49,12 @@
     ]
 
 
-def greet(others):
+def greet(others, meanwhile=None):
     barrier = pltpu.get_barrier_semaphore()
     for other in others:
         pl.semaphore_signal(barrier, inc=1, device_id=other, device_id_type=MESH)
+    if meanwhile is not None:
+        meanwhile()
     pl.semaphore_wait(barrier, len(others))
 
 
@@ -341,23 +343,21 @@
     def start(self):
         for d in (1, 3):
             self.send(self.p, self.q, d, 0, self.src)
-        for d in (1, 3):
-            self.send(self.p, self.q, 0, d, self.src)
-
-    def third(self):
+
+    def second(self):
         for d in (4 - self.way, self.way):
             p = (self.p + d) % 4
             self.wait(p, self.q)
             if d == 4 - self.way:
                 self.send(p, self.q, self.way, 0)
-            for e in (1, 3):
-                self.send(p, self.q, 0, e)
-
-    def third_late(self):
-        p = (self.p + 2) % 4
-        self.wait(p, self.q)
-        for e in (1, 3):
-            self.send(p, self.q, 0, e)
+
+    def third(self):
+        self.wait((self.p + 2) % 4, self.q)
+
+    def spread(self, e):
+        p = (self.p + e) % 4
+        for d in (1, 3):
+            self.send(p, self.q, 0, d, self.src if e == 0 else None)
 
     def fourth(self, e):
         p = (self.p + e) % 4
@@ -433,12 +433,12 @@
 
 
 def forward_kernel(
-    qkv_ref, out_ref, tokens_ref, cot_ref, ff_ref, limit_ref, length_ref, norm_in_ref, norm_ff_ref, bias_ref, cos_ref, sin_ref,
-    a_qkv_ref, b_qkv_ref, ao_ref, bo_ref,
+    tokens_ref, cot_ref, length_ref, qkv_ref, out_ref, gate_up_ref, down_ref, norm_in_ref, norm_ff_ref,
+    bias_ref, freq_ref, a_ref, b_ref, bkv_ref,
     q_ref, mixed_ref, lse_ref, kv_out, wq_out, wo_out, gate_all, up_all, down_all, rows_out, normed_ref,
-    latent_ref, resid_ref, cot_own, nf_all, cot_all,
+    resid_ref, cot_own, nf_all, cot_all, limit_ref, cos_ref, sin_ref, b_qkv_ref, ao_ref,
     kv_all, wq_all, wo_all, rows, cot_in, kv_part, acc_ref, stat_ref, qkv_in, out_in, qkv_part, out_part,
-    nf_own, cross_out, cross_in,
+    nf_own, cross_out, cross_in, qkv_pieces, out_pieces, ff_ref,
     *sems,
 ):
     y, z, x, blk, uly = place()
@@ -458,17 +458,41 @@
     out_to = [(2 * (blk % 16) + q // 2, (blk // 16) * 2 + q % 2) for q in range(4)]
     out_from = [(16 * h + blk // 2, u) for u in range(4)]
     sibling = uly_others()[1]
+    length = length_ref[0] * (1 - core) + length_ref[1] * core
+
+    def prepare():
+        qkv_pieces[...] = jnp.zeros_like(qkv_pieces)
+        out_pieces[...] = jnp.zeros_like(out_pieces)
+        group = GROUP * HEAD
+        for hh in (0, 1):
+            qkv_pieces[2 * hh, :12] = qkv_ref[:, hh * group : hh * group + 512]
+            for place_at, start, size in (
+                (0, hh * group + 512, 256),
+                (256, HEADS * HEAD + hh * HEAD, HEAD),
+                (384, HEADS * HEAD + 256 + hh * HEAD, HEAD),
+            ):
+                qkv_pieces[2 * hh + 1, :12, place_at : place_at + size] = qkv_ref[:, start : start + size]
+        for q in range(4):
+            out_pieces[q, :12] = out_ref[:, q * 384 : (q + 1) * 384]
+        for n in range(3):
+            part = (gate_up_ref[n] if n < 2 else down_ref[...]).astype(F32)
+            none = jnp.zeros((48, 64), F32)
+            left = jnp.concatenate([part, none], axis=1)
+            right = jnp.concatenate([none, part], axis=1)
+            ff_ref[n] = jnp.where(jnp.broadcast_to(core, (48, PADDED)) == 1, right, left).astype(BF)
+
     greet(
         ring_others() + uly_others() + [(blk_of(1 - y, z, x), (uly + 2) % 4)]
-        + row_to[0] + row_to[1] + row_from + out_to + out_from
+        + row_to[0] + row_to[1] + row_from + out_to + out_from,
+        prepare,
     )
 
     deliver = Deliver()
     piece_send, piece_recv, row_send, row_recv = take(4)
     for q in range(4):
-        deliver.send(qkv_ref.at[q], qkv_in.at[uly], piece_send.at[q], piece_recv.at[uly], (blk, q))
+        deliver.send(qkv_pieces.at[q], qkv_in.at[uly], piece_send.at[q], piece_recv.at[uly], (blk, q))
     for q in range(4):
-        deliver.send(out_ref.at[q], out_in.at[uly], piece_send.at[4 + q], piece_recv.at[4 + uly], out_to[q])
+        deliver.send(out_pieces.at[q], out_in.at[uly], piece_send.at[4 + q], piece_recv.at[4 + uly], out_to[q])
     for s in (0, 1):
         for hh in (0, 1):
             deliver.send(
@@ -537,9 +561,40 @@
         ]
         for k in (0, 1)
     )
+    rings = own_ff + other_ff
     wq.second()
+    wq.third()
+    wq.fourth()
     for ring in own_ff:
         ring.start()
+    for n in range(3):
+        y_copies[2 * n].wait_recv()
+    for ring in other_ff:
+        ring.start()
+
+    for slot, at in ((0, blk), (1, 63 - blk)):
+        row = lax.broadcasted_iota(jnp.int32, (CHUNK, HEAD), 0) + at * CHUNK
+        angle = row.astype(F32) * freq_ref[...]
+        first = lax.broadcasted_iota(jnp.int32, (CHUNK, HEAD), 1) < HEAD // 2
+        sine = jnp.sin(angle)
+        cos_ref[slot * CHUNK : (slot + 1) * CHUNK, :] = jnp.cos(angle)
+        sin_ref[slot * CHUNK : (slot + 1) * CHUNK, :] = jnp.where(first, -sine, sine)
+        row = lax.broadcasted_iota(jnp.int32, (8, ROWS), 1) % CHUNK + at * CHUNK
+        limit_ref[slot] = jnp.minimum(row, length - 1)
+    group = GROUP * HEAD
+    group_at = pl.ds(pl.multiple_of(h * group, 128), group)
+    head_at = pl.ds(pl.multiple_of(h * HEAD, 128), HEAD)
+    ao_ref[...] = a_ref[3, :, group_at]
+    b_qkv_ref[...] = jnp.zeros_like(b_qkv_ref)
+    b_qkv_ref[:16, :group] = b_ref[0, :, group_at]
+    b_qkv_ref[16:32, group : group + HEAD] = bkv_ref[0, :, head_at]
+    b_qkv_ref[32:, group + HEAD :] = bkv_ref[1, :, head_at]
+    a_qkv = a_ref[:3].reshape(48, D)
+    bo_ref = b_ref.at[1]
+
+    def bias(n):
+        at = h * GROUP + n if n < GROUP else HEADS + 2 * (n - GROUP) + h
+        return bias_ref[pl.ds(at, 1), :]
 
     for n in range(4):
         wait_arrival(rows.at[n // 2, n % 2], row_recv.at[n])
@@ -547,16 +602,8 @@
         at = slice(n * 64, (n + 1) * 64)
         rows_out[at, :] = rows[n // 2, n % 2]
         normed_ref[at, :] = (value * norm_scale(value) * norm_in_ref[...]).astype(BF)
-    latent = dot_nt(normed_ref[...], a_qkv_ref[...])
-    latent_ref[...] = latent
-    wq.third()
-    wo.start()
-    wq.fourth()
-    wo.second()
-    for n in range(3):
-        y_copies[2 * n].wait_recv()
-    for ring in other_ff:
-        ring.start()
+    latent = dot_nt(normed_ref[...], a_qkv)
+    adapted = dot(latent.astype(BF), b_qkv_ref[...])
     wq.last()
     pair_send, pair_recv = take(2)
 
@@ -564,54 +611,59 @@
         return remote(ref, ref, pair_send.at[n], pair_recv.at[n], sibling)
 
     pair_copy(wq_all.at[core], 0).start()
-    wo.third()
+    wo.start()
     pair_copy(wq_all.at[core], 0).wait_send()
     pair_copy(wq_all.at[1 - core], 0).wait_recv()
 
-    adapted = dot(latent.astype(BF), b_qkv_ref[...]) + bias_ref[...]
     cos_table, sine_table = cos_ref[...], sin_ref[...]
-    for c in (0, 1):
-        columns = dot(normed_ref[...], wq_all[c]) + adapted[:, c * 512 : (c + 1) * 512]
-        for n in range(4):
-            head = columns[:, n * HEAD : (n + 1) * HEAD]
-            if c * 4 + n < GROUP + 1:
-                head = head * cos_table + pltpu.roll(head, HEAD // 2, 1) * sine_table
-            if c * 4 + n < GROUP:
-                at = (c * 4 + n) * HEAD
-                q_ref[:, at : at + HEAD] = (head * (HEAD ** (-0.5) * LOG2E)).astype(BF)
-            else:
-                at = (n - 2) * HEAD
-                kv_part[0, :, at : at + HEAD] = head[:CHUNK].astype(BF)
-                kv_part[1, :, at : at + HEAD] = head[CHUNK:].astype(BF)
+
+    def turn(head):
+        return head * cos_table + pltpu.roll(head, HEAD // 2, 1) * sine_table
+
+    def query(n, head):
+        q_ref[:, n * HEAD : (n + 1) * HEAD] = (turn(head + bias(n)) * (HEAD ** (-0.5) * LOG2E)).astype(BF)
+
+    pairs = dot(normed_ref[...], wq_all[1, :, 256:]) + adapted[:, 768:]
+    for n, head in ((0, turn(pairs[:, :HEAD] + bias(6))), (1, pairs[:, HEAD:] + bias(7))):
+        at = slice(n * HEAD, (n + 1) * HEAD)
+        kv_part[0, :, at] = head[:CHUNK].astype(BF)
+        kv_part[1, :, at] = head[CHUNK:].astype(BF)
     kv = Gather(
         lambda s: kv_part.at[s],
         lambda s, item: kv_all.at[item if s == 0 else 63 - item],
         *take(3),
     )
     kv.start()
-    for ring in own_ff:
+    heads = dot(normed_ref[...], wq_all[1, :, :256]) + adapted[:, 512:768]
+    for n in (4, 5):
+        query(n, heads[:, (n - 4) * HEAD : (n - 3) * HEAD])
+    kv.second()
+    for ring in rings:
+        ring.second()
+    wo.second()
+    heads = dot(normed_ref[...], wq_all[0]) + adapted[:, :512]
+    for n in range(4):
+        query(n, heads[:, n * HEAD : (n + 1) * HEAD])
+    kv.third()
+    for ring in rings:
         ring.third()
-    kv.second()
-    for ring in own_ff:
-        ring.third_late()
-    for ring in other_ff:
-        ring.third()
-    kv.third()
+    wo.third()
+    kv.fourth()
     wo.fourth()
-    for ring in other_ff:
-        ring.third_late()
-    kv.fourth()
 
     for half in (0, 1):
         wait_arrival(cot_in.at[half], row_recv.at[4 + half])
         start = ((1 - h) * blk + h * (63 - blk)) * CHUNK + half * 64
         at = lax.broadcasted_iota(jnp.int32, (64, D), 0) + start
         cot_own[half * 64 : (half + 1) * 64, :] = jnp.where(
-            at < length_ref[...], cot_in[half].astype(F32), 0.0
+            at < length, cot_in[half].astype(F32), 0.0
         ).astype(BF)
     cot_spread = Spread(cot_own, cot_all, *take(3))
     cot_spread.start()
     kv.last()
+    for e in (0, 1, 3, 2):
+        for ring in rings:
+            ring.spread(e)
     (out_sem,) = take(1)
     copies = [
         pltpu.make_async_copy(src, dst, out_sem.at[n])
@@ -627,20 +679,17 @@
     for n in (0, 1):
         pair_copy(wo_columns(core, n), 1 + n).start()
     args = (q_ref, kv_all, limit_ref, mixed_ref, lse_ref, acc_ref, stat_ref)
-    beside = [
-        lambda: [ring.fourth(0) for ring in own_ff],
-        lambda: [ring.fourth(0) for ring in other_ff] + [cot_spread.second()],
-        lambda: [ring.fourth(1) for ring in own_ff],
-        lambda: [ring.fourth(1) for ring in other_ff] + [cot_spread.third()],
-        lambda: [ring.fourth(3) for ring in own_ff],
-        lambda: [ring.fourth(3) for ring in other_ff],
-        lambda: [ring.fourth(2) for ring in own_ff],
-        lambda: [ring.fourth(2) for ring in other_ff],
-    ]
+    beside = {
+        3: lambda: [ring.fourth(0) for ring in rings] + [cot_spread.second()],
+        5: lambda: [ring.fourth(1) for ring in rings],
+        6: lambda: [ring.fourth(3) for ring in rings] + [cot_spread.third()],
+        7: lambda: [ring.fourth(2) for ring in rings],
+    }
     for slot, at in ((0, blk), (1, 63 - blk)):
         for part in range(4):
             forward_slot(slot, at, part, *args)
-            beside.pop(0)()
+            if slot * 4 + part in beside:
+                beside[slot * 4 + part]()
     for n in (0, 1):
         pair_copy(wo_columns(core, n), 1 + n).wait_send()
         pair_copy(wo_columns(1 - core, n), 1 + n).wait_recv()
@@ -666,7 +715,7 @@
     nf_spread.third()
     nf_spread.last()
     cot_spread.last()
-    for ring in own_ff + other_ff:
+    for ring in rings:
         ring.last()
     for n in range(3):
         y_copies[2 * n].wait_send()
@@ -693,13 +742,17 @@
             weight, weight, weight,
             jax.ShapeDtypeStruct((2 * CHUNK, D), BF),
             jax.ShapeDtypeStruct((2 * CHUNK, D), BF),
-            jax.ShapeDtypeStruct((2 * CHUNK, 48), F32),
             jax.ShapeDtypeStruct((CHUNK, D), F32),
             jax.ShapeDtypeStruct((CHUNK, D), BF),
             spread, spread,
+            jax.ShapeDtypeStruct((2, 8, ROWS), jnp.int32),
+            jax.ShapeDtypeStruct((2 * CHUNK, HEAD), F32),
+            jax.ShapeDtypeStruct((2 * CHUNK, HEAD), F32),
+            jax.ShapeDtypeStruct((48, 1024), BF),
+            jax.ShapeDtypeStruct((16, group), BF),
         ),
-        in_specs=[ANY] * 5 + [IN_VMEM] * 11,
-        out_specs=(IN_VMEM,) * 3 + (ANY,) * 6 + (IN_VMEM,) * 5 + (ANY,) * 2,
+        in_specs=[ANY] * 2 + [pl.BlockSpec(memory_space=pltpu.SMEM)] + [IN_VMEM] * 11,
+        out_specs=(IN_VMEM,) * 3 + (ANY,) * 6 + (IN_VMEM,) * 4 + (ANY,) * 2 + (IN_VMEM,) * 5,
         scratch_shapes=[
             pltpu.VMEM((CHUNKS, CHUNK, 2 * HEAD), BF),
             pltpu.VMEM((2, D, 512), BF),
@@ -716,6 +769,9 @@
             pltpu.VMEM((CHUNK, D), BF),
             pltpu.VMEM((CHUNK, D), BF),
             pltpu.VMEM((CHUNK, D), BF),
+            pltpu.VMEM((4, 16, 512), BF),
+            pltpu.VMEM((4, 16, 384), BF),
+            pltpu.VMEM((3, 48, PADDED), BF),
             dma((8,)), dma((8,)), dma((6,)), dma((6,)),
             dma((2, 3, Ring.sends)), dma((2, 3, 16)), dma((3,)), dma((3,)), dma((3,)),
         ]
@@ -806,34 +862,126 @@
         return total
 
 
-def collect_kernel(a_ref, b_ref, a_out, b_out, *scratch):
+def ff_kernel(
+    set_ref, x_hbm, cot_hbm, gate_hbm, up_hbm, down_hbm, a_wide, a_down, b_wide, b_ff,
+    grad_out, down_out, cols_ref, wide_ref,
+    x_ref, cot_ref, gate_w, up_w, down_w, a_ff, b_cols, a_cols, b_out, hidden_ref, grad_gate, grad_up,
+    out_buf, sems, out_sems,
+):
     y, z, x, blk, uly = place()
-    greet([uly_others()[1], (blk_of(1 - y, z, x), uly), (blk_of(1 - y, z, x), (uly + 2) % 4)])
-    a = Collect(a_ref, scratch[: Collect.scratches])
-    b = Collect(b_ref, scratch[Collect.scratches :])
-    a.start()
-    a.second()
-    a.third()
-    b.start()
-    a_out[...] = a.fourth()
-    b.second()
-    b.third()
-    b_out[...] = b.fourth()
-
-
-def collect(a, b):
-    out = jax.ShapeDtypeStruct((CHUNK, D), F32)
+    core = uly % 2
+    first = (35 * uly) // 2 * 128 + y * FF_COLS
+    columns = pl.ds(pl.multiple_of(first, 128), FF_COLS)
+    pairs = [(down_hbm, down_w), (cot_hbm, cot_ref), (x_hbm, x_ref), (gate_hbm, gate_w), (up_hbm, up_w)]
+    for s in (0, 1):
+        chosen = set_ref[s]
+        for n in (0, 1):
+            pairs.append((a_wide.at[4 + n, chosen], a_ff.at[s, pl.ds(16 * n, 16)]))
+            pairs.append((b_ff.at[n, chosen, :, columns], b_cols.at[s, n]))
+        pairs.append((a_down.at[chosen, :, columns], a_cols.at[s]))
+        pairs.append((b_wide.at[2, chosen], b_out.at[s]))
+    copies = [pltpu.make_async_copy(src, dst, sems.at[n]) for n, (src, dst) in enumerate(pairs)]
+    for copy in copies[5:] + copies[:5]:
+        copy.start()
+    for copy in copies[5:]:
+        copy.wait()
+    at = lax.broadcasted_iota(jnp.int32, (16, FF_COLS), 1) + (y * FF_COLS - 64 * core)
+    inside = jnp.logical_and(at >= 0, at < FF // 4)
+
+    def keep(v):
+        return jnp.where(inside, v.astype(F32), 0.0).astype(BF)
+
+    for s in (0, 1):
+        a_cols[s] = keep(a_cols[s])
+        for n in (0, 1):
+            b_cols[s, n] = keep(b_cols[s, n])
+    cols_ref[...] = jnp.zeros_like(cols_ref)
+    here = pl.ds(pl.multiple_of(y * FF_COLS, 128), FF_COLS)
+    copies[0].wait()
+    copies[1].wait()
+
+    def flat(ref, s):
+        return ref[s].reshape(4 * CHUNK, D)
+
+    out_copies = []
+    for s in (0, 1):
+        cot = flat(cot_ref, s)
+        latent_cot = dot_nt(cot, b_out[s])
+        grad_hidden = dot(cot, down_w[...]) + dot(latent_cot.astype(BF), a_cols[s])
+        if s == 0:
+            for copy in copies[2:5]:
+                copy.wait()
+        rows = flat(x_ref, s)
+        latent = dot_nt(rows, a_ff[s])
+        low = latent.astype(BF)
+        gate = dot(rows, gate_w[...]) + dot(low[:, :16], b_cols[s, 0])
+        sigmoid = jax.nn.sigmoid(gate)
+        silu = gate * sigmoid
+        grad_up[...] = (grad_hidden * silu).astype(BF)
+        slope = grad_hidden * (sigmoid * (1.0 + gate * (1.0 - sigmoid)))
+        up = dot(rows, up_w[...]) + dot(low[:, 16:], b_cols[s, 1])
+        grad_gate[...] = (slope * up).astype(BF)
+        hidden_ref[...] = (silu * up).astype(BF)
+        back_gate = dot_nt(grad_gate[...], b_cols[s, 0])
+        back_up = dot_nt(grad_up[...], b_cols[s, 1])
+        grads = (
+            dot_nt(grad_gate[...], gate_w[...])
+            + dot_nt(grad_up[...], up_w[...])
+            + dot(back_gate.astype(BF), a_ff[s, :16])
+            + dot(back_up.astype(BF), a_ff[s, 16:])
+        )
+        out_buf[0, s] = grads.astype(BF).reshape(4, CHUNK, D)
+        copy = pltpu.make_async_copy(out_buf.at[0, s], grad_out.at[s], out_sems.at[0, s])
+        copy.start()
+        out_copies.append(copy)
+        latent_down = dot_nt(hidden_ref[...], a_cols[s])
+        down = dot_nt(hidden_ref[...], down_w[...]) + dot(latent_down.astype(BF), b_out[s])
+        out_buf[1, s] = down.astype(BF).reshape(4, CHUNK, D)
+        copy = pltpu.make_async_copy(out_buf.at[1, s], down_out.at[s], out_sems.at[1, s])
+        copy.start()
+        out_copies.append(copy)
+
+        def put(ref, n, value, at=slice(None)):
+            ref[(2 * n + s) * 16 : (2 * n + s + 1) * 16, at] = value.astype(BF)
+
+        def turned(value):
+            return value.T.astype(BF)
+
+        put(cols_ref, 0, dot(turned(latent_cot), hidden_ref[...]), here)
+        put(cols_ref, 1, dot(turned(latent[:, :16]), grad_gate[...]), here)
+        put(cols_ref, 2, dot(turned(latent[:, 16:]), grad_up[...]), here)
+        put(wide_ref, 0, dot(turned(back_gate), rows))
+        put(wide_ref, 1, dot(turned(back_up), rows))
+        put(wide_ref, 2, dot(turned(latent_down), cot))
+    for copy in out_copies:
+        copy.wait()
+
+
+def feed_forward(set_index, x, cot, gate_w, up_w, down_w, a_wide, a_down, b_wide, b_ff):
+    spread = jax.ShapeDtypeStruct((2, 4, CHUNK, D), BF)
+    weight = pltpu.VMEM((D, FF_COLS), BF)
+    rows = pltpu.VMEM((4 * CHUNK, FF_COLS), BF)
     return pl.pallas_call(
-        collect_kernel,
-        out_shape=(out, out),
-        in_specs=[ANY, ANY],
-        out_specs=(IN_VMEM, IN_VMEM),
-        scratch_shapes=Collect.scratch() * 2,
-        compiler_params=pltpu.CompilerParams(
-            collective_id=4, has_side_effects=True, vmem_limit_bytes=24 * 2**20
+        ff_kernel,
+        out_shape=(
+            spread, spread,
+            jax.ShapeDtypeStruct((96, PADDED), BF),
+            jax.ShapeDtypeStruct((96, D), BF),
         ),
-        name="collect",
-    )(a, b)
+        in_specs=[pl.BlockSpec(memory_space=pltpu.SMEM)] + [ANY] * 9,
+        out_specs=(ANY, ANY, IN_VMEM, IN_VMEM),
+        scratch_shapes=[
+            pltpu.VMEM((2, 4, CHUNK, D), BF), pltpu.VMEM((2, 4, CHUNK, D), BF),
+            weight, weight, weight,
+            pltpu.VMEM((2, 32, D), BF), pltpu.VMEM((2, 2, 16, FF_COLS), BF),
+            pltpu.VMEM((2, 16, FF_COLS), BF), pltpu.VMEM((2, 16, D), BF),
+            rows, rows, rows,
+            pltpu.VMEM((2, 2, 4, CHUNK, D), BF),
+            pltpu.SemaphoreType.DMA((17,)), pltpu.SemaphoreType.DMA((2, 2)),
+        ],
+        compiler_params=pltpu.CompilerParams(vmem_limit_bytes=60 * 2**20),
+        name="feed_forward",
+    )(set_index, x, cot, gate_w, up_w, down_w, a_wide, a_down, b_wide, b_ff)
 
 
 def backward_slot(
@@ -1013,15 +1161,20 @@
             orders=(self.core,),
         )
 
-    def pack(self, kept, summed):
-        for n in range(64 * self.kept):
-            self.part[n // self.kept, n % self.kept] = (
-                kept[n].astype(BF) if n < len(kept) else jnp.zeros(UNIT, BF)
-            )
-        for n in range(64 * self.summed):
-            self.part[n // self.summed, self.kept + n % self.summed] = (
-                summed[n].astype(BF) if n < len(summed) else jnp.zeros(UNIT, BF)
-            )
+    def pack(self, values, first, per, at):
+        for n, value in enumerate(values, first):
+            self.part[n // per, at + n % per] = value.astype(BF)
+
+    def pack_kept(self, values, first=0):
+        self.pack(values, first, self.kept, 0)
+
+    def pack_summed(self, values, first=0):
+        self.pack(values, first, self.summed, self.kept)
+
+    def clear(self, kept, summed):
+        nothing = jnp.zeros(UNIT, BF)
+        self.pack_kept([nothing] * (64 * self.kept - kept), kept)
+        self.pack_summed([nothing] * (64 * self.summed - summed), summed)
 
     def across(self):
         for half, total in enumerate(self.reduce.fourth()):
@@ -1073,40 +1226,119 @@
         ]
 
 
-def units(ref, tiles):
+def units(value):
+    rows, columns = value.shape
     return [
-        ref[n, :, t * 128 : (t + 1) * 128] for n in range(ref.shape[0]) for t in range(tiles)
+        value[n * 16 : (n + 1) * 16, t * 128 : (t + 1) * 128]
+        for n in range(rows // 16) for t in range(columns // 128)
     ]
 
 
-FF_KEPT, FF_SUMMED = 2, 2
+FF_KEPT, FF_SUMMED, QKV_KEPT = 2, 2, 1
 COL_TILES = PADDED // 128
 D_TILES = D // 128
+DKV_SCRATCH = 7
 
 
 def backward_kernel(
-    q_ref, kv_ref, limit_ref, mixed_ref, grad_ref, lse_ref, cols_ref, oa_ref, ob_ref, ff_ref,
-    dq_ref, own_ref, all_ref, dkv_ref, acc_ref, part, *scratch,
+    grad_part_ref, down_part_ref, kv_hbm, wq_hbm, wo_hbm, resid_ref, cot_ref, norm_ff_ref, norm_in_ref,
+    rows_ref, normed_ref, a_qkv_ref, b_qkv_ref, ao_ref, bo_ref, q_ref, mixed_ref, limit_ref, lse_ref,
+    cos_ref, sin_ref, cols_ref, ff_ref,
+    result_ref, input_grad_ref, ff_all, qkv_all,
+    kv_ref, wq_ref, wo_ref, dkv_ref, acc_ref, part, dq_ref, grad_ref, grad_attn, grad_resid, grad_qkv,
+    cross_out, cross_in, home_out, home_in, copy_sem, cross_sem, home_send, home_recv,
+    *scratch,
 ):
     y, z, x, blk, uly = place()
-    greet(reduce_others() + uly_others())
+    core, h = uly % 2, uly // 2
+    scratch = list(scratch)
+
+    def take(count):
+        got = scratch[:count]
+        del scratch[:count]
+        return got
+
+    chunk = 2 * blk + h
+    upper = chunk // 32
+    home = (1 - upper) * chunk + upper * (63 - chunk)
+    home_from = [(home, upper * 2 + s) for s in (0, 1)]
+    own_chunk = (1 - h) * blk + h * (63 - blk)
+    home_to = [(own_chunk // 2, (own_chunk % 2) * 2 + half) for half in (0, 1)]
+    greet(
+        reduce_others() + uly_others() + [(blk_of(1 - y, z, x), (uly + 2) % 4)] + home_from + home_to
+    )
+    copies = [
+        pltpu.make_async_copy(src, dst, copy_sem.at[n])
+        for n, (src, dst) in enumerate(((wo_hbm, wo_ref), (kv_hbm, kv_ref), (wq_hbm, wq_ref)))
+    ]
+    for copy in copies:
+        copy.start()
+    collect_grad = Collect(grad_part_ref, take(Collect.scratches))
+    collect_out = Collect(down_part_ref, take(Collect.scratches))
     reduce = Reduce(
-        part, lambda half, item: item if half == 0 else 63 - item, scratch[:7]
-    )
-    total = Total(FF_KEPT, FF_SUMMED, all_ref, scratch[7:])
-    total.pack(
-        units(cols_ref, COL_TILES) + units(oa_ref, D_TILES // 2) + units(ob_ref, D_TILES),
-        units(ff_ref, D_TILES),
-    )
-    steps = total.steps()
+        part, lambda half, item: item if half == 0 else 63 - item, take(DKV_SCRATCH)
+    )
+    ff_total = Total(FF_KEPT, FF_SUMMED, ff_all, take(Total.scratches))
+    qkv_total = Total(QKV_KEPT, 0, qkv_all, take(Total.scratches))
+    deliver = Deliver()
+
+    def send_home(n, value):
+        home_out[n] = value.astype(BF)
+        for half in (0, 1):
+            deliver.send(
+                home_out.at[n, pl.ds(half * 64, 64)], home_in.at[n, core],
+                home_send.at[n, half], home_recv.at[n, core], home_to[half],
+            )
+
+    def arrived_home(n):
+        for s in (0, 1):
+            wait_arrival(home_in.at[n, s], home_recv.at[n, s])
+        return home_in[n].astype(F32)
+
+    collect_grad.start()
+    ff_total.pack_kept(units(cols_ref))
+    ff_total.pack_summed(units(ff_ref))
+    at_o = 6 * COL_TILES
+    ff_total.clear(at_o + D_TILES // 2 + D_TILES, 6 * D_TILES)
+    qkv_total.clear(3 * D_TILES + D_TILES // 2 + 2, 0)
+    collect_grad.second()
+    collect_grad.third()
+    residual = resid_ref[...]
+    total = collect_grad.fourth()
+    value = cot_ref[...].astype(F32) + norm_back(residual, norm_scale(residual), norm_ff_ref[...], total)
+    grad_resid[...] = value
+    own_rows = pl.ds(pl.multiple_of(h * CHUNK, CHUNK), CHUNK)
+    other_rows = pl.ds(pl.multiple_of((1 - h) * CHUNK, CHUNK), CHUNK)
+    grad_attn[own_rows, :] = value.astype(BF)
+    partner = uly_others()[0]
+    cross = remote(
+        grad_attn.at[own_rows], grad_attn.at[own_rows], cross_sem.at[0], cross_sem.at[1], partner
+    )
+    cross.start()
+    collect_out.start()
+    dkv_ref[...] = jnp.zeros_like(dkv_ref)
+    latent_o = dot_nt(ao_ref[...], mixed_ref[...]).astype(BF)
+    cross.wait_send()
+    wait_arrival(grad_attn.at[other_rows], cross_sem.at[1])
+    copies[0].wait()
+    back_o = dot_nt(grad_attn[...], bo_ref[...]).astype(BF)
+    grad_ref[...] = (dot_nt(grad_attn[...], wo_ref[...]) + dot(back_o, ao_ref[...])).astype(BF)
+    back_o = dot_nt(bo_ref[...], grad_attn[...]).astype(BF)
+    ff_total.pack_kept(
+        units(dot(back_o, mixed_ref[...])) + units(dot(latent_o, grad_attn[...])), at_o
+    )
+
+    copies[1].wait()
+    steps = ff_total.steps()
     steps.pop(0)()
-    dkv_ref[...] = jnp.zeros_like(dkv_ref)
+    more = [collect_out.second, collect_out.third]
     args = (q_ref, kv_ref, limit_ref, mixed_ref, grad_ref, lse_ref, dq_ref, dkv_ref, acc_ref)
-    for slot, chunk in ((0, blk), (1, 63 - blk)):
+    for slot, at in ((0, blk), (1, 63 - blk)):
         for part_of in range(4):
-            backward_slot(slot, chunk, part_of, *args)
-            if steps:
-                steps.pop(0)()
+            backward_slot(slot, at, part_of, *args)
+            if more:
+                more.pop(0)()
+            steps.pop(0)()
 
     def pack(n, carry):
         rows = dkv_ref[pl.ds(pl.multiple_of(n * CHUNK, CHUNK), CHUNK), :]
@@ -1115,61 +1347,98 @@
 
     lax.fori_loop(0, CHUNKS, pack, 0)
     reduce.first()
+    send_home(0, resid_ref[...] + collect_out.fourth())
     while steps:
         steps.pop(0)()
+    cos_table, sine_table = cos_ref[...], sin_ref[...]
+
+    def turn_back(value, rows=slice(None)):
+        return value * cos_table[rows] - pltpu.roll(value, HEAD // 2, 1) * sine_table[rows]
+
+    for n in range(GROUP):
+        at = slice(n * HEAD, (n + 1) * HEAD)
+        grad_qkv[:, at] = turn_back(dq_ref[:, at]).astype(BF)
+    latent_qkv = dot_nt(a_qkv_ref[...], normed_ref[...]).astype(BF)
+    copies[2].wait()
     reduce.second()
     reduce.third()
+    group = GROUP * HEAD
     for half, value in enumerate(reduce.fourth()):
-        own_ref[half] = value
-
-
-def attend_backward(q, kv, limit, mixed, grad, lse, cols, oa, ob, ff):
+        rows = slice(half * CHUNK, (half + 1) * CHUNK)
+        grad_qkv[rows, group : group + HEAD] = turn_back(value[:, :HEAD], rows).astype(BF)
+        grad_qkv[rows, group + HEAD :] = value[:, HEAD:].astype(BF)
+
+    def project_back(rows):
+        grads = grad_qkv[rows, :]
+        lifted = dot(dot_nt(grads, b_qkv_ref[...]).astype(BF), a_qkv_ref[...])
+        return dot_nt(grads[:, :512], wq_ref[0]) + dot_nt(grads[:, 512:], wq_ref[1]) + lifted
+
+    cross_out[...] = project_back(other_rows).astype(BF)
+    cross = remote(cross_out, cross_in, cross_sem.at[2], cross_sem.at[3], partner)
+    cross.start()
+    back_qkv = dot_nt(b_qkv_ref[...], grad_qkv[...]).astype(BF)
+    grad_b = dot(latent_qkv, grad_qkv[...])
+    qkv_total.pack_kept(
+        units(dot(back_qkv, normed_ref[...]))
+        + units(grad_b[:16, :group])
+        + units(grad_b[16:32, group : group + HEAD])
+        + units(grad_b[32:, group + HEAD :])
+    )
+    steps = qkv_total.steps()
+    steps.pop(0)()
+    mine = project_back(own_rows)
+    steps.pop(0)()
+    cross.wait()
+    mine = mine + cross_in[...].astype(F32)
+    tokens = rows_ref[own_rows, :].astype(F32)
+    send_home(1, grad_resid[...] + norm_back(tokens, norm_scale(tokens), norm_in_ref[...], mine))
+    while steps:
+        steps.pop(0)()
+    result_ref[...] = arrived_home(0).astype(BF)
+    input_grad_ref[...] = arrived_home(1)
+    deliver.end()
+
+
+def backward(*args):
+    dma = pltpu.SemaphoreType.DMA
+    group = GROUP * HEAD
     return pl.pallas_call(
         backward_kernel,
         out_shape=(
-            jax.ShapeDtypeStruct((2 * CHUNK, GROUP * HEAD), F32),
-            jax.ShapeDtypeStruct((2, CHUNK, 2 * HEAD), F32),
+            jax.ShapeDtypeStruct((2, CHUNK // 2, D), BF),
+            jax.ShapeDtypeStruct((2, CHUNK // 2, D), F32),
             Total.shape(FF_KEPT, FF_SUMMED),
+            Total.shape(QKV_KEPT, 0),
         ),
-        in_specs=[IN_VMEM] * 10,
-        out_specs=(IN_VMEM, IN_VMEM, ANY),
+        in_specs=[ANY] * 5 + [IN_VMEM] * 18,
+        out_specs=(IN_VMEM, IN_VMEM, ANY, ANY),
         scratch_shapes=[
+            pltpu.VMEM((CHUNKS, CHUNK, 2 * HEAD), BF),
+            pltpu.VMEM((2, D, 512), BF),
+            pltpu.VMEM((D // 2, D), BF),
             pltpu.VMEM((CHUNKS * CHUNK, 2 * HEAD), F32),
             pltpu.VMEM((HEAD, ROWS), F32),
             pltpu.VMEM((CHUNKS, CHUNK, 2 * HEAD), BF),
+            pltpu.VMEM((2 * CHUNK, group), F32),
+            pltpu.VMEM((2 * CHUNK, group), BF),
+            pltpu.VMEM((2 * CHUNK, D), BF),
+            pltpu.VMEM((CHUNK, D), F32),
+            pltpu.VMEM((2 * CHUNK, 1024), BF),
+            pltpu.VMEM((CHUNK, D), BF),
+            pltpu.VMEM((CHUNK, D), BF),
+            pltpu.VMEM((2, CHUNK, D), BF),
+            pltpu.VMEM((2, 2, CHUNK // 2, D), BF),
+            dma((3,)), dma((4,)), dma((2, 2)), dma((2, 2)),
         ]
+        + Collect.scratch() * 2
         + Reduce.scratch((CHUNK, 2 * HEAD))
-        + Total.scratch(FF_KEPT, FF_SUMMED),
+        + Total.scratch(FF_KEPT, FF_SUMMED)
+        + Total.scratch(QKV_KEPT, 0),
         compiler_params=pltpu.CompilerParams(
-            collective_id=2, has_side_effects=True, vmem_limit_bytes=56 * 2**20
+            collective_id=2, has_side_effects=True, vmem_limit_bytes=60 * 2**20
         ),
-        name="attend_backward",
-    )(q, kv, limit, mixed, grad, lse, cols, oa, ob, ff)
-
-
-QKV_KEPT = 1
-
-
-def qkv_total_kernel(a_ref, bq_ref, bkv_ref, all_ref, *scratch):
-    greet(reduce_others() + uly_others())
-    total = Total(QKV_KEPT, 0, all_ref, scratch)
-    total.pack(units(a_ref, D_TILES) + units(bq_ref, D_TILES // 2) + units(bkv_ref, 1), [])
-    for step in total.steps():
-        step()
-
-
-def qkv_total(a, bq, bkv):
-    return pl.pallas_call(
-        qkv_total_kernel,
-        out_shape=Total.shape(QKV_KEPT, 0),
-        in_specs=[IN_VMEM] * 3,
-        out_specs=ANY,
-        scratch_shapes=Total.scratch(QKV_KEPT, 0),
-        compiler_params=pltpu.CompilerParams(
-            collective_id=3, has_side_effects=True, vmem_limit_bytes=24 * 2**20
-        ),
-        name="qkv_total",
-    )(a, bq, bkv)
+        name="backward",
+    )(*args)
 
 
 def fold_kernel(pick_ref, ff_ref, qkv_ref, a_wide, a_down, b_wide, b_kv, b_ff):
@@ -1245,54 +1514,6 @@
     )(pick, ff_all, qkv_all)
 
 
-def device_at(blk, h, core):
-    return blk * 4 + h * 2 + core
-
-
-def moves():
-    def home(blk, h):
-        chunk = 2 * blk + h
-        return (chunk, 0) if chunk < 32 else (63 - chunk, 1)
-
-    return [
-        [
-            (device_at(home(b, h)[0], home(b, h)[1], c ^ j), device_at(b, h, c))
-            for b in range(32) for h in (0, 1) for c in (0, 1)
-        ]
-        for j in (0, 1)
-    ]
-
-
-ALL = ("blk", "uly")
-OVER_H = [(0, 2), (2, 0), (1, 3), (3, 1)]
-OVER_CORE = [(0, 1), (1, 0), (2, 3), (3, 2)]
-OVER_BOTH = [(0, 3), (3, 0), (1, 2), (2, 1)]
-
-
-def flip(parts, first, second):
-    return jnp.where(parts, second, first), jnp.where(parts, first, second)
-
-
-def rope_tables(positions):
-    halves = jnp.arange(0, HEAD, 2, dtype=jnp.int32).astype(F32)
-    freq_table = THETA ** (-halves / HEAD)
-    angles = positions.astype(F32)[:, None] * freq_table[None, :]
-    angles = jnp.concatenate([angles, angles], axis=-1)
-    return jnp.cos(angles), jnp.sin(angles)
-
-
-def rope_turn(values, cos_table, sine_table):
-    middle = HEAD // 2
-    turned = jnp.concatenate([-values[..., middle:], values[..., :middle]], axis=-1)
-    return values * cos_table + turned * sine_table
-
-
-def rope_back(values, cos_table, sine_table):
-    middle = HEAD // 2
-    turned = jnp.concatenate([values[..., middle:], -values[..., :middle]], axis=-1)
-    return values * cos_table + turned * sine_table
-
-
 def norm_scale(hidden):
     return lax.rsqrt(jnp.mean(hidden * hidden, axis=-1, keepdims=True) + EPS)
 
@@ -1303,203 +1524,35 @@
     return scaled * (weighted - normed * jnp.mean(weighted * normed, axis=-1, keepdims=True))
 
 
-def mm(spec, a, b):
-    return jnp.einsum(spec, a.astype(BF), b.astype(BF), preferred_element_type=F32)
-
-
 def body(
     tokens, cotangent, lengths, set_index, norm_in, norm_ff, qkv_bias, w_qkv, w_out, w_gate_up, w_down,
     a_wide, a_down, b_wide, b_kv, b_ff,
 ):
-    blk = lax.axis_index("blk")
-    uly = lax.axis_index("uly")
-    h = uly // 2
-    core = uly % 2
-    y_lo = blk // 16
-    back_moves = moves()
-    local_ff = w_down.shape[0]
-    group_cols = GROUP * HEAD
-    zero = jnp.zeros
-
-    def pick_set(table, axis, at):
-        return lax.dynamic_index_in_dim(table, at, axis, keepdims=False)
-
-    def halve(v, size, axis):
-        return lax.dynamic_slice_in_dim(v, h * size, size, axis)
-
-    def widen(v):
-        left, right = (
-            jnp.pad(v, ((0, 0),) * (v.ndim - 1) + (side,))
-            for side in ((0, PADDED - local_ff), (PADDED - local_ff, 0))
-        )
-        return jnp.where(core == 1, right, left)
-
-    quarters = jnp.concatenate(
-        [
-            w_qkv[:, : HEADS * HEAD].reshape(12, 2, group_cols),
-            w_qkv[:, HEADS * HEAD : HEADS * HEAD + 256].reshape(12, 2, HEAD),
-            w_qkv[:, HEADS * HEAD + 256 :].reshape(12, 2, HEAD),
-        ],
-        axis=2,
-    )
-    quarters = jnp.moveaxis(quarters.reshape(12, 4, 512), 1, 0)
-    quarters = jnp.pad(quarters, ((0, 0), (0, 4), (0, 0)))
-    out_quarters = jnp.pad(jnp.moveaxis(w_out.reshape(12, 4, 384), 1, 0), ((0, 0), (0, 4), (0, 0)))
-    ff_part = widen(jnp.concatenate([w_gate_up, w_down.T[None]], axis=0))
-
-    chunks = jnp.stack([blk, 63 - blk])
-    positions = (chunks[:, None] * CHUNK + jnp.arange(CHUNK, dtype=jnp.int32)[None, :]).reshape(-1)
-    length = lengths[core]
-    limit = jnp.minimum(positions, length - 1).reshape(2, 1, 1, CHUNK)
-    limit = jnp.broadcast_to(limit, (2, 8, GROUP, CHUNK)).reshape(2, 8, ROWS)
-    cos_table, sine_table = rope_tables(positions)
-    cos_heads, sine_heads = cos_table[:, None, :], sine_table[:, None, :]
-    signed = jnp.where(jnp.arange(HEAD) < HEAD // 2, -sine_table, sine_table)
-
-    own_set = set_index[core]
-    a_own = pick_set(a_wide, 1, own_set)
-    bq = halve(pick_set(b_wide[0], 0, own_set), group_cols, 1)
-    bo = pick_set(b_wide[1], 0, own_set)
-    bk, bv = (halve(pick_set(b_kv[n], 0, own_set), HEAD, 1) for n in (0, 1))
-    ao = halve(a_own[3], group_cols, 1)
-    bias = jnp.concatenate(
-        [
-            halve(qkv_bias[: HEADS * HEAD], group_cols, 0),
-            halve(qkv_bias[HEADS * HEAD : HEADS * HEAD + 256], HEAD, 0),
-            halve(qkv_bias[HEADS * HEAD + 256 :], HEAD, 0),
-        ]
-    )
-    a_qkv = a_own[:3].reshape(48, D)
-    b_qkv = jnp.concatenate(
-        [
-            jnp.concatenate([bq, zero((16, 256), BF)], axis=1),
-            jnp.concatenate([zero((16, group_cols), BF), bk, zero((16, HEAD), BF)], axis=1),
-            jnp.concatenate([zero((16, group_cols + HEAD), BF), bv], axis=1),
-        ],
-        axis=0,
-    )
+    own_set = set_index[lax.axis_index("uly") % 2]
+
+    def chosen(table):
+        return lax.dynamic_index_in_dim(table, own_set, 1, keepdims=False)
+
+    a_own, b_own = chosen(a_wide[:4]), chosen(b_wide[:2])
+    frequencies = np.float64(THETA) ** (-np.arange(0, HEAD, 2, dtype=np.float64) / HEAD)
+    frequencies = np.concatenate([frequencies, frequencies])[None].astype(np.float32)
     (
-        q, mixed, lse, kv_all, qkv_w, out_w, gate_w, up_w, down_w, rows, normed, latent_qkv, residual,
-        grad_out, gathered, grad_gathered,
+        q, mixed, lse, kv_all, qkv_w, out_w, gate_w, up_w, down_w, rows, normed, residual, grad_out,
+        gathered, grad_gathered, limit, cos_table, sine_table, b_qkv, ao,
     ) = forward(
-        quarters, out_quarters, tokens, cotangent, ff_part, limit,
-        jnp.broadcast_to(length, (1, D)), norm_in[None], norm_ff[None], bias[None], cos_table, signed,
-        a_qkv, b_qkv, ao, bo,
+        tokens, cotangent, lengths, w_qkv, w_out, w_gate_up, w_down.T, norm_in[None], norm_ff[None],
+        qkv_bias.reshape(16, HEAD), frequencies, a_own, b_own, chosen(b_kv),
     )
     gate_w, up_w, down_w = (w.reshape(D, FF_COLS) for w in (gate_w, up_w, down_w))
-    gathered, grad_gathered = (v.reshape(2, 4 * CHUNK, D) for v in (gathered, grad_gathered))
-    rows = rows.reshape(2, CHUNK, D).astype(F32)
-    scale_in = norm_scale(rows)
-    own_rows = jnp.where(h == 0, rows[0], rows[1])
-    scale_ff = norm_scale(residual)
-    latent_o = mm("tc,rc->tr", mixed, ao)
-
-    def swap_h(v):
-        return lax.ppermute(v, "uly", OVER_H)
-
-    def own_slot(v):
-        return flip(h == 1, v[0], v[1])
-
-    def by_sequence(table, axis):
-        return jnp.stack([pick_set(table, axis, set_index[s]) for s in (0, 1)])
-
-    def own_cols(v):
-        v = lax.dynamic_slice_in_dim(v, uly * local_ff, local_ff, v.ndim - 1)
-        return lax.dynamic_slice_in_dim(widen(v), y_lo * FF_COLS, FF_COLS, v.ndim - 1)
-
-    a_ff = by_sequence(a_wide[4:6], 1).reshape(2, 32, D)
-    b_cols = own_cols(by_sequence(b_ff, 1))
-    a_cols = own_cols(by_sequence(a_down, 0))
-    b_out = by_sequence(b_wide[2], 0)
-    latent_ff = mm("std,srd->str", gathered, a_ff)
-    gate = mm("std,df->stf", gathered, gate_w) + mm("str,srf->stf", latent_ff[..., :16], b_cols[:, 0])
-    up = mm("std,df->stf", gathered, up_w) + mm("str,srf->stf", latent_ff[..., 16:], b_cols[:, 1])
-    sigmoid = jax.nn.sigmoid(gate)
-    silu = gate * sigmoid
-    hidden = (silu * up).astype(BF)
-    latent_down = mm("stf,srf->str", hidden, a_cols)
-    down = mm("stf,df->std", hidden, down_w) + mm("str,srd->std", latent_down, b_out)
-    latent_back = mm("std,srd->str", grad_gathered, b_out)
-    grad_hidden = mm("std,df->stf", grad_gathered, down_w) + mm("str,srf->stf", latent_back, a_cols)
-    grad_a_cols = mm("str,stf->srf", latent_back, hidden)
-    grad_b_out = mm("str,std->srd", latent_down, grad_gathered)
-    grad_up = (grad_hidden * silu).astype(BF)
-    grad_gate = (grad_hidden * up * (sigmoid * (1.0 + gate * (1.0 - sigmoid)))).astype(BF)
-    back_gate = mm("stf,srf->str", grad_gate, b_cols[:, 0])
-    back_up = mm("stf,srf->str", grad_up, b_cols[:, 1])
-    back_ff = jnp.concatenate([back_gate, back_up], axis=-1)
-    grad_a_ff = mm("str,std->srd", back_ff, gathered)
-    grad_b_gate = mm("str,stf->srf", latent_ff[..., :16], grad_gate)
-    grad_b_up = mm("str,stf->srf", latent_ff[..., 16:], grad_up)
-    grad_ff_in = (
-        mm("stf,df->std", grad_gate, gate_w)
-        + mm("stf,df->std", grad_up, up_w)
-        + mm("str,srd->std", back_ff, a_ff)
-    )
-    grad_normed_ff, ff_out = collect(
-        grad_ff_in.astype(BF).reshape(2, 4, CHUNK, D), down.astype(BF).reshape(2, 4, CHUNK, D)
-    )
-    result = (residual + ff_out).astype(BF)
-    grad_resid = grad_out.astype(F32) + norm_back(residual, scale_ff, norm_ff, grad_normed_ff)
-    grad_attn = grad_resid.astype(BF)
-    grad_attn = jnp.concatenate(flip(h == 1, grad_attn, swap_h(grad_attn)), axis=0)
-
-    back_o = mm("td,rd->tr", grad_attn, bo)
-    grad_a_o = mm("tr,tc->rc", back_o, mixed)
-    grad_b_o = mm("tr,td->rd", latent_o, grad_attn)
-    grad_mixed = (mm("td,cd->tc", grad_attn, out_w) + mm("tr,rc->tc", back_o, ao)).astype(BF)
-
-    cols = jnp.stack([grad_a_cols, grad_b_gate, grad_b_up]).reshape(6, 16, FF_COLS).astype(BF)
-    none = jnp.zeros_like(cols)
-    cols = jnp.concatenate(flip(y_lo == 1, cols, none), axis=2)
-    ff_wide = jnp.concatenate([grad_a_ff.reshape(2, 2, 16, D), grad_b_out[:, None]], axis=1)
-    ff_wide = jnp.moveaxis(ff_wide, 0, 1).reshape(6, 16, D).astype(BF)
-    dq, dkv, ff_all = attend_backward(
-        q, kv_all, limit, mixed, grad_mixed, lse, cols, grad_a_o.astype(BF)[None],
-        grad_b_o.astype(BF)[None], ff_wide,
-    )
-    dkv = dkv.reshape(2 * CHUNK, 2 * HEAD)
-    grad_q = rope_back(dq.reshape(2 * CHUNK, GROUP, HEAD), cos_heads, sine_heads)
-    grad_k = rope_back(dkv[:, :HEAD], cos_table, sine_table)
-    grad_qkv = jnp.concatenate(
-        [grad_q.reshape(2 * CHUNK, group_cols), grad_k, dkv[:, HEAD:]], axis=1
-    ).astype(BF)
-    back_qkv = mm("to,ro->tr", grad_qkv, b_qkv)
-    grad_a_qkv = mm("tr,td->rd", back_qkv, normed)
-    grad_b_qkv = mm("tr,to->ro", latent_qkv, grad_qkv)
-    grad_normed = (
-        mm("to,do->td", grad_qkv[:, :512], qkv_w[0])
-        + mm("to,do->td", grad_qkv[:, 512:], qkv_w[1])
-        + mm("tr,rd->td", back_qkv, a_qkv)
-    ).reshape(2, CHUNK, D)
-    mine, theirs = own_slot(grad_normed)
-    grad_normed = mine + swap_h(theirs.astype(BF)).astype(F32)
-    own_scale = jnp.where(h == 0, scale_in[0], scale_in[1])
-    input_grad = grad_resid + norm_back(own_rows, own_scale, norm_in, grad_normed)
-
-    def home(v):
-        halves = v.astype(BF).reshape(2, CHUNK // 2, D)
-        got = [
-            lax.ppermute(lax.dynamic_index_in_dim(halves, core ^ j, 0, keepdims=False), ALL, back_moves[j])
-            for j in (0, 1)
-        ]
-        return jnp.stack(flip(core == 1, got[0], got[1]))
-
-    result_tokens = home(result)
-    input_grad = home(input_grad).astype(F32)
-
-    qkv_all = qkv_total(
-        grad_a_qkv.reshape(3, 16, D).astype(BF),
-        grad_b_qkv[:16, :group_cols].astype(BF)[None],
-        jnp.stack(
-            [
-                grad_b_qkv[16:32, group_cols : group_cols + HEAD],
-                grad_b_qkv[32:, group_cols + HEAD :],
-            ]
-        ).astype(BF),
+    grad_part, down_part, cols, ff_wide = feed_forward(
+        set_index, gathered, grad_gathered, gate_w, up_w, down_w, a_wide, a_down, b_wide, b_ff
+    )
+    result, input_grad, ff_all, qkv_all = backward(
+        grad_part, down_part, kv_all, qkv_w, out_w, residual, grad_out, norm_ff[None], norm_in[None], rows, normed,
+        a_own[:3].reshape(48, D), b_qkv, ao, b_own[1], q, mixed, limit, lse, cos_table, sine_table, cols, ff_wide,
     )
     pick = (jnp.arange(SETS, dtype=jnp.int32)[:, None] == set_index[None, :]).astype(F32)
-    return (result_tokens, input_grad) + tuple(fold(pick, ff_all, qkv_all))
+    return (result, input_grad) + tuple(fold(pick, ff_all, qkv_all))
 
 
 def solution(mesh):

time: 554 us -> 455 us (0.82)
  the two profiles are of different devices: /device:TPU:8 before, /device:TPU:31 now
where the time goes in v2:
time: 455 us; the launch traced here: 446 us
  Pallas kernels  423 us (93%)
  local copies, waits for them, and re-layouts  19.5 us (4%)
    pallas_call x1, Pallas kernels, backward(): pl.pallas_call(backward_kernel, out_shape=(jax.ShapeDtypeStruct((2, CHUNK...  199 us
    pallas_call x1, Pallas kernels, forward(): pl.pallas_call(forward_kernel, out_shape=(jax.ShapeDtypeStruct((2 * CHUNK...  169 us
    pallas_call x1, Pallas kernels, feed_forward(): pl.pallas_call(ff_kernel, out_shape=(spread, spread, jax.ShapeDtypeStruct...  46 us
    unnamed x60, local copies, waits for them, and re-layouts  12.7 us
    pallas_call x1, Pallas kernels, fold(): pl.pallas_call(fold_kernel, grid=(SETS,), out_shape=tuple((out(*o) for o...  9.65 us

profile of v2, /device:TPU:31, one launch (start us, length us, event | category | flops | bytes accessed | tf_op | source)
XLA Modules:
  0.0 446.3 jit_solution(12167590881373168744)
XLA Ops:
  0.8 1.4 dynamic_slice.15
  4.1 0.7 fusion.pick_ref
  4.7 0.7 broadcast_in_dim.4.norm_in_ref
  5.4 0.7 broadcast_in_dim.5.norm_ff_ref
  6.2 1.2 slice.15
  8.0 1.5 slice.14
  9.5 0.7 constant_dynamic-slice_fusion
  10.3 168.7 %forward.1 = (bf16[256,768]{1,0:T(8,128)(2,1)S(1)}, bf16[256,768]{1,0:T(8,128)(2,1)S(1)}, f32[2,8,768]{2,1,0:T(8,128)S(1)}, bf16[64,128,256]{2,1,0:T(8,128)(2,1)...) custom-call(bf16[2,64,1536]{2,1,0:T(8,128)(2,1)S(1)} %copy-done.8, ...), custom_call_target="tpu_custom_call" | custom-call | tf_op jit(solution)/shard_map/forward/pallas_call | solution.py:733
  179.0 0.9 copy-done.4
  179.9 0.9 copy-done.5
  180.7 0.9 copy-done.6
  181.6 0.8 copy-done.10
  182.4 0.7 copy-done.11
  183.1 0.7 copy-done.12
  183.9 0.6 copy-done.14
  184.5 0.6 copy-done.15
  185.1 0.6 copy-done.16
  187.0 46.0 %feed_forward.1 = (bf16[2,4,128,1536]{3,2,1,0:T(8,128)(2,1)}, bf16[2,4,128,1536]{3,2,1,0:T(8,128)(2,1)}, bf16[96,2304]{1,0:T(8,128)(2,1)}, bf16[96,1536]{1,0:T(8,128)(2,1)}) custom-call(s32[2]{0:T(128)} %set_ref.1, bf16[2,4,128,1536]{3,2,1,0:T(8,128)(2,1)} %get-tuple-element.40.x_hbm, bf16[2,4,128,1536]{3,2,1,0:T(8,128)(2,1)} %get-tuple-element.41.cot_hbm, ...), custom_call_target="tpu_custom_call" | custom-call | tf_op jit(solution)/shard_map/feed_forward/pallas_call | solution.py:964
  233.1 198.8 %backward.1 = (bf16[2,64,1536]{2,1,0:T(8,128)(2,1)}, f32[2,64,1536]{2,1,0:T(8,128)}, bf16[2,32,10,16,128]{4,3,2,1,0:T(8,128)(2,1)}, bf16[2,32,4,16,128]{4,3,2,1,0:T(8,128)(2,1)}) custom-call(bf16[2,4,128,1536]{3,2,1,0:T(8,128)(2,1)} %get-tuple-element.45.grad_part_ref, bf16[2,4,128,1536]{3,2,1,0:T(8,128)(2,1)} %get-tuple-element.46.down_part_ref, ...), custom_call_target="tpu_custom_call" | custom-call | tf_op jit(solution)/shard_map/backward/pallas_call | solution.py:1405
  431.9 1.7 copy-done.2
  433.6 1.2 copy-done.3
  434.8 9.7 %fold.1 = (f32[6,8,16,1536]{3,2,1,0:T(8,128)}, f32[8,16,8960]{2,1,0:T(8,128)}, f32[3,8,16,1536]{3,2,1,0:T(8,128)}, f32[2,8,16,256]{3,2,1,0:T(8,128)}, f32[2,8,16,8960]{3,2,1,0:T(8,128)}) custom-call(f32[8,2]{1,0:T(8,128)S(1)} %fusion.pick_ref, bf16[2,32,10,16,128]{4,3,2,1,0:T(8,128)(2,1)S(1)} %copy-done.2, bf16[2,32,4,16,128]{4,3,2,1,0:T(8,128)(2,1)S(1)} %copy-done.3), custom_call_target="tpu_custom_call" | custom-call | tf_op jit(solution)/shard_map/fold/pallas_call | solution.py:1506
  444.5 0.7 copy.26
  445.2 0.9 copy.27
  (51 shorter events, 2.0 us)
Async XLA Ops:
  0.6 5.5 %copy-start = (bf16[2,8,16,256]{3,2,1,0:T(8,128)(2,1)S(1)}, bf16[2,8,16,256]{3,2,1,0:T(8,128)(2,1)}, u32[]{:S(2)}) copy-start(bf16[2,8,16,256]{3,2,1,0:T(8,128)(2,1)} %param.31) | copy-start | bytes 393220
  0.7 9.6 %copy-start.26 = (f32[1,128]{1,0:T(1,128)S(1)}, f32[1,128]{1,0:T(1,128)}, u32[]{:S(2)}) copy-start(f32[1,128]{1,0:T(1,128)} %constant.33.clone.freq_ref) | copy-start | bytes 1540
  0.7 9.6 %copy-start.13 = (bf16[2240,48]{0,1:T(8,128)(2,1)S(1)}, bf16[2240,48]{0,1:T(8,128)(2,1)}, u32[]{:S(2)}) copy-start(bf16[2240,48]{0,1:T(8,128)(2,1)} %param.27) | copy-start | bytes 645124
  0.7 9.6 %copy-start.7 = (bf16[2,48,2240]{2,1,0:T(8,128)(2,1)S(1)}, bf16[2,48,2240]{2,1,0:T(8,128)(2,1)}, u32[]{:S(2)}) copy-start(bf16[2,48,2240]{2,1,0:T(8,128)(2,1)} %gate_up_ref.1) | copy-start | bytes 1290244
  0.7 9.6 %copy-start.22 = (bf16[12,1536]{1,0:T(8,128)(2,1)S(1)}, bf16[12,1536]{1,0:T(8,128)(2,1)}, u32[]{:S(2)}) copy-start(bf16[12,1536]{1,0:T(8,128)(2,1)} %out_ref.1) | copy-start | bytes 110596
  0.7 9.6 %copy-start.17 = (bf16[12,2048]{1,0:T(8,128)(2,1)S(1)}, bf16[12,2048]{1,0:T(8,128)(2,1)}, u32[]{:S(2)}) copy-start(bf16[12,2048]{1,0:T(8,128)(2,1)} %qkv_ref.1) | copy-start | bytes 147460
  0.7 9.6 %copy-start.24 = (f32[2048]{0:T(1024)S(1)}, f32[2048]{0:T(1024)}, u32[]{:S(2)}) copy-start(f32[2048]{0:T(1024)} %param.23) | copy-start | bytes 24580
  0.7 9.6 %copy-start.25 = (s32[2]{0:T(128)S(1)}, s32[2]{0:T(128)}, u32[]{:S(2)}) copy-start(s32[2]{0:T(128)} %length_ref.1) | copy-start | bytes 28
  0.7 9.6 %copy-start.9 = (bf16[2,64,1536]{2,1,0:T(8,128)(2,1)S(1)}, bf16[2,64,1536]{2,1,0:T(8,128)(2,1)}, u32[]{:S(2)}) copy-start(bf16[2,64,1536]{2,1,0:T(8,128)(2,1)} %cot_ref.1) | copy-start | bytes 1179652
  0.7 9.6 %copy-start.8 = (bf16[2,64,1536]{2,1,0:T(8,128)(2,1)S(1)}, bf16[2,64,1536]{2,1,0:T(8,128)(2,1)}, u32[]{:S(2)}) copy-start(bf16[2,64,1536]{2,1,0:T(8,128)(2,1)} %tokens_ref.1) | copy-start | bytes 1179652
  5.4 173.5 %copy-start.18 = (f32[1,1536]{1,0:T(1,128)}, f32[1,1536]{1,0:T(1,128)S(1)}, u32[]{:S(2)}) copy-start(f32[1,1536]{1,0:T(1,128)S(1)} %broadcast_in_dim.4.norm_in_ref) | copy-start | bytes 18436
  6.2 172.8 %copy-start.19 = (f32[1,1536]{1,0:T(1,128)}, f32[1,1536]{1,0:T(1,128)S(1)}, u32[]{:S(2)}) copy-start(f32[1,1536]{1,0:T(1,128)S(1)} %broadcast_in_dim.5.norm_ff_ref) | copy-start | bytes 18436
  179.0 0.9 copy-start.4
  179.9 0.9 copy-start.5
  180.7 0.9 copy-start.6
  181.6 0.8 copy-start.10
  182.4 0.7 copy-start.11
  183.1 0.7 copy-start.12
  187.0 46.0 %copy-start.23 = (bf16[16,768]{1,0:T(8,128)(2,1)}, bf16[16,768]{1,0:T(8,128)(2,1)S(1)}, u32[]{:S(2)}) copy-start(bf16[16,768]{1,0:T(8,128)(2,1)S(1)} %get-tuple-element.55.ao_ref) | copy-start | bytes 73732
  233.1 213.0 %copy-start.1 = (bf16[2,8,16,256]{3,2,1,0:T(8,128)(2,1)S(1)}, bf16[2,8,16,256]{3,2,1,0:T(8,128)(2,1)}, u32[]{:S(2)}) copy-start(bf16[2,8,16,256]{3,2,1,0:T(8,128)(2,1)} %param.31) | copy-start | bytes 393220
  431.8 1.7 copy-start.2
  433.6 1.2 copy-start.3
  434.8 9.7 %copy-start.28 = (bf16[2,64,1536]{2,1,0:T(8,128)(2,1)S(1)}, bf16[2,64,1536]{2,1,0:T(8,128)(2,1)}, u32[]{:S(2)}) copy-start(bf16[2,64,1536]{2,1,0:T(8,128)(2,1)} %get-tuple-element.80) | copy-start | bytes 1179652
  434.8 10.4 %copy-start.27 = (f32[2,64,1536]{2,1,0:T(8,128)S(1)}, f32[2,64,1536]{2,1,0:T(8,128)}, u32[]{:S(2)}) copy-start(f32[2,64,1536]{2,1,0:T(8,128)} %get-tuple-element.81) | copy-start | bytes 2359300
  (5 other events, 3.2 us)

commit v3 on v2

--- a/solution.py
+++ b/solution.py
@@ -181,7 +181,7 @@
 ]
 
 
-KEYS = 512
+KEYS = 1024
 STEP = KEYS // CHUNK
 ROWS = GROUP * CHUNK
 
@@ -435,9 +435,10 @@
 def forward_kernel(
     tokens_ref, cot_ref, length_ref, qkv_ref, out_ref, gate_up_ref, down_ref, norm_in_ref, norm_ff_ref,
     bias_ref, freq_ref, a_ref, b_ref, bkv_ref,
-    q_ref, mixed_ref, lse_ref, kv_out, wq_out, wo_out, gate_all, up_all, down_all, rows_out, normed_ref,
-    resid_ref, cot_own, nf_all, cot_all, limit_ref, cos_ref, sin_ref, b_qkv_ref, ao_ref,
-    kv_all, wq_all, wo_all, rows, cot_in, kv_part, acc_ref, stat_ref, qkv_in, out_in, qkv_part, out_part,
+    q_out, mixed_out, lse_out, kv_out, wq_out, wo_out, gate_all, up_all, down_all, rows_hbm, normed_out,
+    resid_out, cot_out, nf_all, cot_all, limit_out, cos_out, sin_out, b_qkv_out, ao_out,
+    q_ref, mixed_ref, lse_ref, rows_out, normed_ref, resid_ref, cot_own, limit_ref, cos_ref, sin_ref,
+    b_qkv_ref, ao_ref, kv_all, wq_all, wo_all, rows, cot_in, kv_part, acc_ref, stat_ref, qkv_in, out_in, qkv_part, out_part,
     nf_own, cross_out, cross_in, qkv_pieces, out_pieces, ff_ref,
     *sems,
 ):
@@ -665,12 +666,18 @@
         for ring in rings:
             ring.spread(e)
     (out_sem,) = take(1)
-    copies = [
-        pltpu.make_async_copy(src, dst, out_sem.at[n])
-        for n, (src, dst) in enumerate(((kv_all, kv_out), (wq_all, wq_out), (wo_all, wo_out)))
-    ]
-    copies[0].start()
-    copies[1].start()
+    copies = []
+
+    def keep(*pairs):
+        for src, dst in pairs:
+            copies.append(pltpu.make_async_copy(src, dst, out_sem.at[len(copies)]))
+            copies[-1].start()
+
+    keep(
+        (kv_all, kv_out), (wq_all, wq_out), (q_ref, q_out), (rows_out, rows_hbm), (normed_ref, normed_out),
+        (cot_own, cot_out), (limit_ref, limit_out), (cos_ref, cos_out), (sin_ref, sin_out),
+        (b_qkv_ref, b_qkv_out), (ao_ref, ao_out),
+    )
     wo.last()
 
     def wo_columns(c, n):
@@ -693,7 +700,7 @@
     for n in (0, 1):
         pair_copy(wo_columns(core, n), 1 + n).wait_send()
         pair_copy(wo_columns(1 - core, n), 1 + n).wait_recv()
-    copies[2].start()
+    keep((wo_all, wo_out), (mixed_ref, mixed_out), (lse_ref, lse_out))
 
     def project(slot):
         mixed = mixed_ref[pl.ds(pl.multiple_of(slot * CHUNK, CHUNK), CHUNK), :]
@@ -708,6 +715,7 @@
     cross.wait()
     residual = mine + cross_in[...].astype(F32)
     resid_ref[...] = residual
+    keep((resid_ref, resid_out))
     nf_own[...] = (residual * norm_scale(residual) * norm_ff_ref[...]).astype(BF)
     nf_spread = Spread(nf_own, nf_all, *take(3))
     nf_spread.start()
@@ -752,8 +760,20 @@
             jax.ShapeDtypeStruct((16, group), BF),
         ),
         in_specs=[ANY] * 2 + [pl.BlockSpec(memory_space=pltpu.SMEM)] + [IN_VMEM] * 11,
-        out_specs=(IN_VMEM,) * 3 + (ANY,) * 6 + (IN_VMEM,) * 4 + (ANY,) * 2 + (IN_VMEM,) * 5,
+        out_specs=(ANY,) * 20,
         scratch_shapes=[
+            pltpu.VMEM((2 * CHUNK, group), BF),
+            pltpu.VMEM((2 * CHUNK, group), BF),
+            pltpu.VMEM((2, 8, ROWS), F32),
+            pltpu.VMEM((2 * CHUNK, D), BF),
+            pltpu.VMEM((2 * CHUNK, D), BF),
+            pltpu.VMEM((CHUNK, D), F32),
+            pltpu.VMEM((CHUNK, D), BF),
+            pltpu.VMEM((2, 8, ROWS), jnp.int32),
+            pltpu.VMEM((2 * CHUNK, HEAD), F32),
+            pltpu.VMEM((2 * CHUNK, HEAD), F32),
+            pltpu.VMEM((48, 1024), BF),
+            pltpu.VMEM((16, group), BF),
             pltpu.VMEM((CHUNKS, CHUNK, 2 * HEAD), BF),
             pltpu.VMEM((2, D, 512), BF),
             pltpu.VMEM((D // 2, D), BF),
@@ -780,7 +800,7 @@
         + [dma((3,)), dma((3,))]
         + GATHER_SEMS()
         + SPREAD_SEMS
-        + [dma((3,)), dma((2,))]
+        + [dma((15,)), dma((2,))]
         + SPREAD_SEMS,
         compiler_params=pltpu.CompilerParams(
             collective_id=1, has_side_effects=True, vmem_limit_bytes=48 * 2**20
@@ -864,8 +884,8 @@
 
 def ff_kernel(
     set_ref, x_hbm, cot_hbm, gate_hbm, up_hbm, down_hbm, a_wide, a_down, b_wide, b_ff,
-    grad_out, down_out, cols_ref, wide_ref,
-    x_ref, cot_ref, gate_w, up_w, down_w, a_ff, b_cols, a_cols, b_out, hidden_ref, grad_gate, grad_up,
+    grad_out, down_out, cols_out, wide_out,
+    cols_ref, wide_ref, x_ref, cot_ref, gate_w, up_w, down_w, a_ff, b_cols, a_cols, b_out, hidden_ref, grad_gate, grad_up,
     out_buf, sems, out_sems,
 ):
     y, z, x, blk, uly = place()
@@ -953,6 +973,10 @@
         put(wide_ref, 0, dot(turned(back_gate), rows))
         put(wide_ref, 1, dot(turned(back_up), rows))
         put(wide_ref, 2, dot(turned(latent_down), cot))
+    for n, (src, dst) in enumerate(((cols_ref, cols_out), (wide_ref, wide_out))):
+        copy = pltpu.make_async_copy(src, dst, out_sems.at[2, n])
+        copy.start()
+        out_copies.append(copy)
     for copy in out_copies:
         copy.wait()
 
@@ -969,15 +993,16 @@
             jax.ShapeDtypeStruct((96, D), BF),
         ),
         in_specs=[pl.BlockSpec(memory_space=pltpu.SMEM)] + [ANY] * 9,
-        out_specs=(ANY, ANY, IN_VMEM, IN_VMEM),
+        out_specs=(ANY,) * 4,
         scratch_shapes=[
+            pltpu.VMEM((96, PADDED), BF), pltpu.VMEM((96, D), BF),
             pltpu.VMEM((2, 4, CHUNK, D), BF), pltpu.VMEM((2, 4, CHUNK, D), BF),
             weight, weight, weight,
             pltpu.VMEM((2, 32, D), BF), pltpu.VMEM((2, 2, 16, FF_COLS), BF),
             pltpu.VMEM((2, 16, FF_COLS), BF), pltpu.VMEM((2, 16, D), BF),
             rows, rows, rows,
             pltpu.VMEM((2, 2, 4, CHUNK, D), BF),
-            pltpu.SemaphoreType.DMA((17,)), pltpu.SemaphoreType.DMA((2, 2)),
+            pltpu.SemaphoreType.DMA((17,)), pltpu.SemaphoreType.DMA((3, 2)),
         ],
         compiler_params=pltpu.CompilerParams(vmem_limit_bytes=60 * 2**20),
         name="feed_forward",
@@ -1241,11 +1266,12 @@
 
 
 def backward_kernel(
-    grad_part_ref, down_part_ref, kv_hbm, wq_hbm, wo_hbm, resid_ref, cot_ref, norm_ff_ref, norm_in_ref,
-    rows_ref, normed_ref, a_qkv_ref, b_qkv_ref, ao_ref, bo_ref, q_ref, mixed_ref, limit_ref, lse_ref,
-    cos_ref, sin_ref, cols_ref, ff_ref,
+    grad_part_ref, down_part_ref, norm_ff_ref, norm_in_ref, a_qkv_ref, bo_ref,
+    cols_hbm, ff_hbm, resid_hbm, cot_hbm, ao_hbm, mixed_hbm, wo_hbm, kv_hbm, q_hbm, limit_hbm, lse_hbm,
+    wq_hbm, rows_hbm, normed_hbm, b_qkv_hbm, cos_hbm, sin_hbm,
     result_ref, input_grad_ref, ff_all, qkv_all,
-    kv_ref, wq_ref, wo_ref, dkv_ref, acc_ref, part, dq_ref, grad_ref, grad_attn, grad_resid, grad_qkv,
+    cols_ref, ff_ref, resid_ref, cot_ref, ao_ref, mixed_ref, wo_ref, kv_ref, q_ref, limit_ref, lse_ref,
+    wq_ref, rows_ref, normed_ref, b_qkv_ref, cos_ref, sin_ref, dkv_ref, acc_ref, part, dq_ref, grad_ref, grad_attn, grad_resid, grad_qkv,
     cross_out, cross_in, home_out, home_in, copy_sem, cross_sem, home_send, home_recv,
     *scratch,
 ):
@@ -1269,10 +1295,16 @@
     )
     copies = [
         pltpu.make_async_copy(src, dst, copy_sem.at[n])
-        for n, (src, dst) in enumerate(((wo_hbm, wo_ref), (kv_hbm, kv_ref), (wq_hbm, wq_ref)))
+        for n, (src, dst) in enumerate(
+            (
+                (cols_hbm, cols_ref), (ff_hbm, ff_ref), (resid_hbm, resid_ref), (cot_hbm, cot_ref),
+                (ao_hbm, ao_ref), (mixed_hbm, mixed_ref), (wo_hbm, wo_ref), (kv_hbm, kv_ref),
+                (q_hbm, q_ref), (limit_hbm, limit_ref), (lse_hbm, lse_ref), (wq_hbm, wq_ref),
+                (rows_hbm, rows_ref), (normed_hbm, normed_ref), (b_qkv_hbm, b_qkv_ref),
+                (cos_hbm, cos_ref), (sin_hbm, sin_ref),
+            )
+        )
     ]
-    for copy in copies:
-        copy.start()
     collect_grad = Collect(grad_part_ref, take(Collect.scratches))
     collect_out = Collect(down_part_ref, take(Collect.scratches))
     reduce = Reduce(
@@ -1295,7 +1327,14 @@
             wait_arrival(home_in.at[n, s], home_recv.at[n, s])
         return home_in[n].astype(F32)
 
+    def ready(first, last):
+        for copy in copies[first:last]:
+            copy.wait()
+
     collect_grad.start()
+    for copy in copies:
+        copy.start()
+    ready(0, 2)
     ff_total.pack_kept(units(cols_ref))
     ff_total.pack_summed(units(ff_ref))
     at_o = 6 * COL_TILES
@@ -1303,6 +1342,7 @@
     qkv_total.clear(3 * D_TILES + D_TILES // 2 + 2, 0)
     collect_grad.second()
     collect_grad.third()
+    ready(2, 7)
     residual = resid_ref[...]
     total = collect_grad.fourth()
     value = cot_ref[...].astype(F32) + norm_back(residual, norm_scale(residual), norm_ff_ref[...], total)
@@ -1320,7 +1360,6 @@
     latent_o = dot_nt(ao_ref[...], mixed_ref[...]).astype(BF)
     cross.wait_send()
     wait_arrival(grad_attn.at[other_rows], cross_sem.at[1])
-    copies[0].wait()
     back_o = dot_nt(grad_attn[...], bo_ref[...]).astype(BF)
     grad_ref[...] = (dot_nt(grad_attn[...], wo_ref[...]) + dot(back_o, ao_ref[...])).astype(BF)
     back_o = dot_nt(bo_ref[...], grad_attn[...]).astype(BF)
@@ -1328,7 +1367,7 @@
         units(dot(back_o, mixed_ref[...])) + units(dot(latent_o, grad_attn[...])), at_o
     )
 
-    copies[1].wait()
+    ready(7, 11)
     steps = ff_total.steps()
     steps.pop(0)()
     more = [collect_out.second, collect_out.third]
@@ -1347,6 +1386,7 @@
 
     lax.fori_loop(0, CHUNKS, pack, 0)
     reduce.first()
+    ready(11, 17)
     send_home(0, resid_ref[...] + collect_out.fourth())
     while steps:
         steps.pop(0)()
@@ -1359,7 +1399,6 @@
         at = slice(n * HEAD, (n + 1) * HEAD)
         grad_qkv[:, at] = turn_back(dq_ref[:, at]).astype(BF)
     latent_qkv = dot_nt(a_qkv_ref[...], normed_ref[...]).astype(BF)
-    copies[2].wait()
     reduce.second()
     reduce.third()
     group = GROUP * HEAD
@@ -1410,12 +1449,26 @@
             Total.shape(FF_KEPT, FF_SUMMED),
             Total.shape(QKV_KEPT, 0),
         ),
-        in_specs=[ANY] * 5 + [IN_VMEM] * 18,
+        in_specs=[ANY] * 2 + [IN_VMEM] * 4 + [ANY] * 17,
         out_specs=(IN_VMEM, IN_VMEM, ANY, ANY),
         scratch_shapes=[
+            pltpu.VMEM((96, PADDED), BF),
+            pltpu.VMEM((96, D), BF),
+            pltpu.VMEM((CHUNK, D), F32),
+            pltpu.VMEM((CHUNK, D), BF),
+            pltpu.VMEM((16, group), BF),
+            pltpu.VMEM((2 * CHUNK, group), BF),
+            pltpu.VMEM((D // 2, D), BF),
             pltpu.VMEM((CHUNKS, CHUNK, 2 * HEAD), BF),
+            pltpu.VMEM((2 * CHUNK, group), BF),
+            pltpu.VMEM((2, 8, ROWS), jnp.int32),
+            pltpu.VMEM((2, 8, ROWS), F32),
             pltpu.VMEM((2, D, 512), BF),
-            pltpu.VMEM((D // 2, D), BF),
+            pltpu.VMEM((2 * CHUNK, D), BF),
+            pltpu.VMEM((2 * CHUNK, D), BF),
+            pltpu.VMEM((48, 1024), BF),
+            pltpu.VMEM((2 * CHUNK, HEAD), F32),
+            pltpu.VMEM((2 * CHUNK, HEAD), F32),
             pltpu.VMEM((CHUNKS * CHUNK, 2 * HEAD), F32),
             pltpu.VMEM((HEAD, ROWS), F32),
             pltpu.VMEM((CHUNKS, CHUNK, 2 * HEAD), BF),
@@ -1428,7 +1481,7 @@
             pltpu.VMEM((CHUNK, D), BF),
             pltpu.VMEM((2, CHUNK, D), BF),
             pltpu.VMEM((2, 2, CHUNK // 2, D), BF),
-            dma((3,)), dma((4,)), dma((2, 2)), dma((2, 2)),
+            dma((17,)), dma((4,)), dma((2, 2)), dma((2, 2)),
         ]
         + Collect.scratch() * 2
         + Reduce.scratch((CHUNK, 2 * HEAD))
@@ -1548,8 +1601,9 @@
         set_index, gathered, grad_gathered, gate_w, up_w, down_w, a_wide, a_down, b_wide, b_ff
     )
     result, input_grad, ff_all, qkv_all = backward(
-        grad_part, down_part, kv_all, qkv_w, out_w, residual, grad_out, norm_ff[None], norm_in[None], rows, normed,
-        a_own[:3].reshape(48, D), b_qkv, ao, b_own[1], q, mixed, limit, lse, cos_table, sine_table, cols, ff_wide,
+        grad_part, down_part, norm_ff[None], norm_in[None], a_own[:3].reshape(48, D), b_own[1],
+        cols, ff_wide, residual, grad_out, ao, mixed, out_w, kv_all, q, limit, lse,
+        qkv_w, rows, normed, b_qkv, cos_table, sine_table,
     )
     pick = (jnp.arange(SETS, dtype=jnp.int32)[:, None] == set_index[None, :]).astype(F32)
     return (result, input_grad) + tuple(fold(pick, ff_all, qkv_all))

time: 455 us -> 448 us (0.985)
  the two profiles are of different devices: /device:TPU:31 before, /device:TPU:15 now
where the time goes in v3:
time: 448 us; the launch traced here: 439 us
  Pallas kernels  415 us (93%)
  local copies, waits for them, and re-layouts  19.5 us (4%)
    pallas_call x1, Pallas kernels, backward(): pl.pallas_call(backward_kernel, out_shape=(jax.ShapeDtypeStruct((2, CHUNK...  190 us
    pallas_call x1, Pallas kernels, forward(): pl.pallas_call(forward_kernel, out_shape=(jax.ShapeDtypeStruct((2 * CHUNK...  170 us
    pallas_call x1, Pallas kernels, feed_forward(): pl.pallas_call(ff_kernel, out_shape=(spread, spread, jax.ShapeDtypeStruct...  45.5 us
    unnamed x60, local copies, waits for them, and re-layouts  12.7 us
    pallas_call x1, Pallas kernels, fold(): pl.pallas_call(fold_kernel, grid=(SETS,), out_shape=tuple((out(*o) for o...  9.65 us

profile of v3, /device:TPU:15, one launch (start us, length us, event | category | flops | bytes accessed | tf_op | source)
XLA Modules:
  0.0 438.7 jit_solution(18435002029379675520)
XLA Ops:
  0.8 1.4 dynamic_slice.15
  4.1 0.7 fusion.pick_ref
  4.7 0.7 broadcast_in_dim.4.norm_in_ref
  5.4 0.7 broadcast_in_dim.5.norm_ff_ref
  6.2 1.2 slice.15
  8.0 1.5 slice.14
  9.5 0.7 constant_dynamic-slice_fusion
  10.3 169.9 %forward.1 = (bf16[256,768]{1,0:T(8,128)(2,1)S(1)}, bf16[256,768]{1,0:T(8,128)(2,1)S(1)}, f32[2,8,768]{2,1,0:T(8,128)S(1)}, bf16[64,128,256]{2,1,0:T(8,128)(2,1)...) custom-call(bf16[2,64,1536]{2,1,0:T(8,128)(2,1)S(1)} %copy-done.8, ...), custom_call_target="tpu_custom_call" | custom-call | tf_op jit(solution)/shard_map/forward/pallas_call | solution.py:741
  180.3 0.9 copy-done.4
  181.1 0.9 copy-done.5
  182.0 0.9 copy-done.6
  182.9 0.7 copy-done.10
  183.6 0.8 copy-done.11
  184.4 0.7 copy-done.12
  185.1 0.6 copy-done.14
  185.8 0.6 copy-done.15
  186.4 0.6 copy-done.16
  188.3 45.5 %feed_forward.1 = (bf16[2,4,128,1536]{3,2,1,0:T(8,128)(2,1)}, bf16[2,4,128,1536]{3,2,1,0:T(8,128)(2,1)}, bf16[96,2304]{1,0:T(8,128)(2,1)}, bf16[96,1536]{1,0:T(8,128)(2,1)}) custom-call(s32[2]{0:T(128)} %set_ref.1, bf16[2,4,128,1536]{3,2,1,0:T(8,128)(2,1)} %get-tuple-element.40.x_hbm, bf16[2,4,128,1536]{3,2,1,0:T(8,128)(2,1)} %get-tuple-element.41.cot_hbm, ...), custom_call_target="tpu_custom_call" | custom-call | tf_op jit(solution)/shard_map/feed_forward/pallas_call | solution.py:988
  233.8 190.4 %backward.1 = (bf16[2,64,1536]{2,1,0:T(8,128)(2,1)}, f32[2,64,1536]{2,1,0:T(8,128)}, bf16[2,32,10,16,128]{4,3,2,1,0:T(8,128)(2,1)}, bf16[2,32,4,16,128]{4,3,2,1,0:T(8,128)(2,1)}) custom-call(bf16[2,4,128,1536]{3,2,1,0:T(8,128)(2,1)} %get-tuple-element.45.grad_part_ref, bf16[2,4,128,1536]{3,2,1,0:T(8,128)(2,1)} %get-tuple-element.46.down_part_ref, ...), custom_call_target="tpu_custom_call" | custom-call | tf_op jit(solution)/shard_map/backward/pallas_call | solution.py:1444
  424.2 1.7 copy-done.2
  426.0 1.2 copy-done.3
  427.2 9.7 %fold.1 = (f32[6,8,16,1536]{3,2,1,0:T(8,128)}, f32[8,16,8960]{2,1,0:T(8,128)}, f32[3,8,16,1536]{3,2,1,0:T(8,128)}, f32[2,8,16,256]{3,2,1,0:T(8,128)}, f32[2,8,16,8960]{3,2,1,0:T(8,128)}) custom-call(f32[8,2]{1,0:T(8,128)S(1)} %fusion.pick_ref, bf16[2,32,10,16,128]{4,3,2,1,0:T(8,128)(2,1)S(1)} %copy-done.2, bf16[2,32,4,16,128]{4,3,2,1,0:T(8,128)(2,1)S(1)} %copy-done.3), custom_call_target="tpu_custom_call" | custom-call | tf_op jit(solution)/shard_map/fold/pallas_call | solution.py:1559
  436.8 0.7 copy.26
  437.6 0.9 copy.27
  (51 shorter events, 2.0 us)
Async XLA Ops:
  0.6 5.5 %copy-start = (bf16[2,8,16,256]{3,2,1,0:T(8,128)(2,1)S(1)}, bf16[2,8,16,256]{3,2,1,0:T(8,128)(2,1)}, u32[]{:S(2)}) copy-start(bf16[2,8,16,256]{3,2,1,0:T(8,128)(2,1)} %param.31) | copy-start | bytes 393220
  0.7 9.6 %copy-start.26 = (f32[1,128]{1,0:T(1,128)S(1)}, f32[1,128]{1,0:T(1,128)}, u32[]{:S(2)}) copy-start(f32[1,128]{1,0:T(1,128)} %constant.33.clone.freq_ref) | copy-start | bytes 1540
  0.7 9.6 %copy-start.13 = (bf16[2240,48]{0,1:T(8,128)(2,1)S(1)}, bf16[2240,48]{0,1:T(8,128)(2,1)}, u32[]{:S(2)}) copy-start(bf16[2240,48]{0,1:T(8,128)(2,1)} %param.27) | copy-start | bytes 645124
  0.7 9.6 %copy-start.7 = (bf16[2,48,2240]{2,1,0:T(8,128)(2,1)S(1)}, bf16[2,48,2240]{2,1,0:T(8,128)(2,1)}, u32[]{:S(2)}) copy-start(bf16[2,48,2240]{2,1,0:T(8,128)(2,1)} %gate_up_ref.1) | copy-start | bytes 1290244
  0.7 9.6 %copy-start.22 = (bf16[12,1536]{1,0:T(8,128)(2,1)S(1)}, bf16[12,1536]{1,0:T(8,128)(2,1)}, u32[]{:S(2)}) copy-start(bf16[12,1536]{1,0:T(8,128)(2,1)} %out_ref.1) | copy-start | bytes 110596
  0.7 9.6 %copy-start.17 = (bf16[12,2048]{1,0:T(8,128)(2,1)S(1)}, bf16[12,2048]{1,0:T(8,128)(2,1)}, u32[]{:S(2)}) copy-start(bf16[12,2048]{1,0:T(8,128)(2,1)} %qkv_ref.1) | copy-start | bytes 147460
  0.7 9.6 %copy-start.24 = (f32[2048]{0:T(1024)S(1)}, f32[2048]{0:T(1024)}, u32[]{:S(2)}) copy-start(f32[2048]{0:T(1024)} %param.23) | copy-start | bytes 24580
  0.7 9.6 %copy-start.25 = (s32[2]{0:T(128)S(1)}, s32[2]{0:T(128)}, u32[]{:S(2)}) copy-start(s32[2]{0:T(128)} %length_ref.1) | copy-start | bytes 28
  0.7 9.6 %copy-start.9 = (bf16[2,64,1536]{2,1,0:T(8,128)(2,1)S(1)}, bf16[2,64,1536]{2,1,0:T(8,128)(2,1)}, u32[]{:S(2)}) copy-start(bf16[2,64,1536]{2,1,0:T(8,128)(2,1)} %cot_ref.1) | copy-start | bytes 1179652
  0.7 9.6 %copy-start.8 = (bf16[2,64,1536]{2,1,0:T(8,128)(2,1)S(1)}, bf16[2,64,1536]{2,1,0:T(8,128)(2,1)}, u32[]{:S(2)}) copy-start(bf16[2,64,1536]{2,1,0:T(8,128)(2,1)} %tokens_ref.1) | copy-start | bytes 1179652
  5.4 174.8 %copy-start.18 = (f32[1,1536]{1,0:T(1,128)}, f32[1,1536]{1,0:T(1,128)S(1)}, u32[]{:S(2)}) copy-start(f32[1,1536]{1,0:T(1,128)S(1)} %broadcast_in_dim.4.norm_in_ref) | copy-start | bytes 18436
  6.2 174.1 %copy-start.19 = (f32[1,1536]{1,0:T(1,128)}, f32[1,1536]{1,0:T(1,128)S(1)}, u32[]{:S(2)}) copy-start(f32[1,1536]{1,0:T(1,128)S(1)} %broadcast_in_dim.5.norm_ff_ref) | copy-start | bytes 18436
  180.2 0.9 copy-start.4
  181.1 0.9 copy-start.5
  182.0 0.9 copy-start.6
  182.9 0.7 copy-start.10
  183.6 0.8 copy-start.11
  184.4 0.7 copy-start.12
  188.3 45.5 %copy-start.23 = (bf16[16,768]{1,0:T(8,128)(2,1)}, bf16[16,768]{1,0:T(8,128)(2,1)S(1)}, u32[]{:S(2)}) copy-start(bf16[16,768]{1,0:T(8,128)(2,1)S(1)} %get-tuple-element.51.ao_hbm) | copy-start | bytes 73732
  233.8 204.7 %copy-start.1 = (bf16[2,8,16,256]{3,2,1,0:T(8,128)(2,1)S(1)}, bf16[2,8,16,256]{3,2,1,0:T(8,128)(2,1)}, u32[]{:S(2)}) copy-start(bf16[2,8,16,256]{3,2,1,0:T(8,128)(2,1)} %param.31) | copy-start | bytes 393220
  424.2 1.7 copy-start.2
  426.0 1.2 copy-start.3
  427.2 9.7 %copy-start.28 = (bf16[2,64,1536]{2,1,0:T(8,128)(2,1)S(1)}, bf16[2,64,1536]{2,1,0:T(8,128)(2,1)}, u32[]{:S(2)}) copy-start(bf16[2,64,1536]{2,1,0:T(8,128)(2,1)} %get-tuple-element.80) | copy-start | bytes 1179652
  427.2 10.4 %copy-start.27 = (f32[2,64,1536]{2,1,0:T(8,128)S(1)}, f32[2,64,1536]{2,1,0:T(8,128)}, u32[]{:S(2)}) copy-start(f32[2,64,1536]{2,1,0:T(8,128)} %get-tuple-element.81) | copy-start | bytes 2359300
  (5 other events, 3.2 us)
